TPU v7x, 128 devices: a whole 4x4x4 slice. The times are simulated.
128 devices in a mesh: ctx: 8 (over z_lo, x), tp: 16 (over y, z_hi, core).
Axes of the slice: x: 4, y: 4, z: 4 (z_hi: 2, z_lo: 2; z = z_hi * 2 + z_lo), core: 2. Of those that a mesh axis runs over, the one named last changes fastest.
Arguments:
- tokens: bfloat16 [8192, 4096], P('ctx', 'tp'), may hold values from -6 to 6
- norm_gain: float32 [4096], replicated, may hold values from 0.1 to 1.9
- w_in: bfloat16 [4096, 3, 4096], P(None, None, 'tp'), may hold values from -0.09375 to 0.09375
- w_short: float32 [7, 3, 4096], P(None, None, 'tp'), may hold values from -2 to 2
- decay_rate: float32 [4096, 16], P('tp'), may hold values from 5e-05 to 0.05
- residue: float32 [4096, 16], P('tp'), may hold values from -1.5 to 1.5
- w_out: bfloat16 [4096, 4096], P(None, 'tp'), may hold values from -0.09375 to 0.09375
Outputs:
- output: bfloat16 [8192, 4096], P('ctx', 'tp')
All inputs are finite; a program needn't handle non-finite values.
Results may differ from a plain program's by a relative error of at most 0.015.
Values may be sent and summed in bfloat16 or wider, within the bound.
No kernel may reach another device: no remote copies, remote signals or barrier semaphores. Data moves between devices by JAX's collectives and lax.ppermute only.
A program may use at most 128 MiB of HBM per device.

v0:
```python
import jax
import jax.numpy as jnp
from jax import lax
from jax.sharding import PartitionSpec as P

BLOCK = 128


HIGH = lax.Precision.HIGHEST


def short_filter(proj, taps, before):
    length = proj.shape[2]
    span = taps.shape[0]
    padded = jnp.concatenate([before, proj], axis=2).astype(jnp.float32)
    total = jnp.zeros(proj.shape, jnp.float32)
    for offset in range(span):
        begin = span - 1 - offset
        total = total + taps[offset][:, :, None] * padded[:, :, begin : begin + length]
    return (total[0].astype(jnp.bfloat16), (total[1] * total[2]).astype(jnp.bfloat16))


def link_states(earlier, later):
    return (earlier[0] * later[0], later[0] * earlier[1] + later[1])


def modal_local(gated, rate, weight_res):
    values = gated.astype(jnp.float32)
    chans, length = values.shape
    count = length // BLOCK
    position = jnp.arange(BLOCK).astype(jnp.float32)
    rise = jnp.exp(rate[:, :, None] * position)
    fall = jnp.exp(-rate[:, :, None] * position)
    lifted = values.reshape(chans, 1, count, BLOCK) * rise[:, :, None, :]
    lower = (position[None, :] <= position[:, None]).astype(jnp.float32)
    running = jnp.einsum("cnbu,tu->cnbt", lifted, lower, precision=HIGH)
    block_end = running[:, :, :, BLOCK - 1] * fall[:, :, BLOCK - 1][:, :, None]
    factors = jnp.broadcast_to(jnp.exp(-rate * BLOCK)[:, :, None], block_end.shape)
    inclusive = lax.associative_scan(link_states, (factors, block_end), axis=2)[1]
    starting = jnp.zeros((chans, rate.shape[1], 1), jnp.float32)
    incoming = jnp.concatenate([starting, inclusive[:, :, :-1]], axis=2)
    running = running + jnp.exp(-rate)[:, :, None, None] * incoming[:, :, :, None]
    result = jnp.einsum("cn,cnbt->cbt", weight_res, fall[:, :, None, :] * running, precision=HIGH)
    return (result.reshape(chans, length), inclusive[:, :, count - 1])


def body(tokens, norm_gain, w_in, w_short, decay_rate, residue, w_out):
    chans = w_in.shape[2]
    span = w_short.shape[0]
    whole = lax.all_gather(tokens, "tp", axis=1, tiled=True)
    wide = whole.astype(jnp.float32)
    scale = lax.rsqrt(jnp.mean(wide * wide, axis=1, keepdims=True) + 1e-05)
    normed = (wide * scale * norm_gain).astype(jnp.bfloat16)
    proj = lax.dot_general(
        w_in, normed, (((0,), (1,)), ((), ())), preferred_element_type=jnp.float32
    )
    proj = proj.astype(jnp.bfloat16)
    weight_res = residue * jnp.sqrt(decay_rate)
    part = lax.axis_index("ctx")
    sub = chans // lax.axis_size("ctx")
    first = part * sub
    moved = lax.all_to_all(proj, "ctx", split_axis=1, concat_axis=2, tiled=True)
    taps_sub = lax.dynamic_slice_in_dim(w_short, first, sub, 2)
    before = jnp.zeros((3, sub, span - 1), jnp.bfloat16)
    gate_q, gated_kv = short_filter(moved, taps_sub, before)
    rate_sub = lax.dynamic_slice_in_dim(decay_rate, first, sub, 0)
    res_sub = lax.dynamic_slice_in_dim(weight_res, first, sub, 0)
    long_out, final_state = modal_local(gated_kv, rate_sub, res_sub)
    mixed_sub = (gate_q.astype(jnp.float32) * long_out).astype(jnp.bfloat16)
    mixed = lax.all_to_all(mixed_sub, "ctx", split_axis=1, concat_axis=0, tiled=True)
    projected = lax.dot_general(
        lax.all_gather(mixed, "tp", axis=0, tiled=True),
        w_out,
        (((0,), (0,)), ((), ())),
        preferred_element_type=jnp.float32,
    )
    return (tokens.astype(jnp.float32) + projected).astype(jnp.bfloat16)


def solution(mesh):
    placed = (
        P("ctx", "tp"),
        P(),
        P(None, None, "tp"),
        P(None, None, "tp"),
        P("tp", None),
        P("tp", None),
        P(None, "tp"),
    )
    return jax.shard_map(
        body, mesh=mesh, in_specs=placed, out_specs=P("ctx", "tp"), check_vma=False
    )
```

profile of v0, /device:TPU:1, one launch (start us, length us, event | category | flops | bytes accessed | tf_op | source)
XLA Modules:
  0.0 445.8 jit_solution(9972016029235072817)
XLA Ops:
  7.3 86.3 %all-gather.3.cloned.1.call-done = bf16[1024,4096]{1,0:T(8,128)(2,1)} async-done(((bf16[1024,256]{1,0:T(8,128)(2,1)}), bf16[1024,4096]{1,0:T(8,128)(2,1)}) %all-gather.3.cloned.1.call-update) | async-done | bytes 8388624 | tf_op jit(solution)/shard_map/all_gather | solution.py:50
  93.5 5.2 %fusion = f32[1024]{0:T(1024)S(1)} fusion(bf16[1024,4096]{1,0:T(8,128)(2,1)} %all-gather.3.cloned.1.call-done), kind=kLoop, calls=%fused_computation.2 | loop fusion | flops 12581888 | bytes 8392704 | tf_op jit(solution)/shard_map/reduce_sum | solution.py:52
  99.3 10.9 %fusion.23 = bf16[3,256,1024]{1,2,0:T(8,128)(2,1)} fusion(bf16[4096,3,256]{2,0,1:T(8,128)(2,1)} %param.9, bf16[1024,4096]{1,0:T(8,128)(2,1)S(1)} %copy-done.2, f32[4096]{0:T(1024)S(1)} %copy-done.9, f32[1024]{0:T(1024)S(1)} %add_rsqrt_fusion), kind=kOutput, calls=%fused_computation.32 | convolution fusion | flops 6460014592 | bytes 16273408 | tf_op jit(solution)/shard_map/dot_general | solution.py:54
  110.2 4.5 copy.86
  114.7 4.3 all-to-all-start
  124.1 22.1 %all-to-all-done = bf16[3,256,1024]{2,0,1:T(4,128)(2,1)} async-done(((bf16[3,256,1024]{2,0,1:T(4,128)(2,1)}), bf16[3,256,1024]{2,0,1:T(4,128)(2,1)}, u32[]{:S(2)}, u32[]{:S(2)}) %all-to-all-start) | async-done | bytes 1572896 | tf_op jit(solution)/shard_map/all_to_all | solution.py:62
  146.2 2.2 copy.87
  149.0 5.4 %fusion.14 = f32[3,32,8192]{2,1,0:T(8,128)S(1)} fusion(f32[3,32,8198]{2,1,0:T(8,128)S(1)} %pad_convert_fusion, f32[3,32]{1,0:T(4,128)S(1)} %get-tuple-element.29, f32[3,32]{1,0:T(4,128)S(1)} %get-tuple-element.30, f32[3,32]{1,0:T(4,128)S(1)} %get-tuple-element.31, f32[3,32]{1,0:T(4,128)S(1)} %get-tuple-element.32, f32[3,32]{1,0:T(4,128)S(1)} %get-tuple-element.33, ...), kind=kLoop, calls=%fused_computation.18 | loop fusion | flops 10223616 | bytes 25168512 | tf_op jit(solution)/shard_map/add | solution.py:19
  155.8 9.0 %fusion.5 = f32[32,16,64,128]{3,2,1,0:T(8,128)S(1)} fusion(f32[32,16,128]{2,1,0:T(8,128)S(1)} %get-tuple-element.28, f32[32,64,128]{2,1,0:T(8,128)S(1)} %bitcast.65, f32[128]{0:T(128)S(1)} %iota_convert_fusion), kind=kOutput, calls=%fused_computation.9 | convolution fusion | flops 6446661632 | bytes 18088448 | tf_op jit(solution)/shard_map/cnbu,tu->cnbt/dot_general | solution.py:36
  164.8 9.0 %slice_reduce_fusion = f32[32,16,64]{2,1,0:T(8,128)S(1)} fusion(f32[32,16,64,128]{3,2,1,0:T(8,128)S(1)} %fusion.5), kind=kLoop, calls=%fused_computation.5 | loop fusion | bytes 262144 | tf_op jit(solution)/shard_map/slice | solution.py:37
  173.9 3.7 slice.240
  177.7 3.3 slice.207
  181.0 3.2 slice.206
  184.3 2.4 slice.238
  186.7 1.9 slice.212
  188.6 1.8 slice.211
  190.5 1.9 slice.236
  192.4 12.8 %slice.217 = f32[32,16,8]{2,1,0:T(8,128)S(1)} slice(f32[32,16,16]{2,1,0:T(8,128)S(1)} %multiply_add_fusion.3), slice={[0:32:1], [0:16:1], [1:16:2]} | slice | bytes 32768 | tf_op jit(solution)/shard_map/slice | solution.py:39
  205.2 1.9 slice.216
  208.2 1.6 slice.234
  209.8 1.7 slice.222
  211.5 1.6 slice.221
  213.1 1.2 multiply_add_fusion.1
  214.3 1.6 slice.227
  215.9 1.5 slice.226
  217.4 2.9 copy.120
  220.2 1.2 multiply_add_fusion
  221.4 1.1 slice_add_fusion.1
  224.3 12.4 %pad.42 = f32[32,16,4]{2,1,0:T(8,128)S(1)} pad(f32[32,16,2]{2,1,0:T(8,128)} %pad_add_fusion, f32[]{:T(128)} %constant.7.clone.1), padding=0_0_0x0_0_0x1_0_1 | pad | bytes 12292 | tf_op jit(solution)/shard_map/pad | solution.py:39
  236.6 1.9 pad_maximum_fusion
  238.5 15.9 %pad.41 = f32[32,16,4]{2,1,0:T(8,128)} pad(f32[32,16,2]{2,1,0:T(8,128)} %pad_maximum_fusion, f32[]{:T(128)} %constant.7.clone.1), padding=0_0_0x0_0_0x0_1_1 | pad | bytes 12292 | tf_op jit(solution)/shard_map/pad | solution.py:39
  254.4 1.7 add.141
  256.0 1.2 fusion.33
  258.0 12.4 %pad.43 = f32[32,16,8]{2,1,0:T(8,128)S(1)} pad(f32[32,16,4]{2,1,0:T(8,128)} %pad_maximum_fusion.1, f32[]{:T(128)} %constant.7.clone.1), padding=0_0_0x0_0_0x0_1_1 | pad | bytes 24580 | tf_op jit(solution)/shard_map/pad | solution.py:39
  270.4 12.4 %pad.44 = f32[32,16,8]{2,1,0:T(8,128)S(1)} pad(f32[32,16,4]{2,1,0:T(8,128)} %add.141, f32[]{:T(128)} %constant.7.clone.1), padding=0_0_0x0_0_0x1_0_1 | pad | bytes 24580 | tf_op jit(solution)/shard_map/pad | solution.py:39
  284.8 2.7 pad.45
  287.5 12.6 %pad.46 = f32[32,16,16]{2,1,0:T(8,128)S(1)} pad(f32[32,16,8]{2,1,0:T(8,128)} %add.143, f32[]{:T(128)} %constant.7.clone.1), padding=0_0_0x0_0_0x1_0_1 | pad | bytes 49156 | tf_op jit(solution)/shard_map/pad | solution.py:39
  301.4 3.2 pad.47
  304.6 3.2 pad.48
  309.1 4.3 pad.62
  313.4 4.3 pad.78
  317.9 7.6 %add_multiply_fusion = f32[32,16,64,128]{3,2,1,0:T(8,128)S(1)} fusion(f32[32,16,64,128]{3,2,1,0:T(8,128)} %copy-done.1, f32[32,16,64]{2,1,0:T(8,128)S(1)} %pad_multiply_fusion, f32[32,16,128]{2,1,0:T(8,128)S(1)} %copy-done.4), kind=kLoop, calls=%fused_computation.8 | loop fusion | flops 8388608 | bytes 33947648 | tf_op jit(solution)/shard_map/mul | solution.py:43
  325.5 16.0 %fusion.3 = f32[32,1,64,128]{3,1,2,0:T(1,128)S(1)} fusion(f32[32,16,1,1]{1,2,3,0:T(1,128)S(1)} %copy.107, f32[32,16,64,128]{3,2,1,0:T(8,128)S(1)} %add_multiply_fusion), kind=kOutput, calls=%fused_computation.6 | convolution fusion | flops 50331648 | bytes 17827840 | tf_op jit(solution)/shard_map/cn,cnbt->cbt/dot_general | solution.py:43
  341.5 1.1 reshape.70
  342.7 1.7 fusion.27
  344.7 16.4 %all_to_all.34 = bf16[32,8,1024]{2,0,1:T(8,128)(2,1)} all-to-all(bf16[32,8,1024]{2,0,1:T(8,128)(2,1)S(1)} %copy.105), channel_id=1, replica_groups=mesh['ctx'=8,'tp'=16] {'ctx'}, dimensions={1} | all-to-all | bytes 1048576 | tf_op jit(solution)/shard_map/all_to_all | solution.py:70
  361.1 71.1 %all-gather.5.cloned.1.call-done = bf16[4096,1024]{1,0:T(8,128)(2,1)} async-done(((bf16[256,1024]{1,0:T(8,128)(2,1)}), bf16[4096,1024]{1,0:T(8,128)(2,1)}) %all-gather.5.cloned.1.call-update) | async-done | bytes 8388624 | tf_op jit(solution)/shard_map/all_gather | solution.py:72
  432.2 6.6 %fusion.26 = bf16[1024,256]{1,0:T(8,128)(2,1)} fusion(bf16[4096,1024]{1,0:T(8,128)(2,1)} %all-gather.5.cloned.1.call-done, bf16[4096,256]{1,0:T(8,128)(2,1)S(1)} %copy-done, bf16[1024,256]{1,0:T(8,128)(2,1)S(1)} %copy-done.5), kind=kOutput, calls=%fused_computation.34 | convolution fusion | flops 2148270080 | bytes 11534336 | tf_op jit(solution)/shard_map/dot_general | solution.py:71
  (71 shorter events, 17.4 us)
Async XLA Ops:
  6.5 425.7 %copy-start = (bf16[4096,256]{1,0:T(8,128)(2,1)S(1)}, bf16[4096,256]{1,0:T(8,128)(2,1)}, u32[]{:S(2)}) copy-start(bf16[4096,256]{1,0:T(8,128)(2,1)} %param.13) | copy-start | bytes 6291460
  6.5 87.0 %all-gather.3.cloned.1.call-start = ((), (), s32[]{:S(2)}) async-start(), calls=%async_computation.2 | async-start | bytes 8912896 | tf_op jit(solution)/shard_map/all_gather | solution.py:50
  6.5 92.2 %copy-start.9 = (f32[4096]{0:T(1024)S(1)}, f32[4096]{0:T(1024)}, u32[]{:S(2)}) copy-start(f32[4096]{0:T(1024)} %param.8) | copy-start | bytes 49156
  93.5 5.8 %copy-start.2 = (bf16[1024,4096]{1,0:T(8,128)(2,1)S(1)}, bf16[1024,4096]{1,0:T(8,128)(2,1)}, u32[]{:S(2)}) copy-start(bf16[1024,4096]{1,0:T(8,128)(2,1)} %all-gather.3.cloned.1.call-done) | copy-start | bytes 25165828
  110.2 9.9 %copy-start.7 = (f32[256,16]{0,1:T(8,128)S(1)}, f32[256,16]{0,1:T(8,128)}, u32[]{:S(2)}) copy-start(f32[256,16]{0,1:T(8,128)} %param.11) | copy-start | bytes 49156
  110.2 10.2 %copy-start.8 = (f32[256,16]{0,1:T(8,128)S(1)}, f32[256,16]{0,1:T(8,128)}, u32[]{:S(2)}) copy-start(f32[256,16]{0,1:T(8,128)} %param.12) | copy-start | bytes 49156
  114.7 31.5 %all-to-all-start = ((bf16[3,256,1024]{2,0,1:T(4,128)(2,1)}), bf16[3,256,1024]{2,0,1:T(4,128)(2,1)}, u32[]{:S(2)}, u32[]{:S(2)}) async-start(bf16[3,256,1024]{2,0,1:T(4,128)(2,1)} %copy.86), calls=%async_computation | async-start | bytes 4194304 | tf_op jit(solution)/shard_map/all_to_all | solution.py:62
  119.0 313.2 %all-gather.5.cloned.1.call-start = ((), (), s32[]{:S(2)}) async-start(), calls=%async_computation.3 | async-start | bytes 8912896 | tf_op jit(solution)/shard_map/all_gather | solution.py:72
  123.0 0.7 copy-start.3
  164.7 9.1 %copy-start.1 = (f32[32,16,64,128]{3,2,1,0:T(8,128)}, f32[32,16,64,128]{3,2,1,0:T(8,128)S(1)}, u32[]{:S(2)}) copy-start(f32[32,16,64,128]{3,2,1,0:T(8,128)S(1)} %fusion.5) | copy-start | bytes 50331652
  217.4 6.0 %copy-start.6 = (f32[32,16,1]{2,1,0:T(8,128)S(1)}, f32[32,16,1]{2,1,0:T(8,128)}, u32[]{:S(2)}) copy-start(f32[32,16,1]{2,1,0:T(8,128)} %copy.104) | copy-start | bytes 6148
  301.4 16.6 %copy-start.4 = (f32[32,16,128]{2,1,0:T(8,128)S(1)}, f32[32,16,128]{2,1,0:T(8,128)}, u32[]{:S(2)}) copy-start(f32[32,16,128]{2,1,0:T(8,128)} %copy-done.3) | copy-start | bytes 786436
  342.7 89.6 %copy-start.5 = (bf16[1024,256]{1,0:T(8,128)(2,1)S(1)}, bf16[1024,256]{1,0:T(8,128)(2,1)}, u32[]{:S(2)}) copy-start(bf16[1024,256]{1,0:T(8,128)(2,1)} %param.7) | copy-start | bytes 1572868
Sparse Core Ops, SparseCore 0:
  9.6 83.8 all-gather.2
  361.2 70.9 all-gather.4
where the time goes:
time: 450 us; the launch traced here: 446 us
  waiting for transfers between devices  180 us (40%)
  local copies, waits for them, and re-layouts  150 us (33%)
  matrix products  42.4 us (9%)
  other arithmetic  38.9 us (9%)
  blocking collectives  16.4 us (4%)
  between operations  14 us (3%)
    all_gather x1, waiting for transfers between devices, body(): whole = lax.all_gather(tokens, 'tp', axis=1, tiled=True)  86.3 us
    pad x8, local copies, waits for them, and re-layouts, modal_local(): lax.associative_scan(link_states, (factors, block_end), axis=2)[1]  74.7 us
    all_gather x1, waiting for transfers between devices, body(): lax.all_gather(mixed, 'tp', axis=0, tiled=True)  71.1 us
    slice x16, local copies, waits for them, and re-layouts, modal_local(): lax.associative_scan(link_states, (factors, block_end), axis=2)[1]  42.6 us
    all_to_all x1, waiting for transfers between devices, body(): moved = lax.all_to_all(proj, 'ctx', split_axis=1, concat_axis=2, tiled=True)  22.1 us
    all_to_all x1, blocking collectives, body(): lax.all_to_all(mixed_sub, 'ctx', split_axis=1, concat_axis=0, tiled=True)  16.4 us
    dot_general x1, matrix products, modal_local(): jnp.einsum('cn,cnbt->cbt', weight_res, fall[:, :, None, :] * running, pre...  16 us
    dot_general x1, matrix products, body(): lax.dot_general(w_in, normed, (((0,), (1,)), ((), ())), preferred_element...  10.9 us
  transfers between devices with their start and end apart: 3, of which 3 were waited for; matrix products, arithmetic and copies ran while one was open for 1% of the time, Pallas kernels for 0%

commit v1 on v0

v1 whole, which is shorter than its diff:
```python
import jax
import jax.numpy as jnp
from jax import lax
from jax.experimental import pallas as pl
from jax.experimental.pallas import tpu as pltpu
from jax.sharding import PartitionSpec as P

F32 = jnp.float32
BF16 = jnp.bfloat16
MODES = 16
SPAN = 7
REACH = SPAN - 1
LANES = 128
SUBS = 8
VMEM = pl.BlockSpec(memory_space=pltpu.VMEM)
HBM = pl.BlockSpec(memory_space=pl.ANY)
SMEM = pl.BlockSpec(memory_space=pltpu.SMEM)
MIB = 1024 * 1024


def call(kernel, outs, ins, specs, scratch, limit, flops, aliases=None):
    moved = sum(a.size * a.dtype.itemsize for a in ins)
    return pl.pallas_call(
        kernel,
        out_shape=outs,
        in_specs=specs,
        out_specs=[VMEM] * len(outs) if isinstance(outs, list) else VMEM,
        scratch_shapes=scratch,
        input_output_aliases=aliases or {},
        compiler_params=pltpu.CompilerParams(vmem_limit_bytes=limit * MIB),
        cost_estimate=pl.CostEstimate(flops=flops, bytes_accessed=moved // 4, transcendentals=0),
    )(*ins)


def order_kernel(order, w_in, w_out, first, second, sems):
    count = first.shape[0]
    width = first.shape[2]
    copies = []
    for i in range(count):
        rows = pl.ds(pl.multiple_of(order[i] * width, width), width)
        copies.append(pltpu.make_async_copy(w_in.at[:, rows, :], first.at[i], sems.at[0, i]))
        copies.append(pltpu.make_async_copy(w_out.at[rows, :], second.at[i], sems.at[1, i]))
    for copy in copies:
        copy.start()
    for copy in copies:
        copy.wait()


def add_pieces(begin, layout, order, gain, w, refs, r, tile):
    total = [None] * 3
    squares = None
    for number, parts in enumerate(layout):
        x = refs_rows(refs, parts, r, tile).astype(F32)
        row = gain[pl.ds(order[begin + number], 1), :]
        scaled = (x * row).astype(BF16)
        square = x * x
        square = square[:, :LANES] + square[:, LANES:]
        squares = square if squares is None else squares + square
        for s in range(3):
            part = jnp.dot(scaled, w[begin + number, s], preferred_element_type=F32)
            total[s] = part if total[s] is None else total[s] + part
    return total, squares


def refs_rows(refs, parts, r, tile):
    if len(parts) == 1:
        return refs[parts[0]][pl.ds(r * tile, tile), :]
    half = refs[parts[0]].shape[0]
    if r * tile < half:
        return refs[parts[0]][pl.ds(r * tile, tile), :]
    return refs[parts[1]][pl.ds(r * tile - half, tile), :]


def proj_kernel(begin, layout, fresh, order, gain, w, *refs):
    count = sum(len(p) for p in layout)
    pieces = refs[:count]
    if fresh:
        acc, ss = refs[count:]
    else:
        acc_in, ss_in, acc, ss = refs[count:]
    tile = 256
    for r in range(acc.shape[0] // tile):
        rows = pl.ds(r * tile, tile)
        total, squares = add_pieces(begin, layout, order, gain, w, pieces, r, tile)
        for s in range(3):
            cols = slice(s * 256, (s + 1) * 256)
            acc[rows, cols] = total[s] if fresh else acc_in[rows, cols] + total[s]
        ss[rows, :] = squares if fresh else ss_in[rows, :] + squares


def number(pieces):
    layout, flat = [], []
    for p in pieces:
        parts = p if isinstance(p, tuple) else (p,)
        layout.append(tuple(range(len(flat), len(flat) + len(parts))))
        flat.extend(parts)
    return layout, flat


def project(begin, pieces, order, gain, w, state):
    layout, flat = number(pieces)
    rows = flat[0].shape[0] * len(layout[0])
    outs = [jax.ShapeDtypeStruct((rows, 768), F32), jax.ShapeDtypeStruct((rows, LANES), F32)]
    ins = [order, gain, w] + flat + (list(state) if state else [])
    specs = [SMEM, VMEM, VMEM] + [VMEM] * (len(ins) - 3)
    fresh = state is None

    def kernel(*refs):
        proj_kernel(begin, layout, fresh, *refs)

    aliases = {} if fresh else {len(ins) - 2: 0, len(ins) - 1: 1}
    return call(kernel, outs, ins, specs, [], 16, len(pieces) * 2 * rows * 256 * 768, aliases)


def local_kernel(begin, layout, chunk, order, gain, w, *refs):
    count = sum(len(p) for p in layout)
    pieces = refs[:count]
    acc, ss, taps, decay, weight, jumps, gate, local, before, load, proj = refs[count:]
    tile = 256
    width = gate.shape[1]
    rows_all = acc.shape[0]
    halves = width // LANES
    proj[:, 0:8, :] = jnp.zeros((3 * halves, 8, LANES), F32)
    for r in range(rows_all // tile):
        rows = pl.ds(r * tile, tile)
        total, squares = add_pieces(begin, layout, order, gain, w, pieces, r, tile)
        mean = jnp.sum(ss[rows, :] + squares, axis=1, keepdims=True) / (16 * width)
        scale = lax.rsqrt(mean + 1e-05)
        for s in range(3):
            cols = slice(s * 256, (s + 1) * 256)
            value = (acc[rows, cols] + total[s]) * scale
            value = value.astype(BF16).astype(F32)
            for g in range(halves):
                proj[s * halves + g, pl.ds(8 + r * tile, tile), :] = value[:, g * LANES : (g + 1) * LANES]
    head = lax.broadcasted_iota(jnp.int32, (SUBS, LANES), 0) == 0
    for g in range(width // LANES):
        lanes = slice(g * LANES, (g + 1) * LANES)

        def strided(s, t):
            return proj[s * halves + g, pl.ds(8 + t, SUBS, stride=chunk), :]

        def step(t, carry, masked):
            windows, states = carry
            short = []
            moved = []
            for s in range(3):
                newest = strided(s, t)
                line = windows[s] + [newest]
                value = None
                for j in range(SPAN):
                    at = (j * 3 + s) * SUBS
                    term = taps[at : at + SUBS, lanes] * line[REACH - j]
                    value = term if value is None else value + term
                short.append(value)
                moved.append(line[1:])
            kv = (short[1] * short[2]).astype(BF16).astype(F32)
            if masked:
                kv = jnp.where(head, 0.0, kv)
            out = None
            later = []
            for n in range(MODES):
                at = n * SUBS
                state = decay[at : at + SUBS, lanes] * states[n] + kv
                later.append(state)
                term = weight[at : at + SUBS, lanes] * state
                out = term if out is None else out + term
            place = pl.ds(pl.multiple_of(t * SUBS, SUBS), SUBS)
            gate[place, lanes] = short[0].astype(BF16).astype(F32)
            local[place, lanes] = out
            return moved, later

        windows = [
            [strided(s, t) for t in range(-REACH, 0)]
            for s in range(3)
        ]
        carry = (windows, [jnp.zeros((SUBS, LANES), F32)] * MODES)
        unroll = 8
        for t in range(unroll):
            carry = step(t, carry, t < REACH)

        def steps(i, carry):
            for u in range(unroll):
                carry = step(i * unroll + u, carry, False)
            return carry

        carry = lax.fori_loop(1, chunk // unroll, steps, carry)
        place = lax.broadcasted_iota(jnp.int32, (SUBS, LANES), 0)
        for n in range(MODES):
            at = n * SUBS
            state = carry[1][n]
            for level, hop in enumerate((1, 2, 4)):
                moved = jnp.where(place >= hop, pltpu.roll(state, hop, 0), 0.0)
                jump = jumps[level * MODES + n : level * MODES + n + 1, lanes]
                state = state + jump * moved
            before[at : at + SUBS, lanes] = jnp.where(place >= 1, pltpu.roll(state, 1, 0), 0.0)
            load[n : n + 1, lanes] = state[SUBS - 1 : SUBS, :]
    for s in range(3):
        for g in range(halves):
            lanes = slice(g * LANES, (g + 1) * LANES)
            load[16 + s * 16 : 24 + s * 16, lanes] = proj[s * halves + g, rows_all : rows_all + 8, :]
            load[24 + s * 16 : 32 + s * 16, lanes] = proj[s * halves + g, 8:16, :]


def join_kernel(chunk, *refs):
    loads = refs[:8]
    gate, local, before, taps, decay, weight, power, power_less, ahead, early, late = refs[8:19]
    mixed, held, whole, start = refs[19:]
    step_rows = loads[0].shape[0]
    width = mixed.shape[1]
    for g in range(width // LANES):
        for d in range(8):
            held[g, d * step_rows : (d + 1) * step_rows, :] = loads[d][:, g * LANES : (g + 1) * LANES]
        held[g, 8 * step_rows : 9 * step_rows, :] = jnp.zeros((step_rows, LANES), F32)
    place = lax.broadcasted_iota(jnp.int32, (SUBS, LANES), 0)
    head = place == 0
    for g in range(width // LANES):
        lanes = slice(g * LANES, (g + 1) * LANES)

        def strided(row):
            return held[g, pl.ds(row, SUBS, stride=step_rows), :]

        short = []
        for s in range(3):
            line = [strided(step_rows + 16 + s * 16 + 8 - REACH + t) for t in range(REACH)]
            line += [strided(24 + s * 16 + t) for t in range(REACH)]
            values = []
            for t in range(REACH):
                value = None
                for j in range(SPAN):
                    at = (j * 3 + s) * SUBS
                    term = taps[at : at + SUBS, lanes] * line[REACH + t - j]
                    value = term if value is None else value + term
                values.append(value)
            short.append(values)
        kv = [(short[1][t] * short[2][t]).astype(BF16).astype(F32) for t in range(REACH)]
        q = [short[0][t].astype(BF16).astype(F32) for t in range(REACH)]
        for n in range(MODES):
            at = n * SUBS
            full = strided(n)
            own = None
            for t in range(REACH):
                row = t * MODES + n
                full = full + late[row : row + 1, lanes] * kv[t]
                term = early[row : row + 1, lanes] * kv[t]
                own = term if own is None else own + term
            arrived = jnp.sum(ahead[at : at + SUBS, lanes] * full, axis=0, keepdims=True)
            state = before[at : at + SUBS, lanes] + power[at : at + SUBS, lanes] * arrived
            state = state + power_less[at : at + SUBS, lanes] * own[0:1, :]
            start[at : at + SUBS, lanes] = state * weight[at : at + SUBS, lanes]

        def step(t, states, extra, fixed):
            out = None
            later = []
            for n in range(MODES):
                at = n * SUBS
                state = decay[at : at + SUBS, lanes] * states[n]
                if extra is not None:
                    state = state + weight[at : at + SUBS, lanes] * extra
                later.append(state)
                out = state if out is None else out + state
            rows = pl.ds(pl.multiple_of(t * SUBS, SUBS), SUBS)
            q_now = gate[rows, lanes]
            if fixed is not None:
                q_now = jnp.where(head, fixed, q_now)
            whole[g, pl.ds(t, SUBS, stride=chunk), :] = q_now * (out + local[rows, lanes])
            return later

        states = [start[n * SUBS : (n + 1) * SUBS, lanes] for n in range(MODES)]
        unroll = 8
        for t in range(unroll):
            first = t < REACH
            extra = jnp.where(head, kv[t], 0.0) if first else None
            states = step(t, states, extra, q[t] if first else None)

        def steps(i, states):
            for u in range(unroll):
                states = step(i * unroll + u, states, None, None)
            return states

        lax.fori_loop(1, chunk // unroll, steps, states)
    for g in range(width // LANES):
        mixed[:, g * LANES : (g + 1) * LANES] = whole[g].astype(BF16)


def out_kernel(begin, layout, fresh, last, w, *refs):
    count = sum(len(p) for p in layout)
    pieces = refs[:count]
    rest = list(refs[count:])
    acc_in = None if fresh else rest.pop(0)
    tokens = rest.pop(0) if last else None
    out = rest.pop(0)
    tile = 256
    for r in range(out.shape[0] // tile):
        rows = pl.ds(r * tile, tile)
        total = None if fresh else acc_in[rows, :]
        for i, parts in enumerate(layout):
            x = refs_rows(pieces, parts, r, tile)
            part = jnp.dot(x, w[begin + i], preferred_element_type=F32)
            total = part if total is None else total + part
        if last:
            total = total + tokens[rows, :].astype(F32)
        out[rows, :] = total.astype(out.dtype)


def out_project(begin, pieces, w, state, tokens=None):
    layout, flat = number(pieces)
    rows = flat[0].shape[0] * len(layout[0])
    last = tokens is not None
    ins = [w] + flat + ([] if state is None else [state]) + ([tokens] if last else [])

    def kernel(*refs):
        out_kernel(begin, layout, state is None, last, *refs)

    outs = jax.ShapeDtypeStruct((rows, 256), BF16 if last else F32)
    aliases = {1 + len(flat): 0} if (state is not None and not last) else {}
    return call(
        kernel, outs, ins, [VMEM] * len(ins), [], 12, len(pieces) * 2 * rows * 256 * 256, aliases
    )


def shifted(x, dy, dz, dc):
    pairs = []
    for i in range(16):
        y, z, c = i // 4, (i // 2) % 2, i % 2
        pairs.append((i, ((y + dy) % 4) * 4 + ((z + dz) % 2) * 2 + (c + dc) % 2))
    return lax.ppermute(x, "tp", pairs)


def gather(x):
    half = x.shape[0] // 2
    other = lambda p: shifted(p, 0, 0, 1)
    left = shifted(x, 1, 0, 0)
    right = shifted(x, -1, 0, 0)
    up = shifted(x, 0, 1, 0)
    far = (shifted(left[:half], 1, 0, 0), shifted(right[half:], -1, 0, 0))
    up_left = shifted(up, 1, 0, 0)
    up_right = shifted(up, -1, 0, 0)
    up_far = tuple(shifted(p, 0, 1, 0) for p in far)
    groups = [[x], [left, right], [up], [far], [up_left, up_right], [up_far]]
    result = []
    for group in groups:
        pieces = []
        for p in group:
            pieces.append(p)
            pieces.append(tuple(other(h) for h in p) if isinstance(p, tuple) else other(p))
        result.append(pieces)
    return result


def body(tokens, norm_gain, w_in, w_short, decay_rate, residue, w_out):
    length, chans = tokens.shape
    chunk = length // SUBS
    me = lax.axis_index("tp")
    y, z, c = me // 4, (me // 2) % 2, me % 2
    places = [(0, 0), (-1, 0), (1, 0), (0, 1), (2, 0), (-1, 1), (1, 1), (2, 1)]
    order = jnp.stack(
        [
            ((y + dy) % 4) * 4 + ((z + dz) % 2) * 2 + (c + dc) % 2
            for dy, dz in places
            for dc in (0, 1)
        ]
    ).astype(jnp.int32)
    first, second = pl.pallas_call(
        order_kernel,
        out_shape=[
            jax.ShapeDtypeStruct((16, 3, chans, chans), BF16),
            jax.ShapeDtypeStruct((16, chans, chans), BF16),
        ],
        in_specs=[SMEM, HBM, HBM],
        out_specs=[VMEM, VMEM],
        scratch_shapes=[pltpu.SemaphoreType.DMA((2, 16))],
        compiler_params=pltpu.CompilerParams(vmem_limit_bytes=2 * MIB),
        cost_estimate=pl.CostEstimate(flops=0, bytes_accessed=8 * MIB, transcendentals=0),
    )(order, w_in.transpose(1, 0, 2), w_out)

    rate = decay_rate.T
    gain = norm_gain.reshape(16, chans)

    def rows8(table):
        return jnp.broadcast_to(table[:, None, :], (table.shape[0], SUBS, chans)).reshape(-1, chans)

    def powers(counts):
        counts = jnp.asarray(counts, F32)
        return jnp.exp(-rate[:, None, :] * counts[None, :, None])

    decay = rows8(jnp.exp(-rate))
    weight = rows8((residue * jnp.sqrt(decay_rate)).T)
    taps = rows8(w_short.reshape(SPAN * 3, chans))
    jumps = jnp.concatenate([jnp.exp(-rate * (chunk * hop)) for hop in (1, 2, 4)])
    power = powers([chunk * k for k in range(SUBS)])
    off = jnp.zeros((MODES, 1, chans), F32)
    power_less = jnp.concatenate([off, power[:, :-1]], axis=1).reshape(-1, chans)
    ahead = jnp.concatenate([off, powers([length * d for d in range(7)])], axis=1).reshape(-1, chans)
    power = power.reshape(-1, chans)
    early = jnp.concatenate([jnp.exp(-rate * (chunk - 1 - t)) for t in range(REACH)])
    late = jnp.concatenate([jnp.exp(-rate * (length - 1 - t)) for t in range(REACH)])

    groups = gather(tokens)
    state = None
    begin = 0
    for pieces in groups[:-1]:
        state = project(begin, pieces, order, gain, first, state)
        begin += len(pieces)
    layout, flat = number(groups[-1])
    ins = [order, gain, first] + flat + list(state) + [taps, decay, weight, jumps]

    def kernel(*refs):
        local_kernel(begin, layout, chunk, *refs)

    gate, local, before, load = call(
        kernel,
        [
            jax.ShapeDtypeStruct((length, chans), F32),
            jax.ShapeDtypeStruct((length, chans), F32),
            jax.ShapeDtypeStruct((MODES * SUBS, chans), F32),
            jax.ShapeDtypeStruct((64, chans), F32),
        ],
        ins,
        [SMEM] + [VMEM] * (len(ins) - 1),
        [pltpu.VMEM((3 * chans // LANES, length + 8, LANES), F32)],
        20,
        4 * 10**9,
    )
    loads = [load]
    for d in range(1, 8):
        loads.append(lax.ppermute(load, "ctx", [(i, i + d) for i in range(8 - d)]))
    ins = loads + [gate, local, before, taps, decay, weight, power, power_less, ahead, early, late]

    def kernel_two(*refs):
        join_kernel(chunk, *refs)

    mixed = call(
        kernel_two,
        jax.ShapeDtypeStruct((length, chans), BF16),
        ins,
        [VMEM] * len(ins),
        [
            pltpu.VMEM((chans // LANES, 9 * 64, LANES), F32),
            pltpu.VMEM((chans // LANES, length, LANES), F32),
            pltpu.VMEM((MODES * SUBS, chans), F32),
        ],
        12,
        2 * 10**9,
    )
    groups = gather(mixed)
    acc = None
    begin = 0
    for pieces in groups[:-1]:
        acc = out_project(begin, pieces, second, acc)
        begin += len(pieces)
    return out_project(begin, groups[-1], second, acc, tokens)


def solution(mesh):
    placed = (
        P("ctx", "tp"),
        P(),
        P(None, None, "tp"),
        P(None, None, "tp"),
        P("tp", None),
        P("tp", None),
        P(None, "tp"),
    )
    return jax.shard_map(
        body, mesh=mesh, in_specs=placed, out_specs=P("ctx", "tp"), check_vma=False
    )
```

time: 450 us -> 149 us (0.33)
  waiting for transfers between devices: 180 us -> 28.4 us
  local copies, waits for them, and re-layouts: 150 us -> 10.3 us
  starting transfers between devices: 4.39 us -> 64.7 us
  matrix products: 42.4 us -> 0 us
  Pallas kernels: 0 us -> 32.7 us
  other arithmetic: 38.9 us -> 10.3 us
  blocking collectives: 16.4 us -> 0 us
  between operations: 14 us -> 0.62 us
    all_gather x2 -> x0, waiting for transfers between devices: 157 us -> none  [the longest x1 86.3 us: body(): whole = lax.all_gather(tokens, 'tp', axis=1, tiled=True)]
    pad x8 -> x0, local copies, waits for them, and re-layouts: 74.7 us -> none  [modal_local(): lax.associative_scan(link_states, (factors, block_end), axis=2)[1]]
    ppermute x0 -> x45, starting transfers between devices: none -> 64.7 us  [the longest x38 48 us: shifted(): return lax.ppermute(x, 'tp', pairs)]
    slice x20 -> x4, local copies, waits for them, and re-layouts: 57.1 us -> 0.07 us  [gather(): far = (shifted(left[:half], 1, 0, 0), shifted(right[half:], -1, 0, 0))]
    dot_general x4 -> x0, matrix products: 42.4 us -> none  [the longest x1 16 us: modal_local(): jnp.einsum('cn,cnbt->cbt', weight_res, fall[:, :, None, :] * running, pre...]
    pallas_call x0 -> x14, Pallas kernels: none -> 32.7 us  [the longest x13 28.1 us: call(): pl.pallas_call(kernel, out_shape=outs, in_specs=specs, out_specs=[VMEM] *...]
    ppermute x0 -> x45, waiting for transfers between devices: none -> 28.4 us  [the longest x38 26.6 us: shifted(): return lax.ppermute(x, 'tp', pairs)]
    all_to_all x1 -> x0, waiting for transfers between devices: 22.1 us -> none  [body(): moved = lax.all_to_all(proj, 'ctx', split_axis=1, concat_axis=2, tiled=True)]
  transfers between devices with their start and end apart: 3 -> 45, of which waited for: 3 -> 8; matrix products, arithmetic and copies ran while one was open for 1% -> 10% of each run, Pallas kernels for 0% -> 14%
where the time goes in v1:
time: 149 us; the launch traced here: 147 us
  starting transfers between devices  64.7 us (43%)
  Pallas kernels  32.7 us (22%)
  waiting for transfers between devices  28.4 us (19%)
  local copies, waits for them, and re-layouts  10.3 us (7%)
  other arithmetic  10.3 us (7%)
    ppermute x38, starting transfers between devices, shifted(): return lax.ppermute(x, 'tp', pairs)  48 us
    pallas_call x13, Pallas kernels, call(): pl.pallas_call(kernel, out_shape=outs, in_specs=specs, out_specs=[VMEM] *...  28.1 us
    ppermute x38, waiting for transfers between devices, shifted(): return lax.ppermute(x, 'tp', pairs)  26.6 us
    ppermute x7, starting transfers between devices, body(): loads.append(lax.ppermute(load, 'ctx', [(i, i + d) for i in range(8 - d)]))  16.7 us
    unnamed x45, local copies, waits for them, and re-layouts  6.65 us
    unnamed x9, other arithmetic  6.53 us
    pallas_call x1, Pallas kernels, body(): pl.pallas_call(order_kernel, out_shape=[jax.ShapeDtypeStruct((16, 3, chan...  4.62 us
  transfers between devices with their start and end apart: 45, of which 8 were waited for; matrix products, arithmetic and copies ran while one was open for 10% of the time, Pallas kernels for 14%

profile of v1, /device:TPU:1, one launch (start us, length us, event | category | flops | bytes accessed | tf_op | source)
XLA Modules:
  0.0 147.0 jit_solution(4726118605094347447)
XLA Ops:
  0.0 1.4 collective-permute-start.18
  1.4 1.4 collective-permute-start
  2.8 1.4 collective-permute-start.3
  4.2 3.6 %collective-permute-start.8 = (bf16[1024,256]{1,0:T(8,128)(2,1)}, bf16[1024,256]{1,0:T(8,128)(2,1)}, u32[]{:S(2)}, u32[]{:S(2)}) collective-permute-start(bf16[1024,256]{1,0:T(8,128)(2,1)} %refs_6_.1), channel_id=1, source_target_pairs={{0,2},{1,3},{2,0},{3,1},{4,6},{5,7},{6,4},{7,5},{8,10},{9,11},{10,... | collective-permute-start | bytes 1572872 | tf_op jit(solution)/shard_map/ppermute | solution.py:326
  15.3 1.5 %multiply_exponential_fusion = (f32[16,7,256]{2,1,0:T(8,128)}, f32[16,7,256]{2,1,0:T(8,128)}) fusion(f32[16,256]{1,0:T(8,128)S(1)} %get-tuple-element.45, f32[7]{0:T(128)} %constant.197.clone, f32[7]{0:T(128)} %bitcast.69), kind=kLoop, calls=%fused_computation.3 | loop fusion | flops 57344 | bytes 245816 | tf_op jit(solution)/shard_map/exp | solution.py:384
  17.0 2.7 %collective-permute-start.4 = (bf16[512,256]{1,0:T(8,128)(2,1)S(1)}, bf16[512,256]{1,0:T(8,128)(2,1)}, u32[]{:S(2)}, u32[]{:S(2)}) collective-permute-start(bf16[512,256]{1,0:T(8,128)(2,1)S(1)} %slice.21), channel_id=1, source_target_pairs={{0,12},{1,13},{2,14},{3,15},{4,0},{5,1},{6,2},{7,3},{8,4},{9,5},{1... | collective-permute-start | bytes 786440 | tf_op jit(solution)/shard_map/ppermute | solution.py:326
  20.4 1.4 collective-permute-start.16
  21.8 2.7 %collective-permute-start.11 = (bf16[1024,256]{1,0:T(8,128)(2,1)}, bf16[1024,256]{1,0:T(8,128)(2,1)}, u32[]{:S(2)}, u32[]{:S(2)}) collective-permute-start(bf16[1024,256]{1,0:T(8,128)(2,1)} %collective-permute-done.8.refs_3_), channel_id=1, source_target_pairs={{0,12},{1,13},{2,14},{3,15},{4,0},{5,1},{6,2},{7,3},{8,4},{9,5},{1... | collective-permute-start | bytes 1572872 | tf_op jit(solution)/shard_map/ppermute | solution.py:326
  25.3 2.0 %collective-permute-start.17 = (bf16[1024,256]{1,0:T(8,128)(2,1)S(1)}, bf16[1024,256]{1,0:T(8,128)(2,1)S(1)}, u32[]{:S(2)}, u32[]{:S(2)}) collective-permute-start(bf16[1024,256]{1,0:T(8,128)(2,1)S(1)} %collective-permute-done.3.refs_5_), channel_id=1, source_target_pairs={{0,1},{1,0},{2,3},{3,2},{4,5},{5,4},{6,7},{7,6},{8,9},{9,8},{10,11... | collective-permute-start | bytes 1572872 | tf_op jit(solution)/shard_map/ppermute | solution.py:326
  28.7 0.8 copy-done.3
  30.0 7.3 %collective-permute-done.9.refs_3_ = bf16[1024,256]{1,0:T(8,128)(2,1)} collective-permute-done((bf16[1024,256]{1,0:T(8,128)(2,1)}, bf16[1024,256]{1,0:T(8,128)(2,1)}, u32[]{:S(2)}, u32[]{:S(2)}) %collective-permute-start.9) | collective-permute-done | bytes 524320 | tf_op jit(solution)/shard_map/ppermute | solution.py:326
  37.4 0.8 collective-permute-start.10
  38.9 0.8 copy-done.7
  39.8 3.3 %collective-permute-start.2 = (bf16[512,256]{1,0:T(8,128)(2,1)S(1)}, bf16[512,256]{1,0:T(8,128)(2,1)}, u32[]{:S(2)}, u32[]{:S(2)}) collective-permute-start(bf16[512,256]{1,0:T(8,128)(2,1)S(1)} %collective-permute-done.1.refs_3_), channel_id=1, source_target_pairs={{0,2},{1,3},{2,0},{3,1},{4,6},{5,7},{6,4},{7,5},{8,10},{9,11},{10,... | collective-permute-start | bytes 786440 | tf_op jit(solution)/shard_map/ppermute | solution.py:326
  43.1 0.8 copy-done.5
  45.9 2.8 %copy-done = bf16[4096,3,256]{2,0,1:T(8,128)(2,1)S(1)} copy-done((bf16[4096,3,256]{2,0,1:T(8,128)(2,1)S(1)}, bf16[4096,3,256]{2,0,1:T(8,128)(2,1)}, u32[]{:S(2)}) %copy-start) | copy-done | bytes 6291480
  49.3 4.6 %shard_map.91 = (bf16[16,3,256,256]{3,2,1,0:T(8,128)(2,1)S(1)}, bf16[16,256,256]{2,1,0:T(8,128)(2,1)S(1)}) custom-call(s32[16]{0:T(128)S(1)} %copy-done.13, bf16[3,4096,256]{2,1,0:T(8,128)(2,1)S(1)} %bitcast.68, bf16[4096,256]{1,0:T(8,128)(2,1)S(1)} %copy-done.1), custom_call_target="tpu_custom_call" | custom-call | bytes 8388608 | tf_op jit(solution)/shard_map/pallas_call | solution.py:363
  53.9 0.9 collective-permute-start.14
  54.8 2.1 %shard_map.92 = (f32[1024,768]{1,0:T(8,128)S(1)}, f32[1024,128]{1,0:T(8,128)S(1)}) custom-call(s32[16]{0:T(128)S(1)} %copy-done.14, f32[16,256]{1,0:T(8,128)S(1)} %reshape.28.refs_1_, bf16[16,3,256,256]{3,2,1,0:T(8,128)(2,1)S(1)} %get-tuple-element.22.refs_2_, bf16[1024,256]{1,0:T(8,128)(2,1)S(1)} %copy-done.2, bf16[1024,256]{1,0:T(8,128)(2,1)} %collective-permute-done.18.refs_4_), custom_call_target="tpu_custom_call" | custom-call | flops 805306368 | bytes 1839120 | tf_op jit(solution)/shard_map/pallas_call | solution.py:23
  57.0 2.7 %shard_map.93 = (f32[1024,768]{1,0:T(8,128)S(1)}, f32[1024,128]{1,0:T(8,128)S(1)}) custom-call(s32[16]{0:T(128)S(1)} %copy-done.14, f32[16,256]{1,0:T(8,128)S(1)} %reshape.28.refs_1_, bf16[16,3,256,256]{3,2,1,0:T(8,128)(2,1)S(1)} %get-tuple-element.22.refs_2_, ...), custom_call_target="tpu_custom_call", output_to_operand_aliasing={{0}: (7, {}), {1}: (8, {})} | custom-call | flops 1610612736 | bytes 3018768 | tf_op jit(solution)/shard_map/pallas_call | solution.py:23
  60.3 2.3 %shard_map.94 = (f32[1024,768]{1,0:T(8,128)S(1)}, f32[1024,128]{1,0:T(8,128)S(1)}) custom-call(s32[16]{0:T(128)S(1)} %copy-done.14, f32[16,256]{1,0:T(8,128)S(1)} %reshape.28.refs_1_, bf16[16,3,256,256]{3,2,1,0:T(8,128)(2,1)S(1)} %get-tuple-element.22.refs_2_, ...), custom_call_target="tpu_custom_call", output_to_operand_aliasing={{0}: (5, {}), {1}: (6, {})} | custom-call | flops 805306368 | bytes 2756624 | tf_op jit(solution)/shard_map/pallas_call | solution.py:23
  62.6 2.3 %shard_map.95 = (f32[1024,768]{1,0:T(8,128)S(1)}, f32[1024,128]{1,0:T(8,128)S(1)}) custom-call(s32[16]{0:T(128)S(1)} %copy-done.14, f32[16,256]{1,0:T(8,128)S(1)} %reshape.28.refs_1_, bf16[16,3,256,256]{3,2,1,0:T(8,128)(2,1)S(1)} %get-tuple-element.22.refs_2_, ...), custom_call_target="tpu_custom_call", output_to_operand_aliasing={{0}: (7, {}), {1}: (8, {})} | custom-call | flops 805306368 | bytes 2756624 | tf_op jit(solution)/shard_map/pallas_call | solution.py:23
  65.0 3.7 %shard_map.96 = (f32[1024,768]{1,0:T(8,128)S(1)}, f32[1024,128]{1,0:T(8,128)S(1)}) custom-call(s32[16]{0:T(128)S(1)} %copy-done.14, f32[16,256]{1,0:T(8,128)S(1)} %reshape.28.refs_1_, bf16[16,3,256,256]{3,2,1,0:T(8,128)(2,1)S(1)} %get-tuple-element.22.refs_2_, ...), custom_call_target="tpu_custom_call", output_to_operand_aliasing={{0}: (7, {}), {1}: (8, {})} | custom-call | flops 1610612736 | bytes 3018768 | tf_op jit(solution)/shard_map/pallas_call | solution.py:23
  68.9 8.7 %shard_map.97 = (f32[1024,256]{1,0:T(8,128)S(1)}, f32[1024,256]{1,0:T(8,128)S(1)}, f32[128,256]{1,0:T(8,128)S(1)}, f32[64,256]{1,0:T(8,128)S(1)}) custom-call(s32[16]{0:T(128)S(1)} %copy-done.14, f32[16,256]{1,0:T(8,128)S(1)} %reshape.28.refs_1_, bf16[16,3,256,256]{3,2,1,0:T(8,128)(2,1)S(1)} %get-tuple-element.22.refs_2_, ...), custom_call_target="tpu_custom_call" | custom-call | flops 4000000000 | bytes 2877456 | tf_op jit(solution)/shard_map/pallas_call | solution.py:23
  77.5 3.1 %collective-permute-start.19 = (f32[64,256]{1,0:T(8,128)S(1)}, f32[64,256]{1,0:T(8,128)S(1)}, u32[]{:S(2)}, u32[]{:S(2)}) collective-permute-start(f32[64,256]{1,0:T(8,128)S(1)} %get-tuple-element.33.refs_0_), channel_id=1, source_target_pairs={{0,16},{16,32},{32,48},{48,64},{64,80},{80,96},{96,112},{1,17},{17... | collective-permute-start | bytes 196616 | tf_op jit(solution)/shard_map/ppermute | solution.py:426
  80.7 4.4 %collective-permute-start.20 = (f32[64,256]{1,0:T(8,128)S(1)}, f32[64,256]{1,0:T(8,128)S(1)}, u32[]{:S(2)}, u32[]{:S(2)}) collective-permute-start(f32[64,256]{1,0:T(8,128)S(1)} %get-tuple-element.33.refs_0_), channel_id=1, source_target_pairs={{0,32},{16,48},{32,64},{48,80},{64,96},{80,112},{1,33},{17,49},{33... | collective-permute-start | bytes 196616 | tf_op jit(solution)/shard_map/ppermute | solution.py:426
  85.1 4.1 %collective-permute-start.21 = (f32[64,256]{1,0:T(8,128)S(1)}, f32[64,256]{1,0:T(8,128)S(1)}, u32[]{:S(2)}, u32[]{:S(2)}) collective-permute-start(f32[64,256]{1,0:T(8,128)S(1)} %get-tuple-element.33.refs_0_), channel_id=1, source_target_pairs={{0,48},{16,64},{32,80},{48,96},{64,112},{1,49},{17,65},{33,81},{49... | collective-permute-start | bytes 196616 | tf_op jit(solution)/shard_map/ppermute | solution.py:426
  89.2 1.3 collective-permute-start.22
  90.5 1.3 collective-permute-start.23
  91.8 1.3 collective-permute-start.24
  93.1 1.3 collective-permute-start.25
  95.0 1.3 collective-permute-done.25.refs_7_
  96.3 2.1 %shard_map.98.refs_1_ = bf16[1024,256]{1,0:T(8,128)(2,1)S(1)} custom-call(f32[64,256]{1,0:T(8,128)S(1)} %get-tuple-element.33.refs_0_, f32[64,256]{1,0:T(8,128)S(1)} %collective-permute-done.19.refs_1_, f32[64,256]{1,0:T(8,128)S(1)} %collective-permute-done.20.refs_2_, f32[64,256]{1,0:T(8,128)S(1)} %collective-permute-done.21.refs_3_, ...), custom_call_target="tpu_custom_call" | custom-call | flops 2000000000 | bytes 944128 | tf_op jit(solution)/shard_map/pallas_call | solution.py:23
  98.5 2.7 %collective-permute-start.29 = (bf16[1024,256]{1,0:T(8,128)(2,1)S(1)}, bf16[1024,256]{1,0:T(8,128)(2,1)S(1)}, u32[]{:S(2)}, u32[]{:S(2)}) collective-permute-start(bf16[1024,256]{1,0:T(8,128)(2,1)S(1)} %shard_map.98.refs_1_), channel_id=1, source_target_pairs={{0,12},{1,13},{2,14},{3,15},{4,0},{5,1},{6,2},{7,3},{8,4},{9,5},{1... | collective-permute-start | bytes 1572872 | tf_op jit(solution)/shard_map/ppermute | solution.py:326
  101.2 3.4 %collective-permute-start.34 = (bf16[1024,256]{1,0:T(8,128)(2,1)S(1)}, bf16[1024,256]{1,0:T(8,128)(2,1)S(1)}, u32[]{:S(2)}, u32[]{:S(2)}) collective-permute-start(bf16[1024,256]{1,0:T(8,128)(2,1)S(1)} %shard_map.98.refs_1_), channel_id=1, source_target_pairs={{0,2},{1,3},{2,0},{3,1},{4,6},{5,7},{6,4},{7,5},{8,10},{9,11},{10,... | collective-permute-start | bytes 1572872 | tf_op jit(solution)/shard_map/ppermute | solution.py:326
  104.5 2.0 %collective-permute-start.44 = (bf16[1024,256]{1,0:T(8,128)(2,1)S(1)}, bf16[1024,256]{1,0:T(8,128)(2,1)S(1)}, u32[]{:S(2)}, u32[]{:S(2)}) collective-permute-start(bf16[1024,256]{1,0:T(8,128)(2,1)S(1)} %shard_map.98.refs_1_), channel_id=1, source_target_pairs={{0,1},{1,0},{2,3},{3,2},{4,5},{5,4},{6,7},{7,6},{8,9},{9,8},{10,11... | collective-permute-start | bytes 1572872 | tf_op jit(solution)/shard_map/ppermute | solution.py:326
  106.5 5.5 %collective-permute-done.26.refs_1_ = bf16[1024,256]{1,0:T(8,128)(2,1)S(1)} collective-permute-done((bf16[1024,256]{1,0:T(8,128)(2,1)S(1)}, bf16[1024,256]{1,0:T(8,128)(2,1)S(1)}, u32[]{:S(2)}, u32[]{:S(2)}) %collective-permute-start.26) | collective-permute-done | bytes 524320 | tf_op jit(solution)/shard_map/ppermute | solution.py:326
  112.1 2.7 %collective-permute-start.30 = (bf16[512,256]{1,0:T(8,128)(2,1)S(1)}, bf16[512,256]{1,0:T(8,128)(2,1)S(1)}, u32[]{:S(2)}, u32[]{:S(2)}) collective-permute-start(bf16[512,256]{1,0:T(8,128)(2,1)S(1)} %slice.24), channel_id=1, source_target_pairs={{0,12},{1,13},{2,14},{3,15},{4,0},{5,1},{6,2},{7,3},{8,4},{9,5},{1... | collective-permute-start | bytes 786440 | tf_op jit(solution)/shard_map/ppermute | solution.py:326
  114.8 4.2 %collective-permute-done.27.refs_1_ = bf16[512,256]{1,0:T(8,128)(2,1)S(1)} collective-permute-done((bf16[512,256]{1,0:T(8,128)(2,1)S(1)}, bf16[512,256]{1,0:T(8,128)(2,1)S(1)}, u32[]{:S(2)}, u32[]{:S(2)}) %collective-permute-start.27) | collective-permute-done | bytes 262176 | tf_op jit(solution)/shard_map/ppermute | solution.py:326
  119.1 3.0 %collective-permute-start.39 = (bf16[512,256]{1,0:T(8,128)(2,1)S(1)}, bf16[512,256]{1,0:T(8,128)(2,1)S(1)}, u32[]{:S(2)}, u32[]{:S(2)}) collective-permute-start(bf16[512,256]{1,0:T(8,128)(2,1)S(1)} %collective-permute-done.27.refs_1_), channel_id=1, source_target_pairs={{0,1},{1,0},{2,3},{3,2},{4,5},{5,4},{6,7},{7,6},{8,9},{9,8},{10,11... | collective-permute-start | bytes 786440 | tf_op jit(solution)/shard_map/ppermute | solution.py:326
  122.0 2.7 %collective-permute-start.37 = (bf16[1024,256]{1,0:T(8,128)(2,1)S(1)}, bf16[1024,256]{1,0:T(8,128)(2,1)S(1)}, u32[]{:S(2)}, u32[]{:S(2)}) collective-permute-start(bf16[1024,256]{1,0:T(8,128)(2,1)S(1)} %collective-permute-done.34.refs_1_), channel_id=1, source_target_pairs={{0,12},{1,13},{2,14},{3,15},{4,0},{5,1},{6,2},{7,3},{8,4},{9,5},{1... | collective-permute-start | bytes 1572872 | tf_op jit(solution)/shard_map/ppermute | solution.py:326
  124.7 3.4 %collective-permute-start.28 = (bf16[512,256]{1,0:T(8,128)(2,1)S(1)}, bf16[512,256]{1,0:T(8,128)(2,1)S(1)}, u32[]{:S(2)}, u32[]{:S(2)}) collective-permute-start(bf16[512,256]{1,0:T(8,128)(2,1)S(1)} %collective-permute-done.27.refs_1_), channel_id=1, source_target_pairs={{0,2},{1,3},{2,0},{3,1},{4,6},{5,7},{6,4},{7,5},{8,10},{9,11},{10,... | collective-permute-start | bytes 786440 | tf_op jit(solution)/shard_map/ppermute | solution.py:326
  128.2 0.8 collective-permute-start.42
  129.0 5.2 %collective-permute-done.28.refs_1_ = bf16[512,256]{1,0:T(8,128)(2,1)S(1)} collective-permute-done((bf16[512,256]{1,0:T(8,128)(2,1)S(1)}, bf16[512,256]{1,0:T(8,128)(2,1)S(1)}, u32[]{:S(2)}, u32[]{:S(2)}) %collective-permute-start.28) | collective-permute-done | bytes 262176 | tf_op jit(solution)/shard_map/ppermute | solution.py:326
  134.2 1.8 %collective-permute-start.43 = (bf16[1024,256]{1,0:T(8,128)(2,1)S(1)}, bf16[1024,256]{1,0:T(8,128)(2,1)S(1)}, u32[]{:S(2)}, u32[]{:S(2)}) collective-permute-start(bf16[1024,256]{1,0:T(8,128)(2,1)S(1)} %collective-permute-done.29.refs_3_), channel_id=1, source_target_pairs={{0,1},{1,0},{2,3},{3,2},{4,5},{5,4},{6,7},{7,6},{8,9},{9,8},{10,11... | collective-permute-start | bytes 1572872 | tf_op jit(solution)/shard_map/ppermute | solution.py:326
  136.0 3.8 %collective-permute-done.31.refs_2_ = bf16[512,256]{1,0:T(8,128)(2,1)S(1)} collective-permute-done((bf16[512,256]{1,0:T(8,128)(2,1)S(1)}, bf16[512,256]{1,0:T(8,128)(2,1)S(1)}, u32[]{:S(2)}, u32[]{:S(2)}) %collective-permute-start.31) | collective-permute-done | bytes 262176 | tf_op jit(solution)/shard_map/ppermute | solution.py:326
  139.9 1.1 collective-permute-start.41
  145.8 1.2 shard_map.104
  (128 shorter events, 20.6 us)
Async XLA Ops:
  0.0 45.9 %copy-start.1 = (bf16[4096,256]{1,0:T(8,128)(2,1)S(1)}, bf16[4096,256]{1,0:T(8,128)(2,1)}, u32[]{:S(2)}) copy-start(bf16[4096,256]{1,0:T(8,128)(2,1)} %w_out.1) | copy-start | bytes 6291460
  0.0 21.8 %collective-permute-start.18 = (bf16[1024,256]{1,0:T(8,128)(2,1)}, bf16[1024,256]{1,0:T(8,128)(2,1)}, u32[]{:S(2)}, u32[]{:S(2)}) collective-permute-start(bf16[1024,256]{1,0:T(8,128)(2,1)} %refs_6_.1), channel_id=1, source_target_pairs={{0,1},{1,0},{2,3},{3,2},{4,5},{5,4},{6,7},{7,6},{8,9},{9,8},{10,11... | collective-permute-start | bytes 1572872 | tf_op jit(solution)/shard_map/ppermute | solution.py:326
  1.4 15.4 %collective-permute-start = (bf16[1024,256]{1,0:T(8,128)(2,1)}, bf16[1024,256]{1,0:T(8,128)(2,1)S(1)}, u32[]{:S(2)}, u32[]{:S(2)}) collective-permute-start(bf16[1024,256]{1,0:T(8,128)(2,1)} %refs_6_.1), channel_id=1, source_target_pairs={{0,4},{1,5},{2,6},{3,7},{4,8},{5,9},{6,10},{7,11},{8,12},{9,13},{1... | collective-permute-start | bytes 1572872 | tf_op jit(solution)/shard_map/ppermute | solution.py:326
  2.8 14.1 %collective-permute-start.3 = (bf16[1024,256]{1,0:T(8,128)(2,1)}, bf16[1024,256]{1,0:T(8,128)(2,1)S(1)}, u32[]{:S(2)}, u32[]{:S(2)}) collective-permute-start(bf16[1024,256]{1,0:T(8,128)(2,1)} %refs_6_.1), channel_id=1, source_target_pairs={{0,12},{1,13},{2,14},{3,15},{4,0},{5,1},{6,2},{7,3},{8,4},{9,5},{1... | collective-permute-start | bytes 1572872 | tf_op jit(solution)/shard_map/ppermute | solution.py:326
  4.2 17.6 %collective-permute-start.8 = (bf16[1024,256]{1,0:T(8,128)(2,1)}, bf16[1024,256]{1,0:T(8,128)(2,1)}, u32[]{:S(2)}, u32[]{:S(2)}) collective-permute-start(bf16[1024,256]{1,0:T(8,128)(2,1)} %refs_6_.1), channel_id=1, source_target_pairs={{0,2},{1,3},{2,0},{3,1},{4,6},{5,7},{6,4},{7,5},{8,10},{9,11},{10,... | collective-permute-start | bytes 1572872 | tf_op jit(solution)/shard_map/ppermute | solution.py:326
  16.8 8.4 %collective-permute-start.1 = (bf16[512,256]{1,0:T(8,128)(2,1)S(1)}, bf16[512,256]{1,0:T(8,128)(2,1)S(1)}, u32[]{:S(2)}, u32[]{:S(2)}) collective-permute-start(bf16[512,256]{1,0:T(8,128)(2,1)S(1)} %slice.20), channel_id=1, source_target_pairs={{0,4},{1,5},{2,6},{3,7},{4,8},{5,9},{6,10},{7,11},{8,12},{9,13},{1... | collective-permute-start | bytes 786440 | tf_op jit(solution)/shard_map/ppermute | solution.py:326
  17.0 10.3 %collective-permute-start.4 = (bf16[512,256]{1,0:T(8,128)(2,1)S(1)}, bf16[512,256]{1,0:T(8,128)(2,1)}, u32[]{:S(2)}, u32[]{:S(2)}) collective-permute-start(bf16[512,256]{1,0:T(8,128)(2,1)S(1)} %slice.21), channel_id=1, source_target_pairs={{0,12},{1,13},{2,14},{3,15},{4,0},{5,1},{6,2},{7,3},{8,4},{9,5},{1... | collective-permute-start | bytes 786440 | tf_op jit(solution)/shard_map/ppermute | solution.py:326
  20.4 8.3 %collective-permute-start.16 = (bf16[1024,256]{1,0:T(8,128)(2,1)S(1)}, bf16[1024,256]{1,0:T(8,128)(2,1)S(1)}, u32[]{:S(2)}, u32[]{:S(2)}) collective-permute-start(bf16[1024,256]{1,0:T(8,128)(2,1)S(1)} %collective-permute-done.refs_3_), channel_id=1, source_target_pairs={{0,1},{1,0},{2,3},{3,2},{4,5},{5,4},{6,7},{7,6},{8,9},{9,8},{10,11... | collective-permute-start | bytes 1572872 | tf_op jit(solution)/shard_map/ppermute | solution.py:326
  21.8 15.5 %collective-permute-start.9 = (bf16[1024,256]{1,0:T(8,128)(2,1)}, bf16[1024,256]{1,0:T(8,128)(2,1)}, u32[]{:S(2)}, u32[]{:S(2)}) collective-permute-start(bf16[1024,256]{1,0:T(8,128)(2,1)} %collective-permute-done.8.refs_3_), channel_id=1, source_target_pairs={{0,4},{1,5},{2,6},{3,7},{4,8},{5,9},{6,10},{7,11},{8,12},{9,13},{1... | collective-permute-start | bytes 1572872 | tf_op jit(solution)/shard_map/ppermute | solution.py:326
  21.8 16.4 %collective-permute-start.11 = (bf16[1024,256]{1,0:T(8,128)(2,1)}, bf16[1024,256]{1,0:T(8,128)(2,1)}, u32[]{:S(2)}, u32[]{:S(2)}) collective-permute-start(bf16[1024,256]{1,0:T(8,128)(2,1)} %collective-permute-done.8.refs_3_), channel_id=1, source_target_pairs={{0,12},{1,13},{2,14},{3,15},{4,0},{5,1},{6,2},{7,3},{8,4},{9,5},{1... | collective-permute-start | bytes 1572872 | tf_op jit(solution)/shard_map/ppermute | solution.py:326
  25.3 13.7 %collective-permute-start.17 = (bf16[1024,256]{1,0:T(8,128)(2,1)S(1)}, bf16[1024,256]{1,0:T(8,128)(2,1)S(1)}, u32[]{:S(2)}, u32[]{:S(2)}) collective-permute-start(bf16[1024,256]{1,0:T(8,128)(2,1)S(1)} %collective-permute-done.3.refs_5_), channel_id=1, source_target_pairs={{0,1},{1,0},{2,3},{3,2},{4,5},{5,4},{6,7},{7,6},{8,9},{9,8},{10,11... | collective-permute-start | bytes 1572872 | tf_op jit(solution)/shard_map/ppermute | solution.py:326
  27.3 15.8 %collective-permute-start.15 = (bf16[1024,256]{1,0:T(8,128)(2,1)}, bf16[1024,256]{1,0:T(8,128)(2,1)S(1)}, u32[]{:S(2)}, u32[]{:S(2)}) collective-permute-start(bf16[1024,256]{1,0:T(8,128)(2,1)} %collective-permute-done.8.refs_3_), channel_id=1, source_target_pairs={{0,1},{1,0},{2,3},{3,2},{4,5},{5,4},{6,7},{7,6},{8,9},{9,8},{10,11... | collective-permute-start | bytes 1572872 | tf_op jit(solution)/shard_map/ppermute | solution.py:326
  29.5 24.4 %collective-permute-start.13 = (bf16[512,256]{1,0:T(8,128)(2,1)S(1)}, bf16[512,256]{1,0:T(8,128)(2,1)}, u32[]{:S(2)}, u32[]{:S(2)}) collective-permute-start(bf16[512,256]{1,0:T(8,128)(2,1)S(1)} %collective-permute-done.1.refs_3_), channel_id=1, source_target_pairs={{0,1},{1,0},{2,3},{3,2},{4,5},{5,4},{6,7},{7,6},{8,9},{9,8},{10,11... | collective-permute-start | bytes 786440 | tf_op jit(solution)/shard_map/ppermute | solution.py:326
  37.4 27.6 %collective-permute-start.10 = (bf16[1024,256]{1,0:T(8,128)(2,1)}, bf16[1024,256]{1,0:T(8,128)(2,1)}, u32[]{:S(2)}, u32[]{:S(2)}) collective-permute-start(bf16[1024,256]{1,0:T(8,128)(2,1)} %collective-permute-done.9.refs_3_), channel_id=1, source_target_pairs={{0,1},{1,0},{2,3},{3,2},{4,5},{5,4},{6,7},{7,6},{8,9},{9,8},{10,11... | collective-permute-start | bytes 1572872 | tf_op jit(solution)/shard_map/ppermute | solution.py:326
  38.2 26.8 %collective-permute-start.12 = (bf16[1024,256]{1,0:T(8,128)(2,1)}, bf16[1024,256]{1,0:T(8,128)(2,1)}, u32[]{:S(2)}, u32[]{:S(2)}) collective-permute-start(bf16[1024,256]{1,0:T(8,128)(2,1)} %collective-permute-done.11.refs_5_), channel_id=1, source_target_pairs={{0,1},{1,0},{2,3},{3,2},{4,5},{5,4},{6,7},{7,6},{8,9},{9,8},{10,11... | collective-permute-start | bytes 1572872 | tf_op jit(solution)/shard_map/ppermute | solution.py:326
  39.8 19.9 %collective-permute-start.2 = (bf16[512,256]{1,0:T(8,128)(2,1)S(1)}, bf16[512,256]{1,0:T(8,128)(2,1)}, u32[]{:S(2)}, u32[]{:S(2)}) collective-permute-start(bf16[512,256]{1,0:T(8,128)(2,1)S(1)} %collective-permute-done.1.refs_3_), channel_id=1, source_target_pairs={{0,2},{1,3},{2,0},{3,1},{4,6},{5,7},{6,4},{7,5},{8,10},{9,11},{10,... | collective-permute-start | bytes 786440 | tf_op jit(solution)/shard_map/ppermute | solution.py:326
  43.9 15.9 %collective-permute-start.5 = (bf16[512,256]{1,0:T(8,128)(2,1)}, bf16[512,256]{1,0:T(8,128)(2,1)}, u32[]{:S(2)}, u32[]{:S(2)}) collective-permute-start(bf16[512,256]{1,0:T(8,128)(2,1)} %collective-permute-done.4.refs_4_), channel_id=1, source_target_pairs={{0,2},{1,3},{2,0},{3,1},{4,6},{5,7},{6,4},{7,5},{8,10},{9,11},{10,... | collective-permute-start | bytes 786440 | tf_op jit(solution)/shard_map/ppermute | solution.py:326
  53.9 8.7 %collective-permute-start.14 = (bf16[512,256]{1,0:T(8,128)(2,1)}, bf16[512,256]{1,0:T(8,128)(2,1)S(1)}, u32[]{:S(2)}, u32[]{:S(2)}) collective-permute-start(bf16[512,256]{1,0:T(8,128)(2,1)} %collective-permute-done.4.refs_4_), channel_id=1, source_target_pairs={{0,1},{1,0},{2,3},{3,2},{4,5},{5,4},{6,7},{7,6},{8,9},{9,8},{10,11... | collective-permute-start | bytes 786440 | tf_op jit(solution)/shard_map/ppermute | solution.py:326
  59.7 9.1 %collective-permute-start.6 = (bf16[512,256]{1,0:T(8,128)(2,1)}, bf16[512,256]{1,0:T(8,128)(2,1)S(1)}, u32[]{:S(2)}, u32[]{:S(2)}) collective-permute-start(bf16[512,256]{1,0:T(8,128)(2,1)} %collective-permute-done.2.refs_3_), channel_id=1, source_target_pairs={{0,1},{1,0},{2,3},{3,2},{4,5},{5,4},{6,7},{7,6},{8,9},{9,8},{10,11... | collective-permute-start | bytes 786440 | tf_op jit(solution)/shard_map/ppermute | solution.py:326
  59.8 9.0 %collective-permute-start.7 = (bf16[512,256]{1,0:T(8,128)(2,1)}, bf16[512,256]{1,0:T(8,128)(2,1)S(1)}, u32[]{:S(2)}, u32[]{:S(2)}) collective-permute-start(bf16[512,256]{1,0:T(8,128)(2,1)} %collective-permute-done.5.refs_4_), channel_id=1, source_target_pairs={{0,1},{1,0},{2,3},{3,2},{4,5},{5,4},{6,7},{7,6},{8,9},{9,8},{10,11... | collective-permute-start | bytes 786440 | tf_op jit(solution)/shard_map/ppermute | solution.py:326
  68.8 25.6 %copy-start.20 = (f32[16,7,256]{2,1,0:T(8,128)S(1)}, f32[16,7,256]{2,1,0:T(8,128)}, u32[]{:S(2)}) copy-start(f32[16,7,256]{2,1,0:T(8,128)} %get-tuple-element.43) | copy-start | bytes 344068
  68.9 27.4 %copy-start.18 = (f32[96,256]{1,0:T(8,128)S(1)}, f32[96,256]{1,0:T(8,128)}, u32[]{:S(2)}) copy-start(f32[96,256]{1,0:T(8,128)} %copy-done.17) | copy-start | bytes 294916
  77.5 14.2 %collective-permute-start.19 = (f32[64,256]{1,0:T(8,128)S(1)}, f32[64,256]{1,0:T(8,128)S(1)}, u32[]{:S(2)}, u32[]{:S(2)}) collective-permute-start(f32[64,256]{1,0:T(8,128)S(1)} %get-tuple-element.33.refs_0_), channel_id=1, source_target_pairs={{0,16},{16,32},{32,48},{48,64},{64,80},{80,96},{96,112},{1,17},{17... | collective-permute-start | bytes 196616 | tf_op jit(solution)/shard_map/ppermute | solution.py:426
  80.7 12.4 %collective-permute-start.20 = (f32[64,256]{1,0:T(8,128)S(1)}, f32[64,256]{1,0:T(8,128)S(1)}, u32[]{:S(2)}, u32[]{:S(2)}) collective-permute-start(f32[64,256]{1,0:T(8,128)S(1)} %get-tuple-element.33.refs_0_), channel_id=1, source_target_pairs={{0,32},{16,48},{32,64},{48,80},{64,96},{80,112},{1,33},{17,49},{33... | collective-permute-start | bytes 196616 | tf_op jit(solution)/shard_map/ppermute | solution.py:426
  85.1 9.4 %collective-permute-start.21 = (f32[64,256]{1,0:T(8,128)S(1)}, f32[64,256]{1,0:T(8,128)S(1)}, u32[]{:S(2)}, u32[]{:S(2)}) collective-permute-start(f32[64,256]{1,0:T(8,128)S(1)} %get-tuple-element.33.refs_0_), channel_id=1, source_target_pairs={{0,48},{16,64},{32,80},{48,96},{64,112},{1,49},{17,65},{33,81},{49... | collective-permute-start | bytes 196616 | tf_op jit(solution)/shard_map/ppermute | solution.py:426
  89.2 5.3 %collective-permute-start.22 = (f32[64,256]{1,0:T(8,128)S(1)}, f32[64,256]{1,0:T(8,128)S(1)}, u32[]{:S(2)}, u32[]{:S(2)}) collective-permute-start(f32[64,256]{1,0:T(8,128)S(1)} %get-tuple-element.33.refs_0_), channel_id=1, source_target_pairs={{0,64},{16,80},{32,96},{48,112},{1,65},{17,81},{33,97},{49,113},{2... | collective-permute-start | bytes 196616 | tf_op jit(solution)/shard_map/ppermute | solution.py:426
  90.5 4.0 %collective-permute-start.23 = (f32[64,256]{1,0:T(8,128)S(1)}, f32[64,256]{1,0:T(8,128)S(1)}, u32[]{:S(2)}, u32[]{:S(2)}) collective-permute-start(f32[64,256]{1,0:T(8,128)S(1)} %get-tuple-element.33.refs_0_), channel_id=1, source_target_pairs={{0,80},{16,96},{32,112},{1,81},{17,97},{33,113},{2,82},{18,98},{34... | collective-permute-start | bytes 196616 | tf_op jit(solution)/shard_map/ppermute | solution.py:426
  91.8 3.2 %collective-permute-start.24 = (f32[64,256]{1,0:T(8,128)S(1)}, f32[64,256]{1,0:T(8,128)S(1)}, u32[]{:S(2)}, u32[]{:S(2)}) collective-permute-start(f32[64,256]{1,0:T(8,128)S(1)} %get-tuple-element.33.refs_0_), channel_id=1, source_target_pairs={{0,96},{16,112},{1,97},{17,113},{2,98},{18,114},{3,99},{19,115},{4... | collective-permute-start | bytes 196616 | tf_op jit(solution)/shard_map/ppermute | solution.py:426
  93.1 3.2 %collective-permute-start.25 = (f32[64,256]{1,0:T(8,128)S(1)}, f32[64,256]{1,0:T(8,128)S(1)}, u32[]{:S(2)}, u32[]{:S(2)}) collective-permute-start(f32[64,256]{1,0:T(8,128)S(1)} %get-tuple-element.33.refs_0_), channel_id=1, source_target_pairs={{0,112},{1,113},{2,114},{3,115},{4,116},{5,117},{6,118},{7,119},{8... | collective-permute-start | bytes 196616 | tf_op jit(solution)/shard_map/ppermute | solution.py:426
  98.4 13.6 %collective-permute-start.26 = (bf16[1024,256]{1,0:T(8,128)(2,1)S(1)}, bf16[1024,256]{1,0:T(8,128)(2,1)S(1)}, u32[]{:S(2)}, u32[]{:S(2)}) collective-permute-start(bf16[1024,256]{1,0:T(8,128)(2,1)S(1)} %shard_map.98.refs_1_), channel_id=1, source_target_pairs={{0,4},{1,5},{2,6},{3,7},{4,8},{5,9},{6,10},{7,11},{8,12},{9,13},{1... | collective-permute-start | bytes 1572872 | tf_op jit(solution)/shard_map/ppermute | solution.py:326
  98.5 13.6 %collective-permute-start.29 = (bf16[1024,256]{1,0:T(8,128)(2,1)S(1)}, bf16[1024,256]{1,0:T(8,128)(2,1)S(1)}, u32[]{:S(2)}, u32[]{:S(2)}) collective-permute-start(bf16[1024,256]{1,0:T(8,128)(2,1)S(1)} %shard_map.98.refs_1_), channel_id=1, source_target_pairs={{0,12},{1,13},{2,14},{3,15},{4,0},{5,1},{6,2},{7,3},{8,4},{9,5},{1... | collective-permute-start | bytes 1572872 | tf_op jit(solution)/shard_map/ppermute | solution.py:326
  101.2 20.9 %collective-permute-start.34 = (bf16[1024,256]{1,0:T(8,128)(2,1)S(1)}, bf16[1024,256]{1,0:T(8,128)(2,1)S(1)}, u32[]{:S(2)}, u32[]{:S(2)}) collective-permute-start(bf16[1024,256]{1,0:T(8,128)(2,1)S(1)} %shard_map.98.refs_1_), channel_id=1, source_target_pairs={{0,2},{1,3},{2,0},{3,1},{4,6},{5,7},{6,4},{7,5},{8,10},{9,11},{10,... | collective-permute-start | bytes 1572872 | tf_op jit(solution)/shard_map/ppermute | solution.py:326
  104.5 20.1 %collective-permute-start.44 = (bf16[1024,256]{1,0:T(8,128)(2,1)S(1)}, bf16[1024,256]{1,0:T(8,128)(2,1)S(1)}, u32[]{:S(2)}, u32[]{:S(2)}) collective-permute-start(bf16[1024,256]{1,0:T(8,128)(2,1)S(1)} %shard_map.98.refs_1_), channel_id=1, source_target_pairs={{0,1},{1,0},{2,3},{3,2},{4,5},{5,4},{6,7},{7,6},{8,9},{9,8},{10,11... | collective-permute-start | bytes 1572872 | tf_op jit(solution)/shard_map/ppermute | solution.py:326
  112.0 7.0 %collective-permute-start.27 = (bf16[512,256]{1,0:T(8,128)(2,1)S(1)}, bf16[512,256]{1,0:T(8,128)(2,1)S(1)}, u32[]{:S(2)}, u32[]{:S(2)}) collective-permute-start(bf16[512,256]{1,0:T(8,128)(2,1)S(1)} %slice.23), channel_id=1, source_target_pairs={{0,4},{1,5},{2,6},{3,7},{4,8},{5,9},{6,10},{7,11},{8,12},{9,13},{1... | collective-permute-start | bytes 786440 | tf_op jit(solution)/shard_map/ppermute | solution.py:326
  112.1 16.0 %collective-permute-start.30 = (bf16[512,256]{1,0:T(8,128)(2,1)S(1)}, bf16[512,256]{1,0:T(8,128)(2,1)S(1)}, u32[]{:S(2)}, u32[]{:S(2)}) collective-permute-start(bf16[512,256]{1,0:T(8,128)(2,1)S(1)} %slice.24), channel_id=1, source_target_pairs={{0,12},{1,13},{2,14},{3,15},{4,0},{5,1},{6,2},{7,3},{8,4},{9,5},{1... | collective-permute-start | bytes 786440 | tf_op jit(solution)/shard_map/ppermute | solution.py:326
  119.1 9.1 %collective-permute-start.39 = (bf16[512,256]{1,0:T(8,128)(2,1)S(1)}, bf16[512,256]{1,0:T(8,128)(2,1)S(1)}, u32[]{:S(2)}, u32[]{:S(2)}) collective-permute-start(bf16[512,256]{1,0:T(8,128)(2,1)S(1)} %collective-permute-done.27.refs_1_), channel_id=1, source_target_pairs={{0,1},{1,0},{2,3},{3,2},{4,5},{5,4},{6,7},{7,6},{8,9},{9,8},{10,11... | collective-permute-start | bytes 786440 | tf_op jit(solution)/shard_map/ppermute | solution.py:326
  122.0 18.9 %collective-permute-start.35 = (bf16[1024,256]{1,0:T(8,128)(2,1)S(1)}, bf16[1024,256]{1,0:T(8,128)(2,1)S(1)}, u32[]{:S(2)}, u32[]{:S(2)}) collective-permute-start(bf16[1024,256]{1,0:T(8,128)(2,1)S(1)} %collective-permute-done.34.refs_1_), channel_id=1, source_target_pairs={{0,4},{1,5},{2,6},{3,7},{4,8},{5,9},{6,10},{7,11},{8,12},{9,13},{1... | collective-permute-start | bytes 1572872 | tf_op jit(solution)/shard_map/ppermute | solution.py:326
  122.0 19.0 %collective-permute-start.37 = (bf16[1024,256]{1,0:T(8,128)(2,1)S(1)}, bf16[1024,256]{1,0:T(8,128)(2,1)S(1)}, u32[]{:S(2)}, u32[]{:S(2)}) collective-permute-start(bf16[1024,256]{1,0:T(8,128)(2,1)S(1)} %collective-permute-done.34.refs_1_), channel_id=1, source_target_pairs={{0,12},{1,13},{2,14},{3,15},{4,0},{5,1},{6,2},{7,3},{8,4},{9,5},{1... | collective-permute-start | bytes 1572872 | tf_op jit(solution)/shard_map/ppermute | solution.py:326
  124.7 9.5 %collective-permute-start.28 = (bf16[512,256]{1,0:T(8,128)(2,1)S(1)}, bf16[512,256]{1,0:T(8,128)(2,1)S(1)}, u32[]{:S(2)}, u32[]{:S(2)}) collective-permute-start(bf16[512,256]{1,0:T(8,128)(2,1)S(1)} %collective-permute-done.27.refs_1_), channel_id=1, source_target_pairs={{0,2},{1,3},{2,0},{3,1},{4,6},{5,7},{6,4},{7,5},{8,10},{9,11},{10,... | collective-permute-start | bytes 786440 | tf_op jit(solution)/shard_map/ppermute | solution.py:326
  128.1 11.8 %collective-permute-start.31 = (bf16[512,256]{1,0:T(8,128)(2,1)S(1)}, bf16[512,256]{1,0:T(8,128)(2,1)S(1)}, u32[]{:S(2)}, u32[]{:S(2)}) collective-permute-start(bf16[512,256]{1,0:T(8,128)(2,1)S(1)} %collective-permute-done.30.refs_2_), channel_id=1, source_target_pairs={{0,2},{1,3},{2,0},{3,1},{4,6},{5,7},{6,4},{7,5},{8,10},{9,11},{10,... | collective-permute-start | bytes 786440 | tf_op jit(solution)/shard_map/ppermute | solution.py:326
  128.2 13.3 %collective-permute-start.42 = (bf16[1024,256]{1,0:T(8,128)(2,1)S(1)}, bf16[1024,256]{1,0:T(8,128)(2,1)S(1)}, u32[]{:S(2)}, u32[]{:S(2)}) collective-permute-start(bf16[1024,256]{1,0:T(8,128)(2,1)S(1)} %collective-permute-done.26.refs_1_), channel_id=1, source_target_pairs={{0,1},{1,0},{2,3},{3,2},{4,5},{5,4},{6,7},{7,6},{8,9},{9,8},{10,11... | collective-permute-start | bytes 1572872 | tf_op jit(solution)/shard_map/ppermute | solution.py:326
  134.2 7.3 %collective-permute-start.43 = (bf16[1024,256]{1,0:T(8,128)(2,1)S(1)}, bf16[1024,256]{1,0:T(8,128)(2,1)S(1)}, u32[]{:S(2)}, u32[]{:S(2)}) collective-permute-start(bf16[1024,256]{1,0:T(8,128)(2,1)S(1)} %collective-permute-done.29.refs_3_), channel_id=1, source_target_pairs={{0,1},{1,0},{2,3},{3,2},{4,5},{5,4},{6,7},{7,6},{8,9},{9,8},{10,11... | collective-permute-start | bytes 1572872 | tf_op jit(solution)/shard_map/ppermute | solution.py:326
  139.9 2.6 %collective-permute-start.41 = (bf16[1024,256]{1,0:T(8,128)(2,1)S(1)}, bf16[1024,256]{1,0:T(8,128)(2,1)S(1)}, u32[]{:S(2)}, u32[]{:S(2)}) collective-permute-start(bf16[1024,256]{1,0:T(8,128)(2,1)S(1)} %collective-permute-done.34.refs_1_), channel_id=1, source_target_pairs={{0,1},{1,0},{2,3},{3,2},{4,5},{5,4},{6,7},{7,6},{8,9},{9,8},{10,11... | collective-permute-start | bytes 1572872 | tf_op jit(solution)/shard_map/ppermute | solution.py:326
  141.0 4.0 %collective-permute-start.36 = (bf16[1024,256]{1,0:T(8,128)(2,1)S(1)}, bf16[1024,256]{1,0:T(8,128)(2,1)S(1)}, u32[]{:S(2)}, u32[]{:S(2)}) collective-permute-start(bf16[1024,256]{1,0:T(8,128)(2,1)S(1)} %collective-permute-done.35.refs_1_), channel_id=1, source_target_pairs={{0,1},{1,0},{2,3},{3,2},{4,5},{5,4},{6,7},{7,6},{8,9},{9,8},{10,11... | collective-permute-start | bytes 1572872 | tf_op jit(solution)/shard_map/ppermute | solution.py:326
  141.0 4.0 %collective-permute-start.38 = (bf16[1024,256]{1,0:T(8,128)(2,1)S(1)}, bf16[1024,256]{1,0:T(8,128)(2,1)S(1)}, u32[]{:S(2)}, u32[]{:S(2)}) collective-permute-start(bf16[1024,256]{1,0:T(8,128)(2,1)S(1)} %collective-permute-done.37.refs_3_), channel_id=1, source_target_pairs={{0,1},{1,0},{2,3},{3,2},{4,5},{5,4},{6,7},{7,6},{8,9},{9,8},{10,11... | collective-permute-start | bytes 1572872 | tf_op jit(solution)/shard_map/ppermute | solution.py:326
  141.5 3.0 %collective-permute-start.40 = (bf16[512,256]{1,0:T(8,128)(2,1)S(1)}, bf16[512,256]{1,0:T(8,128)(2,1)S(1)}, u32[]{:S(2)}, u32[]{:S(2)}) collective-permute-start(bf16[512,256]{1,0:T(8,128)(2,1)S(1)} %collective-permute-done.30.refs_2_), channel_id=1, source_target_pairs={{0,1},{1,0},{2,3},{3,2},{4,5},{5,4},{6,7},{7,6},{8,9},{9,8},{10,11... | collective-permute-start | bytes 786440 | tf_op jit(solution)/shard_map/ppermute | solution.py:326
  141.6 4.2 %collective-permute-start.32 = (bf16[512,256]{1,0:T(8,128)(2,1)S(1)}, bf16[512,256]{1,0:T(8,128)(2,1)S(1)}, u32[]{:S(2)}, u32[]{:S(2)}) collective-permute-start(bf16[512,256]{1,0:T(8,128)(2,1)S(1)} %collective-permute-done.28.refs_1_), channel_id=1, source_target_pairs={{0,1},{1,0},{2,3},{3,2},{4,5},{5,4},{6,7},{7,6},{8,9},{9,8},{10,11... | collective-permute-start | bytes 786440 | tf_op jit(solution)/shard_map/ppermute | solution.py:326
  142.5 3.3 %collective-permute-start.33 = (bf16[512,256]{1,0:T(8,128)(2,1)S(1)}, bf16[512,256]{1,0:T(8,128)(2,1)S(1)}, u32[]{:S(2)}, u32[]{:S(2)}) collective-permute-start(bf16[512,256]{1,0:T(8,128)(2,1)S(1)} %collective-permute-done.31.refs_2_), channel_id=1, source_target_pairs={{0,1},{1,0},{2,3},{3,2},{4,5},{5,4},{6,7},{7,6},{8,9},{9,8},{10,11... | collective-permute-start | bytes 786440 | tf_op jit(solution)/shard_map/ppermute | solution.py:326
  (19 other events, 103.4 us)

commit v2 on v1

v2 whole, which is shorter than its diff:
```python
import jax
import jax.numpy as jnp
from jax import lax
from jax.experimental import pallas as pl
from jax.experimental.pallas import tpu as pltpu
from jax.sharding import PartitionSpec as P

F32 = jnp.float32
BF16 = jnp.bfloat16
MODES = 16
SPAN = 7
REACH = SPAN - 1
LANES = 128
SUBS = 8
VMEM = pl.BlockSpec(memory_space=pltpu.VMEM)
HBM = pl.BlockSpec(memory_space=pltpu.HBM)
SMEM = pl.BlockSpec(memory_space=pltpu.SMEM)
MIB = 1024 * 1024
TILE = 512


def call(kernel, outs, ins, specs, scratch, limit, flops, aliases=None):
    moved = sum(a.size * a.dtype.itemsize for a in ins)
    return pl.pallas_call(
        kernel,
        out_shape=outs,
        in_specs=specs,
        out_specs=[VMEM] * len(outs) if isinstance(outs, list) else VMEM,
        scratch_shapes=scratch,
        input_output_aliases=aliases or {},
        compiler_params=pltpu.CompilerParams(vmem_limit_bytes=limit * MIB),
        cost_estimate=pl.CostEstimate(flops=1, bytes_accessed=1, transcendentals=0),
    )(*ins)


TABLE = {}
for _name, _rows in (
    ("decay", MODES * SUBS),
    ("weight", MODES * SUBS),
    ("power", MODES * SUBS),
    ("power_less", MODES * SUBS),
    ("ahead", MODES * SUBS),
    ("taps", SPAN * 3 * SUBS),
    ("jumps", 3 * MODES),
    ("early", REACH * MODES),
    ("late", REACH * MODES),
):
    TABLE[_name] = (sum(rows for _, rows in TABLE.values()), _rows)
TABLE_ROWS = sum(rows for _, rows in TABLE.values())
PLACES = (
    ((0, 0, 0), (0, 0, 1), (0, 1, 0), (0, 1, 1), (2, 0, 0), (2, 0, 1), (2, 1, 0), (-1, 0, 0))
    + ((-1, 1, 0), (1, 0, 0), (1, 1, 0), (2, 1, 1), (-1, 0, 1), (-1, 1, 1), (1, 0, 1), (1, 1, 1))
)


def part(table, name):
    begin, rows = TABLE[name]
    return table.at[pl.ds(begin, rows)]


def order_kernel(chunk, w_in, w_out, gain, rate, residue, short, first, second, scale, table, sems):
    me = lax.axis_index("tp")
    y, z, c = me // 4, (me // 2) % 2, me % 2
    width = second.shape[1]
    copies = []
    for i in range(16):
        dy, dz, dc = PLACES[i]
        source = ((y + dy + 4) % 4) * 4 + ((z + dz) % 2) * 2 + (c + dc) % 2
        rows = pl.ds(pl.multiple_of(source * width, width), width)
        place = pl.ds(i * width, width)
        copies.append(pltpu.make_async_copy(w_in.at[:, rows, :], first.at[:, place, :], sems.at[0, i]))
        copies.append(pltpu.make_async_copy(w_out.at[rows, :], second.at[place, :], sems.at[1, i]))
        scale[i : i + 1, :] = gain[pl.ds(source, 1), :]
    for copy in copies:
        copy.start()

    length = SUBS * chunk
    sub = lax.broadcasted_iota(jnp.int32, (SUBS, width), 0)
    lag = sub.astype(F32)

    def put(name, row, value):
        at = TABLE[name][0] + row
        table[at : at + value.shape[0], :] = value

    rates = rate[...]
    for level, hop in enumerate((1, 2, 4)):
        put("jumps", level * MODES, jnp.exp(-rates * (chunk * hop)))
    for t in range(REACH):
        put("early", t * MODES, jnp.exp(-rates * (chunk - 1 - t)))
        put("late", t * MODES, jnp.exp(-rates * (length - 1 - t)))
    weights = residue[...] * jnp.sqrt(rates)
    decays = jnp.exp(-rates)
    for n in range(MODES):
        wide = jnp.broadcast_to(rates[n : n + 1, :], (SUBS, width))
        put("decay", n * SUBS, jnp.broadcast_to(decays[n : n + 1, :], (SUBS, width)))
        put("weight", n * SUBS, jnp.broadcast_to(weights[n : n + 1, :], (SUBS, width)))
        put("power", n * SUBS, jnp.exp(-wide * (lag * chunk)))
        less = jnp.exp(-wide * (jnp.maximum(lag - 1.0, 0.0) * chunk))
        put("power_less", n * SUBS, jnp.where(sub >= 1, less, 0.0))
        far = jnp.exp(-wide * (jnp.maximum(lag - 1.0, 0.0) * length))
        put("ahead", n * SUBS, jnp.where(sub >= 1, far, 0.0))
    for i in range(SPAN * 3):
        put("taps", i * SUBS, jnp.broadcast_to(short[i : i + 1, :], (SUBS, width)))
    for copy in copies:
        copy.wait()


def add_pieces(begin, layout, gain, w, refs, r, tile):
    squares = None
    scaled = []
    for number, piece in enumerate(layout):
        x = piece_rows(refs, piece, r, tile).astype(F32)
        scaled.append((x * gain[begin + number : begin + number + 1, :]).astype(BF16))
        square = x * x
        square = square[:, :LANES] + square[:, LANES:]
        squares = square if squares is None else squares + square
    scaled = jnp.concatenate(scaled, axis=1)
    rows = slice(begin * 256, (begin + len(layout)) * 256)
    total = [jnp.dot(scaled, w[s, rows, :], preferred_element_type=F32) for s in range(3)]
    return total, squares


def piece_rows(refs, piece, r, tile):
    number, first = piece
    return refs[number][pl.ds(first + r * tile, tile), :]


def proj_kernel(begin, layout, fresh, gain, w, *refs):
    count = 1 + max(p[0] for p in layout)
    pieces = refs[:count]
    if fresh:
        acc, ss = refs[count:]
    else:
        acc_in, ss_in, acc, ss = refs[count:]
    tile = TILE
    for r in range(acc.shape[0] // tile):
        rows = pl.ds(r * tile, tile)
        total, squares = add_pieces(begin, layout, gain, w, pieces, r, tile)
        for s in range(3):
            cols = slice(s * 256, (s + 1) * 256)
            acc[rows, cols] = total[s] if fresh else acc_in[rows, cols] + total[s]
        ss[rows, :] = squares if fresh else ss_in[rows, :] + squares


def number(pieces):
    layout, flat = [], []
    for piece in pieces:
        array, first = piece if isinstance(piece, tuple) else (piece, 0)
        known = [i for i, a in enumerate(flat) if a is array]
        if not known:
            flat.append(array)
        layout.append((known[0] if known else len(flat) - 1, first))
    return layout, flat


def project(length, begin, pieces, gain, w, state):
    layout, flat = number(pieces)
    rows = length
    outs = [jax.ShapeDtypeStruct((rows, 768), F32), jax.ShapeDtypeStruct((rows, LANES), F32)]
    ins = [gain, w] + flat + (list(state) if state else [])
    specs = [VMEM] * len(ins)
    fresh = state is None

    def kernel(*refs):
        proj_kernel(begin, layout, fresh, *refs)

    aliases = {} if fresh else {len(ins) - 2: 0, len(ins) - 1: 1}
    return call(kernel, outs, ins, specs, [], 16, len(pieces) * 2 * rows * 256 * 768, aliases)


def local_kernel(begin, layout, chunk, gain, w, *refs):
    count = 1 + max(p[0] for p in layout)
    pieces = refs[:count]
    acc, ss, table, gate, local, before, load, proj, last = refs[count:]
    taps, decay, weight, jumps = (part(table, n) for n in ("taps", "decay", "weight", "jumps"))
    tile = TILE
    width = gate.shape[1]
    rows_all = acc.shape[0]
    halves = width // LANES
    proj[:, 0:8, :] = jnp.zeros((3 * halves, 8, LANES), F32)
    for r in range(rows_all // tile):
        rows = pl.ds(r * tile, tile)
        total, squares = add_pieces(begin, layout, gain, w, pieces, r, tile)
        mean = jnp.sum(ss[rows, :] + squares, axis=1, keepdims=True) / (16 * width)
        scale = lax.rsqrt(mean + 1e-05)
        for s in range(3):
            cols = slice(s * 256, (s + 1) * 256)
            value = (acc[rows, cols] + total[s]) * scale
            value = value.astype(BF16).astype(F32)
            for g in range(halves):
                proj[s * halves + g, pl.ds(8 + r * tile, tile), :] = value[:, g * LANES : (g + 1) * LANES]
    head = lax.broadcasted_iota(jnp.int32, (SUBS, LANES), 0) == 0
    for g in range(width // LANES):
        lanes = slice(g * LANES, (g + 1) * LANES)

        def strided(s, t):
            return proj[s * halves + g, pl.ds(8 + t, SUBS, stride=chunk), :]

        def step(t, carry, masked):
            windows, states = carry
            short = []
            moved = []
            for s in range(3):
                newest = strided(s, t)
                line = windows[s] + [newest]
                value = None
                for j in range(SPAN):
                    at = (j * 3 + s) * SUBS
                    term = taps[at : at + SUBS, lanes] * line[REACH - j]
                    value = term if value is None else value + term
                short.append(value)
                moved.append(line[1:])
            kv = (short[1] * short[2]).astype(BF16).astype(F32)
            if masked:
                kv = jnp.where(head, 0.0, kv)
            out = None
            later = []
            for n in range(MODES):
                at = n * SUBS
                state = decay[at : at + SUBS, lanes] * states[n] + kv
                later.append(state)
                term = weight[at : at + SUBS, lanes] * state
                out = term if out is None else out + term
            place = pl.ds(pl.multiple_of(t * SUBS, SUBS), SUBS)
            gate[place, lanes] = short[0].astype(BF16).astype(F32)
            local[place, lanes] = out
            return moved, later

        windows = [
            [strided(s, t) for t in range(-REACH, 0)]
            for s in range(3)
        ]
        carry = (windows, [jnp.zeros((SUBS, LANES), F32)] * MODES)
        unroll = 8
        for t in range(unroll):
            carry = step(t, carry, t < REACH)

        def steps(i, carry):
            for u in range(unroll):
                carry = step(i * unroll + u, carry, False)
            return carry

        carry = lax.fori_loop(1, chunk // unroll, steps, carry)
        place = lax.broadcasted_iota(jnp.int32, (SUBS, LANES), 0)
        for n in range(MODES):
            at = n * SUBS
            state = carry[1][n]
            for level, hop in enumerate((1, 2, 4)):
                moved = jnp.where(place >= hop, pltpu.roll(state, hop, 0), 0.0)
                jump = jumps[level * MODES + n : level * MODES + n + 1, lanes]
                state = state + jump * moved
            before[at : at + SUBS, lanes] = jnp.where(place >= 1, pltpu.roll(state, 1, 0), 0.0)
            last[n : n + 1, lanes] = state[SUBS - 1 : SUBS, :]
    high = last[...].astype(BF16)
    low = (last[...] - high.astype(F32)).astype(BF16)
    ends = [high, low]
    for s in range(3):
        sides = []
        for g in range(halves):
            tail = proj[s * halves + g, rows_all : rows_all + 8, :]
            sides.append(jnp.concatenate([tail, proj[s * halves + g, 8:16, :]], axis=0))
        ends.append(jnp.concatenate(sides, axis=1).astype(BF16))
    for i, value in enumerate(ends):
        for d in range(8):
            load[d, i * 16 : (i + 1) * 16, :] = value


def join_kernel(chunk, *refs):
    loads, gate, local, before, table, mixed, held, whole, start = refs
    names = ("taps", "decay", "weight", "power", "power_less", "ahead", "early", "late")
    taps, decay, weight, power, power_less, ahead, early, late = (part(table, n) for n in names)
    step_rows = 64
    width = mixed.shape[1]
    me = lax.axis_index("ctx")
    for d in range(9):
        source = jnp.maximum(me - d, 0)
        value = None
        if d < 8:
            value = loads[source].astype(F32)
            value = jnp.concatenate([value[0:16] + value[16:32], value[32:]], axis=0)
            value = jnp.where(me >= d, value, 0.0)
        for g in range(width // LANES):
            piece = jnp.zeros((step_rows, LANES), F32)
            if d < 8:
                piece = value[:, g * LANES : (g + 1) * LANES]
            held[g, d * step_rows : (d + 1) * step_rows, :] = piece
    place = lax.broadcasted_iota(jnp.int32, (SUBS, LANES), 0)
    head = place == 0
    for g in range(width // LANES):
        lanes = slice(g * LANES, (g + 1) * LANES)

        def strided(row):
            return held[g, pl.ds(row, SUBS, stride=step_rows), :]

        short = []
        for s in range(3):
            line = [strided(step_rows + 16 + s * 16 + 8 - REACH + t) for t in range(REACH)]
            line += [strided(24 + s * 16 + t) for t in range(REACH)]
            values = []
            for t in range(REACH):
                value = None
                for j in range(SPAN):
                    at = (j * 3 + s) * SUBS
                    term = taps[at : at + SUBS, lanes] * line[REACH + t - j]
                    value = term if value is None else value + term
                values.append(value)
            short.append(values)
        kv = [(short[1][t] * short[2][t]).astype(BF16).astype(F32) for t in range(REACH)]
        q = [short[0][t].astype(BF16).astype(F32) for t in range(REACH)]
        for n in range(MODES):
            at = n * SUBS
            full = strided(n)
            own = None
            for t in range(REACH):
                row = t * MODES + n
                full = full + late[row : row + 1, lanes] * kv[t]
                term = early[row : row + 1, lanes] * kv[t]
                own = term if own is None else own + term
            arrived = jnp.sum(ahead[at : at + SUBS, lanes] * full, axis=0, keepdims=True)
            state = before[at : at + SUBS, lanes] + power[at : at + SUBS, lanes] * arrived
            state = state + power_less[at : at + SUBS, lanes] * own[0:1, :]
            start[at : at + SUBS, lanes] = state * weight[at : at + SUBS, lanes]

        def step(t, states, extra, fixed):
            out = None
            later = []
            for n in range(MODES):
                at = n * SUBS
                state = decay[at : at + SUBS, lanes] * states[n]
                if extra is not None:
                    state = state + weight[at : at + SUBS, lanes] * extra
                later.append(state)
                out = state if out is None else out + state
            rows = pl.ds(pl.multiple_of(t * SUBS, SUBS), SUBS)
            q_now = gate[rows, lanes]
            if fixed is not None:
                q_now = jnp.where(head, fixed, q_now)
            whole[g, pl.ds(t, SUBS, stride=chunk), :] = q_now * (out + local[rows, lanes])
            return later

        states = [start[n * SUBS : (n + 1) * SUBS, lanes] for n in range(MODES)]
        unroll = 8
        for t in range(unroll):
            first = t < REACH
            extra = jnp.where(head, kv[t], 0.0) if first else None
            states = step(t, states, extra, q[t] if first else None)

        def steps(i, states):
            for u in range(unroll):
                states = step(i * unroll + u, states, None, None)
            return states

        lax.fori_loop(1, chunk // unroll, steps, states)
    for g in range(width // LANES):
        mixed[:, g * LANES : (g + 1) * LANES] = whole[g].astype(BF16)


def out_kernel(begin, layout, fresh, last, w, *refs):
    count = 1 + max(p[0] for p in layout)
    pieces = refs[:count]
    rest = list(refs[count:])
    acc_in = None if fresh else rest.pop(0)
    tokens = rest.pop(0) if last else None
    out = rest.pop(0)
    tile = TILE
    for r in range(out.shape[0] // tile):
        rows = pl.ds(r * tile, tile)
        total = None if fresh else acc_in[rows, :]
        x = jnp.concatenate([piece_rows(pieces, p, r, tile) for p in layout], axis=1)
        some = slice(begin * 256, (begin + len(layout)) * 256)
        product = jnp.dot(x, w[some, :], preferred_element_type=F32)
        total = product if fresh else total + product
        if last:
            total = total + tokens[rows, :].astype(F32)
        out[rows, :] = total.astype(out.dtype)


def out_project(length, begin, pieces, w, state, tokens=None):
    layout, flat = number(pieces)
    rows = length
    last = tokens is not None
    ins = [w] + flat + ([] if state is None else [state]) + ([tokens] if last else [])

    def kernel(*refs):
        out_kernel(begin, layout, state is None, last, *refs)

    outs = jax.ShapeDtypeStruct((rows, 256), BF16 if last else F32)
    aliases = {1 + len(flat): 0} if (state is not None and not last) else {}
    return call(
        kernel, outs, ins, [VMEM] * len(ins), [], 12, len(pieces) * 2 * rows * 256 * 256, aliases
    )


def shifted(x, dy, dz, dc):
    pairs = []
    for i in range(16):
        y, z, c = i // 4, (i // 2) % 2, i % 2
        pairs.append((i, ((y + dy) % 4) * 4 + ((z + dz) % 2) * 2 + (c + dc) % 2))
    return lax.ppermute(x, "tp", pairs)


def tie(value, *others):
    return lax.optimization_barrier((value,) + others)[0]


def body(tokens, norm_gain, w_in, w_short, decay_rate, residue, w_out):
    length, chans = tokens.shape
    half = length // 2
    chunk = length // SUBS

    def other(p, *after):
        return shifted(tie(p, *after) if after else p, 0, 0, 1)

    def gather(x, start, add):
        up = shifted(x, 0, 1, 0)
        far = shifted(x, 2, 0, 0)
        x_other = other(x)
        if start is not None:
            x_other = tie(x_other, start)
        state, mark = add(0, [x, x_other], None)
        up, far, mark = lax.optimization_barrier((up, far, mark))
        both = jnp.concatenate([x, up], axis=0)
        left = shifted(both, 1, 0, 0)
        right = shifted(both, -1, 0, 0)
        up_far = shifted(far, 0, 1, 0)
        up_other, far_other = other(up), other(far)
        state, mark = add(2, [up, up_other, far, far_other], state)
        up_far, left, right, mark = lax.optimization_barrier((up_far, left, right, mark))
        up_far_other, left_other, right_other = other(up_far), other(left), other(right)
        state, mark = add(6, [up_far, left, (left, length), right, (right, length)], state)
        state, mark = add(11, [up_far_other, left_other, (left_other, length)], state)
        return [right_other, (right_other, length)], state

    width = chans

    def prepare():
        def kernel(*refs):
            order_kernel(chunk, *refs)

        return pl.pallas_call(
            kernel,
            out_shape=[
                jax.ShapeDtypeStruct((3, 16 * width, width), BF16),
                jax.ShapeDtypeStruct((16 * width, width), BF16),
                jax.ShapeDtypeStruct((16, width), F32),
                jax.ShapeDtypeStruct((TABLE_ROWS, width), F32),
            ],
            in_specs=[HBM, HBM] + [VMEM] * 4,
            out_specs=[VMEM] * 4,
            scratch_shapes=[pltpu.SemaphoreType.DMA((2, 16))],
            compiler_params=pltpu.CompilerParams(vmem_limit_bytes=4 * MIB),
            cost_estimate=pl.CostEstimate(flops=1, bytes_accessed=1, transcendentals=0),
        )(
            w_in.transpose(1, 0, 2),
            w_out,
            norm_gain.reshape(16, width),
            decay_rate.T,
            residue.T,
            w_short.reshape(SPAN * 3, width),
        )

    first, second, gain, table = prepare()

    def add_in(begin, pieces, state):
        state = project(length, begin, pieces, gain, first, state)
        return state, state[0]

    pieces, state = gather(tokens, table, add_in)
    layout, flat = number(pieces)
    ins = [gain, first] + flat + list(state) + [table]

    def kernel(*refs):
        local_kernel(14, layout, chunk, *refs)

    gate, local, before, load = call(
        kernel,
        [
            jax.ShapeDtypeStruct((length, chans), F32),
            jax.ShapeDtypeStruct((length, chans), F32),
            jax.ShapeDtypeStruct((MODES * SUBS, chans), F32),
            jax.ShapeDtypeStruct((8, 80, chans), BF16),
        ],
        ins,
        [VMEM] * len(ins),
        [
            pltpu.VMEM((3 * chans // LANES, length + 8, LANES), F32),
            pltpu.VMEM((MODES, chans), F32),
        ],
        20,
        4 * 10**9,
    )
    loads = lax.all_to_all(load, "ctx", 0, 0, tiled=True)
    ins = [loads, gate, local, before, table]

    def kernel_two(*refs):
        join_kernel(chunk, *refs)

    mixed = call(
        kernel_two,
        jax.ShapeDtypeStruct((length, chans), BF16),
        ins,
        [VMEM] * len(ins),
        [
            pltpu.VMEM((chans // LANES, 9 * 64, LANES), F32),
            pltpu.VMEM((chans // LANES, length, LANES), F32),
            pltpu.VMEM((MODES * SUBS, chans), F32),
        ],
        12,
        2 * 10**9,
    )

    def add_out(begin, pieces, state):
        state = out_project(length, begin, pieces, second, state)
        return state, state

    pieces, state = gather(mixed, None, add_out)
    return out_project(length, 14, pieces, second, state, tokens)


def solution(mesh):
    placed = (
        P("ctx", "tp"),
        P(),
        P(None, None, "tp"),
        P(None, None, "tp"),
        P("tp", None),
        P("tp", None),
        P(None, "tp"),
    )
    return jax.shard_map(
        body, mesh=mesh, in_specs=placed, out_specs=P("ctx", "tp"), check_vma=False
    )
```

time: 149 us -> 127 us (0.85)
  starting transfers between devices: 64.7 us -> 26.7 us
  waiting for transfers between devices: 28.4 us -> 54.3 us
  blocking collectives: 0 us -> 12.2 us
  other arithmetic: 10.3 us -> 0.07 us
  Pallas kernels: 32.7 us -> 25.3 us
  local copies, waits for them, and re-layouts: 10.3 us -> 7.37 us
    ppermute x38 -> x22, waiting for transfers between devices: 26.6 us -> 54.3 us  [shifted(): return lax.ppermute(x, 'tp', pairs)]
    ppermute x38 -> x22, starting transfers between devices: 48 us -> 26.7 us  [shifted(): return lax.ppermute(x, 'tp', pairs)]
    ppermute x7 -> x0, starting transfers between devices: 16.7 us -> none  [body(): loads.append(lax.ppermute(load, 'ctx', [(i, i + d) for i in range(8 - d)]))]
    all_to_all x0 -> x1, blocking collectives: none -> 12.2 us  [body(): loads = lax.all_to_all(load, 'ctx', 0, 0, tiled=True)]
    pallas_call x13 -> x11, Pallas kernels: 28.1 us -> 20.5 us  [call(): pl.pallas_call(kernel, out_shape=outs, in_specs=specs, out_specs=[VMEM] *...]
    unnamed x9 -> x0, other arithmetic: 6.53 us -> none
    ppermute x7 -> x0, waiting for transfers between devices: 1.81 us -> none  [body(): loads.append(lax.ppermute(load, 'ctx', [(i, i + d) for i in range(8 - d)]))]
    exp x2 -> x0, other arithmetic: 1.63 us -> none  [powers(): return jnp.exp(-rate[:, None, :] * counts[None, :, None])]
  transfers between devices with their start and end apart: 45 -> 22, of which waited for: 8 -> 11; matrix products, arithmetic and copies ran while one was open for 10% -> 1% of each run, Pallas kernels for 14% -> 12%
where the time goes in v2:
time: 127 us; the launch traced here: 126 us
  waiting for transfers between devices  54.3 us (43%)
  starting transfers between devices  26.7 us (21%)
  Pallas kernels  25.3 us (20%)
  blocking collectives  12.2 us (10%)
  local copies, waits for them, and re-layouts  7.37 us (6%)
    ppermute x22, waiting for transfers between devices, shifted(): return lax.ppermute(x, 'tp', pairs)  54.3 us
    ppermute x22, starting transfers between devices, shifted(): return lax.ppermute(x, 'tp', pairs)  26.7 us
    pallas_call x11, Pallas kernels, call(): pl.pallas_call(kernel, out_shape=outs, in_specs=specs, out_specs=[VMEM] *...  20.5 us
    all_to_all x1, blocking collectives, body(): loads = lax.all_to_all(load, 'ctx', 0, 0, tiled=True)  12.2 us
    unnamed x12, local copies, waits for them, and re-layouts  6.6 us
    pallas_call x1, Pallas kernels, prepare(): pl.pallas_call(kernel, out_shape=[jax.ShapeDtypeStruct((3, 16 * width, wi...  4.8 us
  transfers between devices with their start and end apart: 22, of which 11 were waited for; matrix products, arithmetic and copies ran while one was open for 1% of the time, Pallas kernels for 12%

profile of v2, /device:TPU:1, one launch (start us, length us, event | category | flops | bytes accessed | tf_op | source)
XLA Modules:
  0.0 126.1 jit_solution(12132647581216456951)
XLA Ops:
  0.0 1.4 %collective-permute-start.2 = (bf16[1024,256]{1,0:T(8,128)(2,1)}, bf16[1024,256]{1,0:T(8,128)(2,1)S(1)}, u32[]{:S(2)}, u32[]{:S(2)}) collective-permute-start(bf16[1024,256]{1,0:T(8,128)(2,1)} %refs_3_.1), channel_id=1, source_target_pairs={{0,1},{1,0},{2,3},{3,2},{4,5},{5,4},{6,7},{7,6},{8,9},{9,8},{10,11... | collective-permute-start | bytes 1572872 | tf_op jit(solution)/shard_map/ppermute | solution.py:399
  1.4 3.7 %collective-permute-start = (bf16[1024,256]{1,0:T(8,128)(2,1)}, bf16[1024,256]{1,0:T(8,128)(2,1)S(1)}, u32[]{:S(2)}, u32[]{:S(2)}) collective-permute-start(bf16[1024,256]{1,0:T(8,128)(2,1)} %refs_3_.1), channel_id=1, source_target_pairs={{0,2},{1,3},{2,0},{3,1},{4,6},{5,7},{6,4},{7,5},{8,10},{9,11},{10,... | collective-permute-start | bytes 1572872 | tf_op jit(solution)/shard_map/ppermute | solution.py:399
  5.1 2.9 %collective-permute-start.1 = (bf16[1024,256]{1,0:T(8,128)(2,1)}, bf16[1024,256]{1,0:T(8,128)(2,1)S(1)}, u32[]{:S(2)}, u32[]{:S(2)}) collective-permute-start(bf16[1024,256]{1,0:T(8,128)(2,1)} %refs_3_.1), channel_id=1, source_target_pairs={{0,8},{1,9},{2,10},{3,11},{4,12},{5,13},{6,14},{7,15},{8,0},{9,1},... | collective-permute-start | bytes 1572872 | tf_op jit(solution)/shard_map/ppermute | solution.py:399
  8.0 0.7 copy.18
  8.8 0.7 reshape.6.refs_2_
  9.5 2.8 %copy-done = bf16[4096,3,256]{2,0,1:T(8,128)(2,1)S(1)} copy-done((bf16[4096,3,256]{2,0,1:T(8,128)(2,1)S(1)}, bf16[4096,3,256]{2,0,1:T(8,128)(2,1)}, u32[]{:S(2)}) %copy-start) | copy-done | bytes 6291480
  12.3 1.6 %copy-done.2 = bf16[4096,256]{1,0:T(8,128)(2,1)S(1)} copy-done((bf16[4096,256]{1,0:T(8,128)(2,1)S(1)}, bf16[4096,256]{1,0:T(8,128)(2,1)}, u32[]{:S(2)}) %copy-start.2) | copy-done | bytes 2097176
  13.9 0.7 copy-done.3
  14.6 0.7 copy-done.4
  15.3 4.8 %shard_map.73 = (bf16[3,4096,256]{2,1,0:T(8,128)(2,1)S(1)}, bf16[4096,256]{1,0:T(8,128)(2,1)S(1)}, f32[16,256]{1,0:T(8,128)S(1)}, f32[1048,256]{1,0:T(8,128)S(1)}) custom-call(bf16[3,4096,256]{2,1,0:T(8,128)(2,1)S(1)} %bitcast.3, bf16[4096,256]{1,0:T(8,128)(2,1)S(1)} %copy-done.2, f32[16,256]{1,0:T(8,128)S(1)} %reshape.6.refs_2_, f32[16,256]{1,0:T(8,128)S(1)} %bitcast.4, ...), custom_call_target="tpu_custom_call" | custom-call | flops 1 | bytes 1 | tf_op jit(solution)/shard_map/pallas_call | solution.py:440
  20.2 1.0 shard_map.74
  21.3 0.5 collective-permute-start.4
  21.8 2.3 %collective-permute-start.5 = (bf16[2048,256]{1,0:T(8,128)(2,1)S(1)}, bf16[2048,256]{1,0:T(8,128)(2,1)S(1)}, u32[]{:S(2)}, u32[]{:S(2)}) collective-permute-start(bf16[2048,256]{1,0:T(8,128)(2,1)S(1)} %constant_dynamic-update-slice_fusion), channel_id=1, source_target_pairs={{0,12},{1,13},{2,14},{3,15},{4,0},{5,1},{6,2},{7,3},{8,4},{9,5},{1... | collective-permute-start | bytes 3145736 | tf_op jit(solution)/shard_map/ppermute | solution.py:399
  24.0 1.1 collective-permute-start.6
  25.2 1.5 %collective-permute-done.6.refs_3_ = bf16[1024,256]{1,0:T(8,128)(2,1)S(1)} collective-permute-done((bf16[1024,256]{1,0:T(8,128)(2,1)S(1)}, bf16[1024,256]{1,0:T(8,128)(2,1)S(1)}, u32[]{:S(2)}, u32[]{:S(2)}) %collective-permute-start.6) | collective-permute-done | bytes 524320 | tf_op jit(solution)/shard_map/ppermute | solution.py:399
  26.7 0.7 collective-permute-done.7.refs_5_
  27.4 2.1 %shard_map.75 = (f32[1024,768]{1,0:T(8,128)S(1)}, f32[1024,128]{1,0:T(8,128)S(1)}) custom-call(f32[16,256]{1,0:T(8,128)S(1)} %get-tuple-element.33.refs_0_, bf16[3,4096,256]{2,1,0:T(8,128)(2,1)S(1)} %get-tuple-element.34.refs_1_, bf16[1024,256]{1,0:T(8,128)(2,1)S(1)} %collective-permute-done.refs_2_, ...), custom_call_target="tpu_custom_call", output_to_operand_aliasing={{0}: (6, {}), {1}: (7, {})} | custom-call | flops 1 | bytes 1 | tf_op jit(solution)/shard_map/pallas_call | solution.py:24
  29.5 10.1 %collective-permute-done.3.refs_2_ = bf16[1024,256]{1,0:T(8,128)(2,1)S(1)} collective-permute-done((bf16[1024,256]{1,0:T(8,128)(2,1)S(1)}, bf16[1024,256]{1,0:T(8,128)(2,1)S(1)}, u32[]{:S(2)}, u32[]{:S(2)}) %collective-permute-start.3) | collective-permute-done | bytes 524320 | tf_op jit(solution)/shard_map/ppermute | solution.py:399
  39.6 7.1 %collective-permute-done.4.refs_3_ = bf16[2048,256]{1,0:T(8,128)(2,1)S(1)} collective-permute-done((bf16[2048,256]{1,0:T(8,128)(2,1)S(1)}, bf16[2048,256]{1,0:T(8,128)(2,1)S(1)}, u32[]{:S(2)}, u32[]{:S(2)}) %collective-permute-start.4) | collective-permute-done | bytes 1048608 | tf_op jit(solution)/shard_map/ppermute | solution.py:399
  46.7 1.4 %collective-permute-start.10 = (bf16[2048,256]{1,0:T(8,128)(2,1)S(1)}, bf16[2048,256]{1,0:T(8,128)(2,1)S(1)}, u32[]{:S(2)}, u32[]{:S(2)}) collective-permute-start(bf16[2048,256]{1,0:T(8,128)(2,1)S(1)} %collective-permute-done.4.refs_3_), channel_id=1, source_target_pairs={{0,1},{1,0},{2,3},{3,2},{4,5},{5,4},{6,7},{7,6},{8,9},{9,8},{10,11... | collective-permute-start | bytes 3145736 | tf_op jit(solution)/shard_map/ppermute | solution.py:399
  48.2 0.5 collective-permute-start.9
  48.7 2.5 %shard_map.76 = (f32[1024,768]{1,0:T(8,128)S(1)}, f32[1024,128]{1,0:T(8,128)S(1)}) custom-call(f32[16,256]{1,0:T(8,128)S(1)} %get-tuple-element.33.refs_0_, bf16[3,4096,256]{2,1,0:T(8,128)(2,1)S(1)} %get-tuple-element.34.refs_1_, bf16[1024,256]{1,0:T(8,128)(2,1)S(1)} %collective-permute-done.3.refs_2_, ...), custom_call_target="tpu_custom_call", output_to_operand_aliasing={{0}: (5, {}), {1}: (6, {})} | custom-call | flops 1 | bytes 1 | tf_op jit(solution)/shard_map/pallas_call | solution.py:24
  51.1 1.5 %collective-permute-done.9.refs_2_ = bf16[1024,256]{1,0:T(8,128)(2,1)S(1)} collective-permute-done((bf16[1024,256]{1,0:T(8,128)(2,1)S(1)}, bf16[1024,256]{1,0:T(8,128)(2,1)S(1)}, u32[]{:S(2)}, u32[]{:S(2)}) %collective-permute-start.9) | collective-permute-done | bytes 524320 | tf_op jit(solution)/shard_map/ppermute | solution.py:399
  52.7 1.6 %shard_map.77 = (f32[1024,768]{1,0:T(8,128)S(1)}, f32[1024,128]{1,0:T(8,128)S(1)}) custom-call(f32[16,256]{1,0:T(8,128)S(1)} %get-tuple-element.33.refs_0_, bf16[3,4096,256]{2,1,0:T(8,128)(2,1)S(1)} %get-tuple-element.34.refs_1_, bf16[1024,256]{1,0:T(8,128)(2,1)S(1)} %collective-permute-done.9.refs_2_, ...), custom_call_target="tpu_custom_call", output_to_operand_aliasing={{0}: (4, {}), {1}: (5, {})} | custom-call | flops 1 | bytes 1 | tf_op jit(solution)/shard_map/pallas_call | solution.py:24
  54.3 7.4 %shard_map.78 = (f32[1024,256]{1,0:T(8,128)S(1)}, f32[1024,256]{1,0:T(8,128)S(1)}, f32[128,256]{1,0:T(8,128)S(1)}, bf16[8,80,256]{2,1,0:T(8,128)(2,1)S(1)}) custom-call(f32[16,256]{1,0:T(8,128)S(1)} %get-tuple-element.33.refs_0_, bf16[3,4096,256]{2,1,0:T(8,128)(2,1)S(1)} %get-tuple-element.34.refs_1_, bf16[2048,256]{1,0:T(8,128)(2,1)S(1)} %collective-permute-done.8.refs_2_, ...), custom_call_target="tpu_custom_call" | custom-call | flops 1 | bytes 1 | tf_op jit(solution)/shard_map/pallas_call | solution.py:24
  61.8 12.2 %all_to_all.5.refs_0_ = bf16[8,80,256]{2,1,0:T(8,128)(2,1)S(1)} all-to-all(bf16[8,80,256]{2,1,0:T(8,128)(2,1)S(1)} %get-tuple-element.50), channel_id=1, replica_groups=mesh['ctx'=8,'tp'=16] {'ctx'}, dimensions={0} | all-to-all | bytes 655360 | tf_op jit(solution)/shard_map/all_to_all | solution.py:492
  74.0 2.1 %shard_map.79.refs_1_ = bf16[1024,256]{1,0:T(8,128)(2,1)S(1)} custom-call(bf16[8,80,256]{2,1,0:T(8,128)(2,1)S(1)} %all_to_all.5.refs_0_, f32[1024,256]{1,0:T(8,128)S(1)} %get-tuple-element.51.refs_1_, f32[1024,256]{1,0:T(8,128)S(1)} %get-tuple-element.52.refs_2_, f32[128,256]{1,0:T(8,128)S(1)} %get-tuple-element.53.refs_3_, ...), custom_call_target="tpu_custom_call" | custom-call | flops 1 | bytes 1 | tf_op jit(solution)/shard_map/pallas_call | solution.py:24
  76.1 1.2 collective-permute-start.13
  77.3 0.9 collective-permute-start.11
  78.2 1.6 %collective-permute-start.12 = (bf16[1024,256]{1,0:T(8,128)(2,1)S(1)}, bf16[1024,256]{1,0:T(8,128)(2,1)S(1)}, u32[]{:S(2)}, u32[]{:S(2)}) collective-permute-start(bf16[1024,256]{1,0:T(8,128)(2,1)S(1)} %shard_map.79.refs_1_), channel_id=1, source_target_pairs={{0,8},{1,9},{2,10},{3,11},{4,12},{5,13},{6,14},{7,15},{8,0},{9,1},... | collective-permute-start | bytes 1572872 | tf_op jit(solution)/shard_map/ppermute | solution.py:399
  79.7 0.4 shard_map.80.refs_5_
  80.2 12.1 %collective-permute-done.11.refs_1_ = bf16[1024,256]{1,0:T(8,128)(2,1)S(1)} collective-permute-done((bf16[1024,256]{1,0:T(8,128)(2,1)S(1)}, bf16[1024,256]{1,0:T(8,128)(2,1)S(1)}, u32[]{:S(2)}, u32[]{:S(2)}) %collective-permute-start.11) | collective-permute-done | bytes 524320 | tf_op jit(solution)/shard_map/ppermute | solution.py:399
  92.3 0.6 collective-permute-done.12.refs_3_
  92.8 0.1 pad_maximum_fusion
  92.9 0.4 collective-permute-start.15
  93.3 2.4 %collective-permute-start.16 = (bf16[2048,256]{1,0:T(8,128)(2,1)S(1)}, bf16[2048,256]{1,0:T(8,128)(2,1)S(1)}, u32[]{:S(2)}, u32[]{:S(2)}) collective-permute-start(bf16[2048,256]{1,0:T(8,128)(2,1)S(1)} %pad_maximum_fusion), channel_id=1, source_target_pairs={{0,12},{1,13},{2,14},{3,15},{4,0},{5,1},{6,2},{7,3},{8,4},{9,5},{1... | collective-permute-start | bytes 3145736 | tf_op jit(solution)/shard_map/ppermute | solution.py:399
  95.7 1.7 %collective-permute-start.17 = (bf16[1024,256]{1,0:T(8,128)(2,1)S(1)}, bf16[1024,256]{1,0:T(8,128)(2,1)S(1)}, u32[]{:S(2)}, u32[]{:S(2)}) collective-permute-start(bf16[1024,256]{1,0:T(8,128)(2,1)S(1)} %collective-permute-done.11.refs_1_), channel_id=1, source_target_pairs={{0,1},{1,0},{2,3},{3,2},{4,5},{5,4},{6,7},{7,6},{8,9},{9,8},{10,11... | collective-permute-start | bytes 1572872 | tf_op jit(solution)/shard_map/ppermute | solution.py:399
  97.4 2.1 %collective-permute-start.14 = (bf16[1024,256]{1,0:T(8,128)(2,1)S(1)}, bf16[1024,256]{1,0:T(8,128)(2,1)S(1)}, u32[]{:S(2)}, u32[]{:S(2)}) collective-permute-start(bf16[1024,256]{1,0:T(8,128)(2,1)S(1)} %collective-permute-done.12.refs_3_), channel_id=1, source_target_pairs={{0,2},{1,3},{2,0},{3,1},{4,6},{5,7},{6,4},{7,5},{8,10},{9,11},{10,... | collective-permute-start | bytes 1572872 | tf_op jit(solution)/shard_map/ppermute | solution.py:399
  99.5 0.2 collective-permute-done.18.refs_4_
  99.7 0.7 shard_map.81.refs_4_
  100.4 11.5 %collective-permute-done.14.refs_1_ = bf16[1024,256]{1,0:T(8,128)(2,1)S(1)} collective-permute-done((bf16[1024,256]{1,0:T(8,128)(2,1)S(1)}, bf16[1024,256]{1,0:T(8,128)(2,1)S(1)}, u32[]{:S(2)}, u32[]{:S(2)}) %collective-permute-start.14) | collective-permute-done | bytes 524320 | tf_op jit(solution)/shard_map/ppermute | solution.py:399
  111.9 5.8 %collective-permute-done.15.refs_2_ = bf16[2048,256]{1,0:T(8,128)(2,1)S(1)} collective-permute-done((bf16[2048,256]{1,0:T(8,128)(2,1)S(1)}, bf16[2048,256]{1,0:T(8,128)(2,1)S(1)}, u32[]{:S(2)}, u32[]{:S(2)}) %collective-permute-start.15) | collective-permute-done | bytes 1048608 | tf_op jit(solution)/shard_map/ppermute | solution.py:399
  117.6 2.1 %collective-permute-start.21 = (bf16[2048,256]{1,0:T(8,128)(2,1)S(1)}, bf16[2048,256]{1,0:T(8,128)(2,1)S(1)}, u32[]{:S(2)}, u32[]{:S(2)}) collective-permute-start(bf16[2048,256]{1,0:T(8,128)(2,1)S(1)} %collective-permute-done.15.refs_2_), channel_id=1, source_target_pairs={{0,1},{1,0},{2,3},{3,2},{4,5},{5,4},{6,7},{7,6},{8,9},{9,8},{10,11... | collective-permute-start | bytes 3145736 | tf_op jit(solution)/shard_map/ppermute | solution.py:399
  119.8 0.5 collective-permute-start.20
  120.3 0.9 shard_map.82.refs_3_
  121.1 3.2 %collective-permute-done.20.refs_1_ = bf16[1024,256]{1,0:T(8,128)(2,1)S(1)} collective-permute-done((bf16[1024,256]{1,0:T(8,128)(2,1)S(1)}, bf16[1024,256]{1,0:T(8,128)(2,1)S(1)}, u32[]{:S(2)}, u32[]{:S(2)}) %collective-permute-start.20) | collective-permute-done | bytes 524320 | tf_op jit(solution)/shard_map/ppermute | solution.py:399
  124.3 0.6 shard_map.83.refs_2_
  124.9 1.2 shard_map.84
  (25 shorter events, 0.1 us)
Async XLA Ops:
  0.0 20.2 %collective-permute-start.2 = (bf16[1024,256]{1,0:T(8,128)(2,1)}, bf16[1024,256]{1,0:T(8,128)(2,1)S(1)}, u32[]{:S(2)}, u32[]{:S(2)}) collective-permute-start(bf16[1024,256]{1,0:T(8,128)(2,1)} %refs_3_.1), channel_id=1, source_target_pairs={{0,1},{1,0},{2,3},{3,2},{4,5},{5,4},{6,7},{7,6},{8,9},{9,8},{10,11... | collective-permute-start | bytes 1572872 | tf_op jit(solution)/shard_map/ppermute | solution.py:399
  1.4 19.8 %collective-permute-start = (bf16[1024,256]{1,0:T(8,128)(2,1)}, bf16[1024,256]{1,0:T(8,128)(2,1)S(1)}, u32[]{:S(2)}, u32[]{:S(2)}) collective-permute-start(bf16[1024,256]{1,0:T(8,128)(2,1)} %refs_3_.1), channel_id=1, source_target_pairs={{0,2},{1,3},{2,0},{3,1},{4,6},{5,7},{6,4},{7,5},{8,10},{9,11},{10,... | collective-permute-start | bytes 1572872 | tf_op jit(solution)/shard_map/ppermute | solution.py:399
  5.1 16.1 %collective-permute-start.1 = (bf16[1024,256]{1,0:T(8,128)(2,1)}, bf16[1024,256]{1,0:T(8,128)(2,1)S(1)}, u32[]{:S(2)}, u32[]{:S(2)}) collective-permute-start(bf16[1024,256]{1,0:T(8,128)(2,1)} %refs_3_.1), channel_id=1, source_target_pairs={{0,8},{1,9},{2,10},{3,11},{4,12},{5,13},{6,14},{7,15},{8,0},{9,1},... | collective-permute-start | bytes 1572872 | tf_op jit(solution)/shard_map/ppermute | solution.py:399
  9.5 2.8 %copy-start = (bf16[4096,3,256]{2,0,1:T(8,128)(2,1)S(1)}, bf16[4096,3,256]{2,0,1:T(8,128)(2,1)}, u32[]{:S(2)}) copy-start(bf16[4096,3,256]{2,0,1:T(8,128)(2,1)} %param.9) | copy-start | bytes 18874372
  12.3 1.6 %copy-start.2 = (bf16[4096,256]{1,0:T(8,128)(2,1)S(1)}, bf16[4096,256]{1,0:T(8,128)(2,1)}, u32[]{:S(2)}) copy-start(bf16[4096,256]{1,0:T(8,128)(2,1)} %refs_1_.1) | copy-start | bytes 6291460
  13.9 0.7 copy-start.3
  14.6 0.7 copy-start.4
  15.3 4.8 %copy-start.1 = (bf16[1024,256]{1,0:T(8,128)(2,1)S(1)}, bf16[1024,256]{1,0:T(8,128)(2,1)}, u32[]{:S(2)}) copy-start(bf16[1024,256]{1,0:T(8,128)(2,1)} %refs_3_.1) | copy-start | bytes 1572868
  21.3 25.4 %collective-permute-start.4 = (bf16[2048,256]{1,0:T(8,128)(2,1)S(1)}, bf16[2048,256]{1,0:T(8,128)(2,1)S(1)}, u32[]{:S(2)}, u32[]{:S(2)}) collective-permute-start(bf16[2048,256]{1,0:T(8,128)(2,1)S(1)} %constant_dynamic-update-slice_fusion), channel_id=1, source_target_pairs={{0,4},{1,5},{2,6},{3,7},{4,8},{5,9},{6,10},{7,11},{8,12},{9,13},{1... | collective-permute-start | bytes 3145736 | tf_op jit(solution)/shard_map/ppermute | solution.py:399
  21.8 25.0 %collective-permute-start.5 = (bf16[2048,256]{1,0:T(8,128)(2,1)S(1)}, bf16[2048,256]{1,0:T(8,128)(2,1)S(1)}, u32[]{:S(2)}, u32[]{:S(2)}) collective-permute-start(bf16[2048,256]{1,0:T(8,128)(2,1)S(1)} %constant_dynamic-update-slice_fusion), channel_id=1, source_target_pairs={{0,12},{1,13},{2,14},{3,15},{4,0},{5,1},{6,2},{7,3},{8,4},{9,5},{1... | collective-permute-start | bytes 3145736 | tf_op jit(solution)/shard_map/ppermute | solution.py:399
  24.0 2.7 %collective-permute-start.6 = (bf16[1024,256]{1,0:T(8,128)(2,1)S(1)}, bf16[1024,256]{1,0:T(8,128)(2,1)S(1)}, u32[]{:S(2)}, u32[]{:S(2)}) collective-permute-start(bf16[1024,256]{1,0:T(8,128)(2,1)S(1)} %collective-permute-done.refs_2_), channel_id=1, source_target_pairs={{0,1},{1,0},{2,3},{3,2},{4,5},{5,4},{6,7},{7,6},{8,9},{9,8},{10,11... | collective-permute-start | bytes 1572872 | tf_op jit(solution)/shard_map/ppermute | solution.py:399
  25.2 2.3 %collective-permute-start.7 = (bf16[1024,256]{1,0:T(8,128)(2,1)S(1)}, bf16[1024,256]{1,0:T(8,128)(2,1)S(1)}, u32[]{:S(2)}, u32[]{:S(2)}) collective-permute-start(bf16[1024,256]{1,0:T(8,128)(2,1)S(1)} %collective-permute-done.1.refs_4_), channel_id=1, source_target_pairs={{0,1},{1,0},{2,3},{3,2},{4,5},{5,4},{6,7},{7,6},{8,9},{9,8},{10,11... | collective-permute-start | bytes 1572872 | tf_op jit(solution)/shard_map/ppermute | solution.py:399
  25.2 14.5 %collective-permute-start.3 = (bf16[1024,256]{1,0:T(8,128)(2,1)S(1)}, bf16[1024,256]{1,0:T(8,128)(2,1)S(1)}, u32[]{:S(2)}, u32[]{:S(2)}) collective-permute-start(bf16[1024,256]{1,0:T(8,128)(2,1)S(1)} %collective-permute-done.1.refs_4_), channel_id=1, source_target_pairs={{0,2},{1,3},{2,0},{3,1},{4,6},{5,7},{6,4},{7,5},{8,10},{9,11},{10,... | collective-permute-start | bytes 1572872 | tf_op jit(solution)/shard_map/ppermute | solution.py:399
  46.7 6.0 %collective-permute-start.10 = (bf16[2048,256]{1,0:T(8,128)(2,1)S(1)}, bf16[2048,256]{1,0:T(8,128)(2,1)S(1)}, u32[]{:S(2)}, u32[]{:S(2)}) collective-permute-start(bf16[2048,256]{1,0:T(8,128)(2,1)S(1)} %collective-permute-done.4.refs_3_), channel_id=1, source_target_pairs={{0,1},{1,0},{2,3},{3,2},{4,5},{5,4},{6,7},{7,6},{8,9},{9,8},{10,11... | collective-permute-start | bytes 3145736 | tf_op jit(solution)/shard_map/ppermute | solution.py:399
  48.1 6.2 %collective-permute-start.8 = (bf16[2048,256]{1,0:T(8,128)(2,1)S(1)}, bf16[2048,256]{1,0:T(8,128)(2,1)S(1)}, u32[]{:S(2)}, u32[]{:S(2)}) collective-permute-start(bf16[2048,256]{1,0:T(8,128)(2,1)S(1)} %collective-permute-done.5.refs_4_), channel_id=1, source_target_pairs={{0,1},{1,0},{2,3},{3,2},{4,5},{5,4},{6,7},{7,6},{8,9},{9,8},{10,11... | collective-permute-start | bytes 3145736 | tf_op jit(solution)/shard_map/ppermute | solution.py:399
  48.2 4.5 %collective-permute-start.9 = (bf16[1024,256]{1,0:T(8,128)(2,1)S(1)}, bf16[1024,256]{1,0:T(8,128)(2,1)S(1)}, u32[]{:S(2)}, u32[]{:S(2)}) collective-permute-start(bf16[1024,256]{1,0:T(8,128)(2,1)S(1)} %collective-permute-done.3.refs_2_), channel_id=1, source_target_pairs={{0,1},{1,0},{2,3},{3,2},{4,5},{5,4},{6,7},{7,6},{8,9},{9,8},{10,11... | collective-permute-start | bytes 1572872 | tf_op jit(solution)/shard_map/ppermute | solution.py:399
  76.1 3.7 %collective-permute-start.13 = (bf16[1024,256]{1,0:T(8,128)(2,1)S(1)}, bf16[1024,256]{1,0:T(8,128)(2,1)S(1)}, u32[]{:S(2)}, u32[]{:S(2)}) collective-permute-start(bf16[1024,256]{1,0:T(8,128)(2,1)S(1)} %shard_map.79.refs_1_), channel_id=1, source_target_pairs={{0,1},{1,0},{2,3},{3,2},{4,5},{5,4},{6,7},{7,6},{8,9},{9,8},{10,11... | collective-permute-start | bytes 1572872 | tf_op jit(solution)/shard_map/ppermute | solution.py:399
  77.3 15.0 %collective-permute-start.11 = (bf16[1024,256]{1,0:T(8,128)(2,1)S(1)}, bf16[1024,256]{1,0:T(8,128)(2,1)S(1)}, u32[]{:S(2)}, u32[]{:S(2)}) collective-permute-start(bf16[1024,256]{1,0:T(8,128)(2,1)S(1)} %shard_map.79.refs_1_), channel_id=1, source_target_pairs={{0,2},{1,3},{2,0},{3,1},{4,6},{5,7},{6,4},{7,5},{8,10},{9,11},{10,... | collective-permute-start | bytes 1572872 | tf_op jit(solution)/shard_map/ppermute | solution.py:399
  78.2 14.7 %collective-permute-start.12 = (bf16[1024,256]{1,0:T(8,128)(2,1)S(1)}, bf16[1024,256]{1,0:T(8,128)(2,1)S(1)}, u32[]{:S(2)}, u32[]{:S(2)}) collective-permute-start(bf16[1024,256]{1,0:T(8,128)(2,1)S(1)} %shard_map.79.refs_1_), channel_id=1, source_target_pairs={{0,8},{1,9},{2,10},{3,11},{4,12},{5,13},{6,14},{7,15},{8,0},{9,1},... | collective-permute-start | bytes 1572872 | tf_op jit(solution)/shard_map/ppermute | solution.py:399
  92.9 24.7 %collective-permute-start.15 = (bf16[2048,256]{1,0:T(8,128)(2,1)S(1)}, bf16[2048,256]{1,0:T(8,128)(2,1)S(1)}, u32[]{:S(2)}, u32[]{:S(2)}) collective-permute-start(bf16[2048,256]{1,0:T(8,128)(2,1)S(1)} %pad_maximum_fusion), channel_id=1, source_target_pairs={{0,4},{1,5},{2,6},{3,7},{4,8},{5,9},{6,10},{7,11},{8,12},{9,13},{1... | collective-permute-start | bytes 3145736 | tf_op jit(solution)/shard_map/ppermute | solution.py:399
  93.3 24.3 %collective-permute-start.16 = (bf16[2048,256]{1,0:T(8,128)(2,1)S(1)}, bf16[2048,256]{1,0:T(8,128)(2,1)S(1)}, u32[]{:S(2)}, u32[]{:S(2)}) collective-permute-start(bf16[2048,256]{1,0:T(8,128)(2,1)S(1)} %pad_maximum_fusion), channel_id=1, source_target_pairs={{0,12},{1,13},{2,14},{3,15},{4,0},{5,1},{6,2},{7,3},{8,4},{9,5},{1... | collective-permute-start | bytes 3145736 | tf_op jit(solution)/shard_map/ppermute | solution.py:399
  95.7 3.8 %collective-permute-start.17 = (bf16[1024,256]{1,0:T(8,128)(2,1)S(1)}, bf16[1024,256]{1,0:T(8,128)(2,1)S(1)}, u32[]{:S(2)}, u32[]{:S(2)}) collective-permute-start(bf16[1024,256]{1,0:T(8,128)(2,1)S(1)} %collective-permute-done.11.refs_1_), channel_id=1, source_target_pairs={{0,1},{1,0},{2,3},{3,2},{4,5},{5,4},{6,7},{7,6},{8,9},{9,8},{10,11... | collective-permute-start | bytes 1572872 | tf_op jit(solution)/shard_map/ppermute | solution.py:399
  97.4 2.3 %collective-permute-start.18 = (bf16[1024,256]{1,0:T(8,128)(2,1)S(1)}, bf16[1024,256]{1,0:T(8,128)(2,1)S(1)}, u32[]{:S(2)}, u32[]{:S(2)}) collective-permute-start(bf16[1024,256]{1,0:T(8,128)(2,1)S(1)} %collective-permute-done.12.refs_3_), channel_id=1, source_target_pairs={{0,1},{1,0},{2,3},{3,2},{4,5},{5,4},{6,7},{7,6},{8,9},{9,8},{10,11... | collective-permute-start | bytes 1572872 | tf_op jit(solution)/shard_map/ppermute | solution.py:399
  97.4 14.5 %collective-permute-start.14 = (bf16[1024,256]{1,0:T(8,128)(2,1)S(1)}, bf16[1024,256]{1,0:T(8,128)(2,1)S(1)}, u32[]{:S(2)}, u32[]{:S(2)}) collective-permute-start(bf16[1024,256]{1,0:T(8,128)(2,1)S(1)} %collective-permute-done.12.refs_3_), channel_id=1, source_target_pairs={{0,2},{1,3},{2,0},{3,1},{4,6},{5,7},{6,4},{7,5},{8,10},{9,11},{10,... | collective-permute-start | bytes 1572872 | tf_op jit(solution)/shard_map/ppermute | solution.py:399
  117.6 6.7 %collective-permute-start.21 = (bf16[2048,256]{1,0:T(8,128)(2,1)S(1)}, bf16[2048,256]{1,0:T(8,128)(2,1)S(1)}, u32[]{:S(2)}, u32[]{:S(2)}) collective-permute-start(bf16[2048,256]{1,0:T(8,128)(2,1)S(1)} %collective-permute-done.15.refs_2_), channel_id=1, source_target_pairs={{0,1},{1,0},{2,3},{3,2},{4,5},{5,4},{6,7},{7,6},{8,9},{9,8},{10,11... | collective-permute-start | bytes 3145736 | tf_op jit(solution)/shard_map/ppermute | solution.py:399
  119.8 5.1 %collective-permute-start.19 = (bf16[2048,256]{1,0:T(8,128)(2,1)S(1)}, bf16[2048,256]{1,0:T(8,128)(2,1)S(1)}, u32[]{:S(2)}, u32[]{:S(2)}) collective-permute-start(bf16[2048,256]{1,0:T(8,128)(2,1)S(1)} %collective-permute-done.16.refs_3_), channel_id=1, source_target_pairs={{0,1},{1,0},{2,3},{3,2},{4,5},{5,4},{6,7},{7,6},{8,9},{9,8},{10,11... | collective-permute-start | bytes 3145736 | tf_op jit(solution)/shard_map/ppermute | solution.py:399
  119.8 4.5 %collective-permute-start.20 = (bf16[1024,256]{1,0:T(8,128)(2,1)S(1)}, bf16[1024,256]{1,0:T(8,128)(2,1)S(1)}, u32[]{:S(2)}, u32[]{:S(2)}) collective-permute-start(bf16[1024,256]{1,0:T(8,128)(2,1)S(1)} %collective-permute-done.14.refs_1_), channel_id=1, source_target_pairs={{0,1},{1,0},{2,3},{3,2},{4,5},{5,4},{6,7},{7,6},{8,9},{9,8},{10,11... | collective-permute-start | bytes 1572872 | tf_op jit(solution)/shard_map/ppermute | solution.py:399

commit v3 on v2

--- a/solution.py
+++ b/solution.py
@@ -19,8 +19,7 @@
 TILE = 512
 
 
-def call(kernel, outs, ins, specs, scratch, limit, flops, aliases=None):
-    moved = sum(a.size * a.dtype.itemsize for a in ins)
+def call(kernel, outs, ins, specs, scratch, limit, aliases=None):
     return pl.pallas_call(
         kernel,
         out_shape=outs,
@@ -47,33 +46,21 @@
 ):
     TABLE[_name] = (sum(rows for _, rows in TABLE.values()), _rows)
 TABLE_ROWS = sum(rows for _, rows in TABLE.values())
-PLACES = (
-    ((0, 0, 0), (0, 0, 1), (0, 1, 0), (0, 1, 1), (2, 0, 0), (2, 0, 1), (2, 1, 0), (-1, 0, 0))
-    + ((-1, 1, 0), (1, 0, 0), (1, 1, 0), (2, 1, 1), (-1, 0, 1), (-1, 1, 1), (1, 0, 1), (1, 1, 1))
-)
-
 
 def part(table, name):
     begin, rows = TABLE[name]
     return table.at[pl.ds(begin, rows)]
 
 
-def order_kernel(chunk, w_in, w_out, gain, rate, residue, short, first, second, scale, table, sems):
+def source(place):
     me = lax.axis_index("tp")
     y, z, c = me // 4, (me // 2) % 2, me % 2
-    width = second.shape[1]
-    copies = []
-    for i in range(16):
-        dy, dz, dc = PLACES[i]
-        source = ((y + dy + 4) % 4) * 4 + ((z + dz) % 2) * 2 + (c + dc) % 2
-        rows = pl.ds(pl.multiple_of(source * width, width), width)
-        place = pl.ds(i * width, width)
-        copies.append(pltpu.make_async_copy(w_in.at[:, rows, :], first.at[:, place, :], sems.at[0, i]))
-        copies.append(pltpu.make_async_copy(w_out.at[rows, :], second.at[place, :], sems.at[1, i]))
-        scale[i : i + 1, :] = gain[pl.ds(source, 1), :]
-    for copy in copies:
-        copy.start()
-
+    dy, dz, dc = place
+    return ((y + dy + 4) % 4) * 4 + ((z + dz) % 2) * 2 + (c + dc) % 2
+
+
+def table_kernel(chunk, rate, residue, short, table):
+    width = table.shape[1]
     length = SUBS * chunk
     sub = lax.broadcasted_iota(jnp.int32, (SUBS, width), 0)
     lag = sub.astype(F32)
@@ -100,32 +87,31 @@
         far = jnp.exp(-wide * (jnp.maximum(lag - 1.0, 0.0) * length))
         put("ahead", n * SUBS, jnp.where(sub >= 1, far, 0.0))
     for i in range(SPAN * 3):
-        put("taps", i * SUBS, jnp.broadcast_to(short[i : i + 1, :], (SUBS, width)))
-    for copy in copies:
-        copy.wait()
-
-
-def add_pieces(begin, layout, gain, w, refs, r, tile):
+        tap = short[i // 3, i % 3 : i % 3 + 1, :]
+        put("taps", i * SUBS, jnp.broadcast_to(tap, (SUBS, width)))
+
+
+def add_pieces(layout, gain, w, refs, r, tile):
     squares = None
     scaled = []
-    for number, piece in enumerate(layout):
-        x = piece_rows(refs, piece, r, tile).astype(F32)
-        scaled.append((x * gain[begin + number : begin + number + 1, :]).astype(BF16))
+    blocks = []
+    for number, first, place in layout:
+        block = source(place)
+        x = refs[number][pl.ds(first + r * tile, tile), :].astype(F32)
+        scaled.append((x * gain[pl.ds(block, 1), :]).astype(BF16))
         square = x * x
         square = square[:, :LANES] + square[:, LANES:]
         squares = square if squares is None else squares + square
+        blocks.append(pl.ds(pl.multiple_of(block * 256, 256), 256))
     scaled = jnp.concatenate(scaled, axis=1)
-    rows = slice(begin * 256, (begin + len(layout)) * 256)
-    total = [jnp.dot(scaled, w[s, rows, :], preferred_element_type=F32) for s in range(3)]
+    total = []
+    for s in range(3):
+        weights = jnp.concatenate([w[s, rows, :] for rows in blocks], axis=0)
+        total.append(jnp.dot(scaled, weights, preferred_element_type=F32))
     return total, squares
 
 
-def piece_rows(refs, piece, r, tile):
-    number, first = piece
-    return refs[number][pl.ds(first + r * tile, tile), :]
-
-
-def proj_kernel(begin, layout, fresh, gain, w, *refs):
+def proj_kernel(layout, fresh, gain, w, *refs):
     count = 1 + max(p[0] for p in layout)
     pieces = refs[:count]
     if fresh:
@@ -135,7 +121,7 @@
     tile = TILE
     for r in range(acc.shape[0] // tile):
         rows = pl.ds(r * tile, tile)
-        total, squares = add_pieces(begin, layout, gain, w, pieces, r, tile)
+        total, squares = add_pieces(layout, gain, w, pieces, r, tile)
         for s in range(3):
             cols = slice(s * 256, (s + 1) * 256)
             acc[rows, cols] = total[s] if fresh else acc_in[rows, cols] + total[s]
@@ -144,16 +130,15 @@
 
 def number(pieces):
     layout, flat = [], []
-    for piece in pieces:
-        array, first = piece if isinstance(piece, tuple) else (piece, 0)
+    for array, first, place in pieces:
         known = [i for i, a in enumerate(flat) if a is array]
         if not known:
             flat.append(array)
-        layout.append((known[0] if known else len(flat) - 1, first))
+        layout.append((known[0] if known else len(flat) - 1, first, place))
     return layout, flat
 
 
-def project(length, begin, pieces, gain, w, state):
+def project(length, pieces, gain, w, state):
     layout, flat = number(pieces)
     rows = length
     outs = [jax.ShapeDtypeStruct((rows, 768), F32), jax.ShapeDtypeStruct((rows, LANES), F32)]
@@ -162,13 +147,13 @@
     fresh = state is None
 
     def kernel(*refs):
-        proj_kernel(begin, layout, fresh, *refs)
+        proj_kernel(layout, fresh, *refs)
 
     aliases = {} if fresh else {len(ins) - 2: 0, len(ins) - 1: 1}
-    return call(kernel, outs, ins, specs, [], 16, len(pieces) * 2 * rows * 256 * 768, aliases)
-
-
-def local_kernel(begin, layout, chunk, gain, w, *refs):
+    return call(kernel, outs, ins, specs, [], 16, aliases)
+
+
+def local_kernel(layout, chunk, gain, w, *refs):
     count = 1 + max(p[0] for p in layout)
     pieces = refs[:count]
     acc, ss, table, gate, local, before, load, proj, last = refs[count:]
@@ -180,7 +165,7 @@
     proj[:, 0:8, :] = jnp.zeros((3 * halves, 8, LANES), F32)
     for r in range(rows_all // tile):
         rows = pl.ds(r * tile, tile)
-        total, squares = add_pieces(begin, layout, gain, w, pieces, r, tile)
+        total, squares = add_pieces(layout, gain, w, pieces, r, tile)
         mean = jnp.sum(ss[rows, :] + squares, axis=1, keepdims=True) / (16 * width)
         scale = lax.rsqrt(mean + 1e-05)
         for s in range(3):
@@ -355,7 +340,7 @@
         mixed[:, g * LANES : (g + 1) * LANES] = whole[g].astype(BF16)
 
 
-def out_kernel(begin, layout, fresh, last, w, *refs):
+def out_kernel(layout, fresh, last, w, *refs):
     count = 1 + max(p[0] for p in layout)
     pieces = refs[:count]
     rest = list(refs[count:])
@@ -366,28 +351,34 @@
     for r in range(out.shape[0] // tile):
         rows = pl.ds(r * tile, tile)
         total = None if fresh else acc_in[rows, :]
-        x = jnp.concatenate([piece_rows(pieces, p, r, tile) for p in layout], axis=1)
-        some = slice(begin * 256, (begin + len(layout)) * 256)
-        product = jnp.dot(x, w[some, :], preferred_element_type=F32)
+        parts, weights = [], []
+        for number, first, place in layout:
+            parts.append(pieces[number][pl.ds(first + r * tile, tile), :])
+            weights.append(w[pl.ds(pl.multiple_of(source(place) * 256, 256), 256), :])
+        product = jnp.dot(
+            jnp.concatenate(parts, axis=1),
+            jnp.concatenate(weights, axis=0),
+            preferred_element_type=F32,
+        )
         total = product if fresh else total + product
         if last:
             total = total + tokens[rows, :].astype(F32)
         out[rows, :] = total.astype(out.dtype)
 
 
-def out_project(length, begin, pieces, w, state, tokens=None):
+def out_project(length, pieces, w, state, tokens=None):
     layout, flat = number(pieces)
     rows = length
     last = tokens is not None
     ins = [w] + flat + ([] if state is None else [state]) + ([tokens] if last else [])
 
     def kernel(*refs):
-        out_kernel(begin, layout, state is None, last, *refs)
+        out_kernel(layout, state is None, last, *refs)
 
     outs = jax.ShapeDtypeStruct((rows, 256), BF16 if last else F32)
     aliases = {1 + len(flat): 0} if (state is not None and not last) else {}
     return call(
-        kernel, outs, ins, [VMEM] * len(ins), [], 12, len(pieces) * 2 * rows * 256 * 256, aliases
+        kernel, outs, ins, [VMEM] * len(ins), [], 12, aliases
     )
 
 
@@ -414,55 +405,46 @@
     def gather(x, start, add):
         up = shifted(x, 0, 1, 0)
         far = shifted(x, 2, 0, 0)
+        left = shifted(x, 1, 0, 0)
+        right = shifted(x, -1, 0, 0)
         x_other = other(x)
         if start is not None:
             x_other = tie(x_other, start)
-        state, mark = add(0, [x, x_other], None)
+        state, mark = add([(x, 0, (0, 0, 0)), (x_other, 0, (0, 0, 1))], None)
         up, far, mark = lax.optimization_barrier((up, far, mark))
-        both = jnp.concatenate([x, up], axis=0)
-        left = shifted(both, 1, 0, 0)
-        right = shifted(both, -1, 0, 0)
+        up_left = shifted(up, 1, 0, 0)
+        up_right = shifted(up, -1, 0, 0)
         up_far = shifted(far, 0, 1, 0)
-        up_other, far_other = other(up), other(far)
-        state, mark = add(2, [up, up_other, far, far_other], state)
-        up_far, left, right, mark = lax.optimization_barrier((up_far, left, right, mark))
-        up_far_other, left_other, right_other = other(up_far), other(left), other(right)
-        state, mark = add(6, [up_far, left, (left, length), right, (right, length)], state)
-        state, mark = add(11, [up_far_other, left_other, (left_other, length)], state)
-        return [right_other, (right_other, length)], state
+        up_other, far_other = other(up, left, right), other(far, left, right)
+        left_other, right_other = other(left), other(right)
+        pieces = [(up, 0, (0, 1, 0)), (far, 0, (2, 0, 0)), (left, 0, (-1, 0, 0)), (right, 0, (1, 0, 0))]
+        state, mark = add(pieces, state)
+        up_left, up_right, up_far, mark = lax.optimization_barrier((up_left, up_right, up_far, mark))
+        up_far_other, up_left_other, up_right_other = other(up_far), other(up_left), other(up_right)
+        pieces = [(up_far, 0, (2, 1, 0)), (up_left, 0, (-1, 1, 0)), (up_right, 0, (1, 1, 0))]
+        state, mark = add(pieces, state)
+        pieces = [(up_other, 0, (0, 1, 1)), (far_other, 0, (2, 0, 1))]
+        pieces += [(left_other, 0, (-1, 0, 1)), (right_other, 0, (1, 0, 1))]
+        state, mark = add(pieces, state)
+        pieces = [(up_far_other, 0, (2, 1, 1)), (up_left_other, 0, (-1, 1, 1))]
+        return pieces + [(up_right_other, 0, (1, 1, 1))], state
 
     width = chans
 
-    def prepare():
-        def kernel(*refs):
-            order_kernel(chunk, *refs)
-
-        return pl.pallas_call(
-            kernel,
-            out_shape=[
-                jax.ShapeDtypeStruct((3, 16 * width, width), BF16),
-                jax.ShapeDtypeStruct((16 * width, width), BF16),
-                jax.ShapeDtypeStruct((16, width), F32),
-                jax.ShapeDtypeStruct((TABLE_ROWS, width), F32),
-            ],
-            in_specs=[HBM, HBM] + [VMEM] * 4,
-            out_specs=[VMEM] * 4,
-            scratch_shapes=[pltpu.SemaphoreType.DMA((2, 16))],
-            compiler_params=pltpu.CompilerParams(vmem_limit_bytes=4 * MIB),
-            cost_estimate=pl.CostEstimate(flops=1, bytes_accessed=1, transcendentals=0),
-        )(
-            w_in.transpose(1, 0, 2),
-            w_out,
-            norm_gain.reshape(16, width),
-            decay_rate.T,
-            residue.T,
-            w_short.reshape(SPAN * 3, width),
-        )
-
-    first, second, gain, table = prepare()
-
-    def add_in(begin, pieces, state):
-        state = project(length, begin, pieces, gain, first, state)
+    table = call(
+        lambda *refs: table_kernel(chunk, *refs),
+        jax.ShapeDtypeStruct((TABLE_ROWS, width), F32),
+        [decay_rate.T, residue.T, w_short],
+        [VMEM] * 3,
+        [],
+        4,
+    )
+    gain = norm_gain.reshape(16, width)
+    first = w_in.transpose(1, 0, 2)
+    second = w_out
+
+    def add_in(pieces, state):
+        state = project(length, pieces, gain, first, state)
         return state, state[0]
 
     pieces, state = gather(tokens, table, add_in)
@@ -470,7 +452,7 @@
     ins = [gain, first] + flat + list(state) + [table]
 
     def kernel(*refs):
-        local_kernel(14, layout, chunk, *refs)
+        local_kernel(layout, chunk, *refs)
 
     gate, local, before, load = call(
         kernel,
@@ -487,7 +469,6 @@
             pltpu.VMEM((MODES, chans), F32),
         ],
         20,
-        4 * 10**9,
     )
     loads = lax.all_to_all(load, "ctx", 0, 0, tiled=True)
     ins = [loads, gate, local, before, table]
@@ -506,15 +487,14 @@
             pltpu.VMEM((MODES * SUBS, chans), F32),
         ],
         12,
-        2 * 10**9,
     )
 
-    def add_out(begin, pieces, state):
-        state = out_project(length, begin, pieces, second, state)
+    def add_out(pieces, state):
+        state = out_project(length, pieces, second, state)
         return state, state
 
     pieces, state = gather(mixed, None, add_out)
-    return out_project(length, 14, pieces, second, state, tokens)
+    return out_project(length, pieces, second, state, tokens)
 
 
 def solution(mesh):

time: 127 us -> 114 us (0.90)
  waiting for transfers between devices: 54.3 us -> 34.6 us
  starting transfers between devices: 26.7 us -> 36.4 us
  Pallas kernels: 25.3 us -> 21.8 us
    ppermute x22 -> x30, waiting for transfers between devices: 54.3 us -> 34.6 us  [shifted(): return lax.ppermute(x, 'tp', pairs)]
    ppermute x22 -> x30, starting transfers between devices: 26.7 us -> 36.4 us  [shifted(): return lax.ppermute(x, 'tp', pairs)]
    pallas_call x1 -> x0, Pallas kernels: 4.8 us -> none  [prepare(): pl.pallas_call(kernel, out_shape=[jax.ShapeDtypeStruct((3, 16 * width, wi...]
    pallas_call x11 -> x12, Pallas kernels: 20.5 us -> 21.8 us  [call(): pl.pallas_call(kernel, out_shape=outs, in_specs=specs, out_specs=[VMEM] *...]
    unnamed x12 -> x15, local copies, waits for them, and re-layouts: 6.6 us -> 6.79 us
  transfers between devices with their start and end apart: 22 -> 30, of which waited for: 11 -> 12; matrix products, arithmetic and copies ran while one was open for 1% -> 1% of each run, Pallas kernels for 12% -> 9%
where the time goes in v3:
time: 114 us
  starting transfers between devices  36.4 us (32%)
  waiting for transfers between devices  34.6 us (30%)
  Pallas kernels  21.8 us (19%)
  blocking collectives  13.3 us (12%)
  local copies, waits for them, and re-layouts  7.52 us (7%)
    ppermute x30, starting transfers between devices, shifted(): return lax.ppermute(x, 'tp', pairs)  36.4 us
    ppermute x30, waiting for transfers between devices, shifted(): return lax.ppermute(x, 'tp', pairs)  34.6 us
    pallas_call x12, Pallas kernels, call(): pl.pallas_call(kernel, out_shape=outs, in_specs=specs, out_specs=[VMEM] *...  21.8 us
    all_to_all x1, blocking collectives, body(): loads = lax.all_to_all(load, 'ctx', 0, 0, tiled=True)  13.3 us
    unnamed x15, local copies, waits for them, and re-layouts  6.79 us
  transfers between devices with their start and end apart: 30, of which 12 were waited for; matrix products, arithmetic and copies ran while one was open for 1% of the time, Pallas kernels for 9%

profile of v3, /device:TPU:1, one launch (start us, length us, event | category | flops | bytes accessed | tf_op | source)
XLA Modules:
  0.0 113.7 jit_solution(8896275623023998805)
XLA Ops:
  0.0 1.4 %collective-permute-start.2 = (bf16[1024,256]{1,0:T(8,128)(2,1)}, bf16[1024,256]{1,0:T(8,128)(2,1)S(1)}, u32[]{:S(2)}, u32[]{:S(2)}) collective-permute-start(bf16[1024,256]{1,0:T(8,128)(2,1)} %refs_5_.1), channel_id=1, source_target_pairs={{0,1},{1,0},{2,3},{3,2},{4,5},{5,4},{6,7},{7,6},{8,9},{9,8},{10,11... | collective-permute-start | bytes 1572872 | tf_op jit(solution)/shard_map/ppermute | solution.py:390
  1.4 3.0 %collective-permute-start.1 = (bf16[1024,256]{1,0:T(8,128)(2,1)}, bf16[1024,256]{1,0:T(8,128)(2,1)S(1)}, u32[]{:S(2)}, u32[]{:S(2)}) collective-permute-start(bf16[1024,256]{1,0:T(8,128)(2,1)} %refs_5_.1), channel_id=1, source_target_pairs={{0,8},{1,9},{2,10},{3,11},{4,12},{5,13},{6,14},{7,15},{8,0},{9,1},... | collective-permute-start | bytes 1572872 | tf_op jit(solution)/shard_map/ppermute | solution.py:390
  4.4 3.6 %collective-permute-start = (bf16[1024,256]{1,0:T(8,128)(2,1)}, bf16[1024,256]{1,0:T(8,128)(2,1)S(1)}, u32[]{:S(2)}, u32[]{:S(2)}) collective-permute-start(bf16[1024,256]{1,0:T(8,128)(2,1)} %refs_5_.1), channel_id=1, source_target_pairs={{0,2},{1,3},{2,0},{3,1},{4,6},{5,7},{6,4},{7,5},{8,10},{9,11},{10,... | collective-permute-start | bytes 1572872 | tf_op jit(solution)/shard_map/ppermute | solution.py:390
  8.4 2.3 %collective-permute-start.7 = (bf16[1024,256]{1,0:T(8,128)(2,1)}, bf16[1024,256]{1,0:T(8,128)(2,1)S(1)}, u32[]{:S(2)}, u32[]{:S(2)}) collective-permute-start(bf16[1024,256]{1,0:T(8,128)(2,1)} %refs_5_.1), channel_id=1, source_target_pairs={{0,12},{1,13},{2,14},{3,15},{4,0},{5,1},{6,2},{7,3},{8,4},{9,5},{1... | collective-permute-start | bytes 1572872 | tf_op jit(solution)/shard_map/ppermute | solution.py:390
  10.7 0.7 copy.17.refs_2_
  11.5 0.7 copy-done.3
  12.2 0.7 copy-done.4
  13.0 0.7 reshape.3.refs_0_
  13.7 2.8 %copy-done = bf16[4096,3,256]{2,0,1:T(8,128)(2,1)S(1)} copy-done((bf16[4096,3,256]{2,0,1:T(8,128)(2,1)S(1)}, bf16[4096,3,256]{2,0,1:T(8,128)(2,1)}, u32[]{:S(2)}) %copy-start) | copy-done | bytes 6291480
  16.5 1.0 copy-done.2
  17.6 1.0 shard_map.74
  18.6 1.8 %collective-permute-done.refs_2_ = bf16[1024,256]{1,0:T(8,128)(2,1)S(1)} collective-permute-done((bf16[1024,256]{1,0:T(8,128)(2,1)}, bf16[1024,256]{1,0:T(8,128)(2,1)S(1)}, u32[]{:S(2)}, u32[]{:S(2)}) %collective-permute-start) | collective-permute-done | bytes 524320 | tf_op jit(solution)/shard_map/ppermute | solution.py:390
  20.4 2.7 %collective-permute-start.5 = (bf16[1024,256]{1,0:T(8,128)(2,1)S(1)}, bf16[1024,256]{1,0:T(8,128)(2,1)S(1)}, u32[]{:S(2)}, u32[]{:S(2)}) collective-permute-start(bf16[1024,256]{1,0:T(8,128)(2,1)S(1)} %collective-permute-done.1.refs_3_), channel_id=1, source_target_pairs={{0,2},{1,3},{2,0},{3,1},{4,6},{5,7},{6,4},{7,5},{8,10},{9,11},{10,... | collective-permute-start | bytes 1572872 | tf_op jit(solution)/shard_map/ppermute | solution.py:390
  23.1 0.7 collective-permute-start.4
  23.7 0.8 collective-permute-start.3
  24.5 3.8 %collective-permute-done.6.refs_4_ = bf16[1024,256]{1,0:T(8,128)(2,1)} collective-permute-done((bf16[1024,256]{1,0:T(8,128)(2,1)}, bf16[1024,256]{1,0:T(8,128)(2,1)}, u32[]{:S(2)}, u32[]{:S(2)}) %collective-permute-start.6) | collective-permute-done | bytes 524320 | tf_op jit(solution)/shard_map/ppermute | solution.py:390
  28.4 0.6 collective-permute-start.13
  28.9 0.6 collective-permute-start.14
  29.6 3.1 %shard_map.75 = (f32[1024,768]{1,0:T(8,128)S(1)}, f32[1024,128]{1,0:T(8,128)S(1)}) custom-call(f32[16,256]{1,0:T(8,128)S(1)} %reshape.3.refs_0_, bf16[3,4096,256]{2,1,0:T(8,128)(2,1)S(1)} %bitcast.4, bf16[1024,256]{1,0:T(8,128)(2,1)S(1)} %collective-permute-done.refs_2_, ...), custom_call_target="tpu_custom_call", output_to_operand_aliasing={{0}: (6, {}), {1}: (7, {})} | custom-call | flops 1 | bytes 1 | tf_op jit(solution)/shard_map/pallas_call | solution.py:23
  32.7 1.9 %collective-permute-done.5.refs_2_ = bf16[1024,256]{1,0:T(8,128)(2,1)S(1)} collective-permute-done((bf16[1024,256]{1,0:T(8,128)(2,1)S(1)}, bf16[1024,256]{1,0:T(8,128)(2,1)S(1)}, u32[]{:S(2)}, u32[]{:S(2)}) %collective-permute-start.5) | collective-permute-done | bytes 524320 | tf_op jit(solution)/shard_map/ppermute | solution.py:390
  34.5 1.7 %collective-permute-start.11 = (bf16[1024,256]{1,0:T(8,128)(2,1)S(1)}, bf16[1024,256]{1,0:T(8,128)(2,1)S(1)}, u32[]{:S(2)}, u32[]{:S(2)}) collective-permute-start(bf16[1024,256]{1,0:T(8,128)(2,1)S(1)} %collective-permute-done.refs_2_), channel_id=1, source_target_pairs={{0,1},{1,0},{2,3},{3,2},{4,5},{5,4},{6,7},{7,6},{8,9},{9,8},{10,11... | collective-permute-start | bytes 1572872 | tf_op jit(solution)/shard_map/ppermute | solution.py:390
  36.2 3.4 %collective-permute-done.4.refs_4_ = bf16[1024,256]{1,0:T(8,128)(2,1)S(1)} collective-permute-done((bf16[1024,256]{1,0:T(8,128)(2,1)S(1)}, bf16[1024,256]{1,0:T(8,128)(2,1)S(1)}, u32[]{:S(2)}, u32[]{:S(2)}) %collective-permute-start.4) | collective-permute-done | bytes 524320 | tf_op jit(solution)/shard_map/ppermute | solution.py:390
  39.6 0.8 collective-permute-start.12
  41.2 1.6 %shard_map.76 = (f32[1024,768]{1,0:T(8,128)S(1)}, f32[1024,128]{1,0:T(8,128)S(1)}) custom-call(f32[16,256]{1,0:T(8,128)S(1)} %reshape.3.refs_0_, bf16[3,4096,256]{2,1,0:T(8,128)(2,1)S(1)} %bitcast.5, bf16[1024,256]{1,0:T(8,128)(2,1)S(1)} %collective-permute-done.5.refs_2_, ...), custom_call_target="tpu_custom_call", output_to_operand_aliasing={{0}: (5, {}), {1}: (6, {})} | custom-call | flops 1 | bytes 1 | tf_op jit(solution)/shard_map/pallas_call | solution.py:23
  42.9 2.0 %shard_map.77 = (f32[1024,768]{1,0:T(8,128)S(1)}, f32[1024,128]{1,0:T(8,128)S(1)}) custom-call(f32[16,256]{1,0:T(8,128)S(1)} %reshape.3.refs_0_, bf16[3,4096,256]{2,1,0:T(8,128)(2,1)S(1)} %bitcast.6, bf16[1024,256]{1,0:T(8,128)(2,1)S(1)} %collective-permute-done.11.refs_2_, ...), custom_call_target="tpu_custom_call", output_to_operand_aliasing={{0}: (6, {}), {1}: (7, {})} | custom-call | flops 1 | bytes 1 | tf_op jit(solution)/shard_map/pallas_call | solution.py:23
  45.0 0.7 slice-done.1
  45.7 7.9 %shard_map.78 = (f32[1024,256]{1,0:T(8,128)S(1)}, f32[1024,256]{1,0:T(8,128)S(1)}, f32[128,256]{1,0:T(8,128)S(1)}, bf16[8,80,256]{2,1,0:T(8,128)(2,1)S(1)}) custom-call(f32[16,256]{1,0:T(8,128)S(1)} %reshape.3.refs_0_, bf16[3,4096,256]{2,1,0:T(8,128)(2,1)S(1)} %bitcast.9, bf16[1024,256]{1,0:T(8,128)(2,1)S(1)} %collective-permute-done.8.refs_2_, ...), custom_call_target="tpu_custom_call" | custom-call | flops 1 | bytes 1 | tf_op jit(solution)/shard_map/pallas_call | solution.py:23
  53.7 13.3 %all_to_all.5.refs_0_ = bf16[8,80,256]{2,1,0:T(8,128)(2,1)S(1)} all-to-all(bf16[8,80,256]{2,1,0:T(8,128)(2,1)S(1)} %get-tuple-element.48), channel_id=1, replica_groups=mesh['ctx'=8,'tp'=16] {'ctx'}, dimensions={0} | all-to-all | bytes 655360 | tf_op jit(solution)/shard_map/all_to_all | solution.py:473
  67.0 2.1 %shard_map.79.refs_1_ = bf16[1024,256]{1,0:T(8,128)(2,1)S(1)} custom-call(bf16[8,80,256]{2,1,0:T(8,128)(2,1)S(1)} %all_to_all.5.refs_0_, f32[1024,256]{1,0:T(8,128)S(1)} %get-tuple-element.49.refs_1_, f32[1024,256]{1,0:T(8,128)S(1)} %get-tuple-element.50.refs_2_, f32[128,256]{1,0:T(8,128)S(1)} %get-tuple-element.51.refs_3_, ...), custom_call_target="tpu_custom_call" | custom-call | flops 1 | bytes 1 | tf_op jit(solution)/shard_map/pallas_call | solution.py:23
  69.1 1.2 %collective-permute-start.17 = (bf16[1024,256]{1,0:T(8,128)(2,1)S(1)}, bf16[1024,256]{1,0:T(8,128)(2,1)S(1)}, u32[]{:S(2)}, u32[]{:S(2)}) collective-permute-start(bf16[1024,256]{1,0:T(8,128)(2,1)S(1)} %shard_map.79.refs_1_), channel_id=1, source_target_pairs={{0,1},{1,0},{2,3},{3,2},{4,5},{5,4},{6,7},{7,6},{8,9},{9,8},{10,11... | collective-permute-start | bytes 1572872 | tf_op jit(solution)/shard_map/ppermute | solution.py:390
  70.2 2.3 %collective-permute-start.16 = (bf16[1024,256]{1,0:T(8,128)(2,1)S(1)}, bf16[1024,256]{1,0:T(8,128)(2,1)S(1)}, u32[]{:S(2)}, u32[]{:S(2)}) collective-permute-start(bf16[1024,256]{1,0:T(8,128)(2,1)S(1)} %shard_map.79.refs_1_), channel_id=1, source_target_pairs={{0,8},{1,9},{2,10},{3,11},{4,12},{5,13},{6,14},{7,15},{8,0},{9,1},... | collective-permute-start | bytes 1572872 | tf_op jit(solution)/shard_map/ppermute | solution.py:390
  72.5 2.8 %collective-permute-start.15 = (bf16[1024,256]{1,0:T(8,128)(2,1)S(1)}, bf16[1024,256]{1,0:T(8,128)(2,1)S(1)}, u32[]{:S(2)}, u32[]{:S(2)}) collective-permute-start(bf16[1024,256]{1,0:T(8,128)(2,1)S(1)} %shard_map.79.refs_1_), channel_id=1, source_target_pairs={{0,2},{1,3},{2,0},{3,1},{4,6},{5,7},{6,4},{7,5},{8,10},{9,11},{10,... | collective-permute-start | bytes 1572872 | tf_op jit(solution)/shard_map/ppermute | solution.py:390
  75.3 1.5 %collective-permute-start.22 = (bf16[1024,256]{1,0:T(8,128)(2,1)S(1)}, bf16[1024,256]{1,0:T(8,128)(2,1)S(1)}, u32[]{:S(2)}, u32[]{:S(2)}) collective-permute-start(bf16[1024,256]{1,0:T(8,128)(2,1)S(1)} %shard_map.79.refs_1_), channel_id=1, source_target_pairs={{0,12},{1,13},{2,14},{3,15},{4,0},{5,1},{6,2},{7,3},{8,4},{9,5},{1... | collective-permute-start | bytes 1572872 | tf_op jit(solution)/shard_map/ppermute | solution.py:390
  77.3 7.9 %collective-permute-done.16.refs_2_ = bf16[1024,256]{1,0:T(8,128)(2,1)S(1)} collective-permute-done((bf16[1024,256]{1,0:T(8,128)(2,1)S(1)}, bf16[1024,256]{1,0:T(8,128)(2,1)S(1)}, u32[]{:S(2)}, u32[]{:S(2)}) %collective-permute-start.16) | collective-permute-done | bytes 524320 | tf_op jit(solution)/shard_map/ppermute | solution.py:390
  85.3 1.9 %collective-permute-done.15.refs_1_ = bf16[1024,256]{1,0:T(8,128)(2,1)S(1)} collective-permute-done((bf16[1024,256]{1,0:T(8,128)(2,1)S(1)}, bf16[1024,256]{1,0:T(8,128)(2,1)S(1)}, u32[]{:S(2)}, u32[]{:S(2)}) %collective-permute-start.15) | collective-permute-done | bytes 524320 | tf_op jit(solution)/shard_map/ppermute | solution.py:390
  87.2 2.8 %collective-permute-start.20 = (bf16[1024,256]{1,0:T(8,128)(2,1)S(1)}, bf16[1024,256]{1,0:T(8,128)(2,1)S(1)}, u32[]{:S(2)}, u32[]{:S(2)}) collective-permute-start(bf16[1024,256]{1,0:T(8,128)(2,1)S(1)} %collective-permute-done.16.refs_2_), channel_id=1, source_target_pairs={{0,2},{1,3},{2,0},{3,1},{4,6},{5,7},{6,4},{7,5},{8,10},{9,11},{10,... | collective-permute-start | bytes 1572872 | tf_op jit(solution)/shard_map/ppermute | solution.py:390
  90.0 1.5 %collective-permute-start.19 = (bf16[1024,256]{1,0:T(8,128)(2,1)S(1)}, bf16[1024,256]{1,0:T(8,128)(2,1)S(1)}, u32[]{:S(2)}, u32[]{:S(2)}) collective-permute-start(bf16[1024,256]{1,0:T(8,128)(2,1)S(1)} %collective-permute-done.15.refs_1_), channel_id=1, source_target_pairs={{0,12},{1,13},{2,14},{3,15},{4,0},{5,1},{6,2},{7,3},{8,4},{9,5},{1... | collective-permute-start | bytes 1572872 | tf_op jit(solution)/shard_map/ppermute | solution.py:390
  91.5 4.9 %collective-permute-done.22.refs_4_ = bf16[1024,256]{1,0:T(8,128)(2,1)S(1)} collective-permute-done((bf16[1024,256]{1,0:T(8,128)(2,1)S(1)}, bf16[1024,256]{1,0:T(8,128)(2,1)S(1)}, u32[]{:S(2)}, u32[]{:S(2)}) %collective-permute-start.22) | collective-permute-done | bytes 524320 | tf_op jit(solution)/shard_map/ppermute | solution.py:390
  96.5 1.3 %collective-permute-start.29 = (bf16[1024,256]{1,0:T(8,128)(2,1)S(1)}, bf16[1024,256]{1,0:T(8,128)(2,1)S(1)}, u32[]{:S(2)}, u32[]{:S(2)}) collective-permute-start(bf16[1024,256]{1,0:T(8,128)(2,1)S(1)} %collective-permute-done.22.refs_4_), channel_id=1, source_target_pairs={{0,1},{1,0},{2,3},{3,2},{4,5},{5,4},{6,7},{7,6},{8,9},{9,8},{10,11... | collective-permute-start | bytes 1572872 | tf_op jit(solution)/shard_map/ppermute | solution.py:390
  97.8 0.7 shard_map.81.refs_4_
  98.6 2.3 %collective-permute-done.20.refs_1_ = bf16[1024,256]{1,0:T(8,128)(2,1)S(1)} collective-permute-done((bf16[1024,256]{1,0:T(8,128)(2,1)S(1)}, bf16[1024,256]{1,0:T(8,128)(2,1)S(1)}, u32[]{:S(2)}, u32[]{:S(2)}) %collective-permute-start.20) | collective-permute-done | bytes 524320 | tf_op jit(solution)/shard_map/ppermute | solution.py:390
  100.9 2.1 %collective-permute-start.26 = (bf16[1024,256]{1,0:T(8,128)(2,1)S(1)}, bf16[1024,256]{1,0:T(8,128)(2,1)S(1)}, u32[]{:S(2)}, u32[]{:S(2)}) collective-permute-start(bf16[1024,256]{1,0:T(8,128)(2,1)S(1)} %collective-permute-done.15.refs_1_), channel_id=1, source_target_pairs={{0,1},{1,0},{2,3},{3,2},{4,5},{5,4},{6,7},{7,6},{8,9},{9,8},{10,11... | collective-permute-start | bytes 1572872 | tf_op jit(solution)/shard_map/ppermute | solution.py:390
  103.0 4.7 %collective-permute-done.19.refs_3_ = bf16[1024,256]{1,0:T(8,128)(2,1)S(1)} collective-permute-done((bf16[1024,256]{1,0:T(8,128)(2,1)S(1)}, bf16[1024,256]{1,0:T(8,128)(2,1)S(1)}, u32[]{:S(2)}, u32[]{:S(2)}) %collective-permute-start.19) | collective-permute-done | bytes 524320 | tf_op jit(solution)/shard_map/ppermute | solution.py:390
  107.7 0.9 collective-permute-start.27
  110.1 0.7 shard_map.83.refs_4_
  110.9 0.7 collective-permute-done.24.refs_2_
  111.6 0.7 collective-permute-done.25.refs_3_
  112.4 1.4 %shard_map.84 = bf16[1024,256]{1,0:T(8,128)(2,1)} custom-call(bf16[4096,256]{1,0:T(8,128)(2,1)S(1)} %copy-done.1, bf16[1024,256]{1,0:T(8,128)(2,1)S(1)} %collective-permute-done.23.refs_1_, bf16[1024,256]{1,0:T(8,128)(2,1)S(1)} %collective-permute-done.24.refs_2_, bf16[1024,256]{1,0:T(8,128)(2,1)S(1)} %collective-permute-done.25.refs_3_, ...), custom_call_target="tpu_custom_call" | custom-call | flops 1 | bytes 1 | tf_op jit(solution)/shard_map/pallas_call | solution.py:23
  (42 shorter events, 3.4 us)
Async XLA Ops:
  0.0 13.7 %collective-permute-start.2 = (bf16[1024,256]{1,0:T(8,128)(2,1)}, bf16[1024,256]{1,0:T(8,128)(2,1)S(1)}, u32[]{:S(2)}, u32[]{:S(2)}) collective-permute-start(bf16[1024,256]{1,0:T(8,128)(2,1)} %refs_5_.1), channel_id=1, source_target_pairs={{0,1},{1,0},{2,3},{3,2},{4,5},{5,4},{6,7},{7,6},{8,9},{9,8},{10,11... | collective-permute-start | bytes 1572872 | tf_op jit(solution)/shard_map/ppermute | solution.py:390
  1.4 17.2 %collective-permute-start.1 = (bf16[1024,256]{1,0:T(8,128)(2,1)}, bf16[1024,256]{1,0:T(8,128)(2,1)S(1)}, u32[]{:S(2)}, u32[]{:S(2)}) collective-permute-start(bf16[1024,256]{1,0:T(8,128)(2,1)} %refs_5_.1), channel_id=1, source_target_pairs={{0,8},{1,9},{2,10},{3,11},{4,12},{5,13},{6,14},{7,15},{8,0},{9,1},... | collective-permute-start | bytes 1572872 | tf_op jit(solution)/shard_map/ppermute | solution.py:390
  4.4 15.9 %collective-permute-start = (bf16[1024,256]{1,0:T(8,128)(2,1)}, bf16[1024,256]{1,0:T(8,128)(2,1)S(1)}, u32[]{:S(2)}, u32[]{:S(2)}) collective-permute-start(bf16[1024,256]{1,0:T(8,128)(2,1)} %refs_5_.1), channel_id=1, source_target_pairs={{0,2},{1,3},{2,0},{3,1},{4,6},{5,7},{6,4},{7,5},{8,10},{9,11},{10,... | collective-permute-start | bytes 1572872 | tf_op jit(solution)/shard_map/ppermute | solution.py:390
  8.0 20.3 %collective-permute-start.6 = (bf16[1024,256]{1,0:T(8,128)(2,1)}, bf16[1024,256]{1,0:T(8,128)(2,1)}, u32[]{:S(2)}, u32[]{:S(2)}) collective-permute-start(bf16[1024,256]{1,0:T(8,128)(2,1)} %refs_5_.1), channel_id=1, source_target_pairs={{0,4},{1,5},{2,6},{3,7},{4,8},{5,9},{6,10},{7,11},{8,12},{9,13},{1... | collective-permute-start | bytes 1572872 | tf_op jit(solution)/shard_map/ppermute | solution.py:390
  8.4 20.5 %collective-permute-start.7 = (bf16[1024,256]{1,0:T(8,128)(2,1)}, bf16[1024,256]{1,0:T(8,128)(2,1)S(1)}, u32[]{:S(2)}, u32[]{:S(2)}) collective-permute-start(bf16[1024,256]{1,0:T(8,128)(2,1)} %refs_5_.1), channel_id=1, source_target_pairs={{0,12},{1,13},{2,14},{3,15},{4,0},{5,1},{6,2},{7,3},{8,4},{9,5},{1... | collective-permute-start | bytes 1572872 | tf_op jit(solution)/shard_map/ppermute | solution.py:390
  11.4 0.7 copy-start.3
  12.2 0.7 copy-start.4
  13.7 2.8 %copy-start = (bf16[4096,3,256]{2,0,1:T(8,128)(2,1)S(1)}, bf16[4096,3,256]{2,0,1:T(8,128)(2,1)}, u32[]{:S(2)}) copy-start(bf16[4096,3,256]{2,0,1:T(8,128)(2,1)} %param.9) | copy-start | bytes 18874372
  16.5 1.0 copy-start.2
  20.4 14.2 %collective-permute-start.5 = (bf16[1024,256]{1,0:T(8,128)(2,1)S(1)}, bf16[1024,256]{1,0:T(8,128)(2,1)S(1)}, u32[]{:S(2)}, u32[]{:S(2)}) collective-permute-start(bf16[1024,256]{1,0:T(8,128)(2,1)S(1)} %collective-permute-done.1.refs_3_), channel_id=1, source_target_pairs={{0,2},{1,3},{2,0},{3,1},{4,6},{5,7},{6,4},{7,5},{8,10},{9,11},{10,... | collective-permute-start | bytes 1572872 | tf_op jit(solution)/shard_map/ppermute | solution.py:390
  23.1 16.6 %collective-permute-start.4 = (bf16[1024,256]{1,0:T(8,128)(2,1)S(1)}, bf16[1024,256]{1,0:T(8,128)(2,1)S(1)}, u32[]{:S(2)}, u32[]{:S(2)}) collective-permute-start(bf16[1024,256]{1,0:T(8,128)(2,1)S(1)} %collective-permute-done.refs_2_), channel_id=1, source_target_pairs={{0,12},{1,13},{2,14},{3,15},{4,0},{5,1},{6,2},{7,3},{8,4},{9,5},{1... | collective-permute-start | bytes 1572872 | tf_op jit(solution)/shard_map/ppermute | solution.py:390
  23.7 16.7 %collective-permute-start.3 = (bf16[1024,256]{1,0:T(8,128)(2,1)S(1)}, bf16[1024,256]{1,0:T(8,128)(2,1)S(1)}, u32[]{:S(2)}, u32[]{:S(2)}) collective-permute-start(bf16[1024,256]{1,0:T(8,128)(2,1)S(1)} %collective-permute-done.refs_2_), channel_id=1, source_target_pairs={{0,4},{1,5},{2,6},{3,7},{4,8},{5,9},{6,10},{7,11},{8,12},{9,13},{1... | collective-permute-start | bytes 1572872 | tf_op jit(solution)/shard_map/ppermute | solution.py:390
  28.4 12.1 %collective-permute-start.13 = (bf16[1024,256]{1,0:T(8,128)(2,1)}, bf16[1024,256]{1,0:T(8,128)(2,1)S(1)}, u32[]{:S(2)}, u32[]{:S(2)}) collective-permute-start(bf16[1024,256]{1,0:T(8,128)(2,1)} %collective-permute-done.6.refs_4_), channel_id=1, source_target_pairs={{0,1},{1,0},{2,3},{3,2},{4,5},{5,4},{6,7},{7,6},{8,9},{9,8},{10,11... | collective-permute-start | bytes 1572872 | tf_op jit(solution)/shard_map/ppermute | solution.py:390
  28.9 12.0 %collective-permute-start.14 = (bf16[1024,256]{1,0:T(8,128)(2,1)S(1)}, bf16[1024,256]{1,0:T(8,128)(2,1)S(1)}, u32[]{:S(2)}, u32[]{:S(2)}) collective-permute-start(bf16[1024,256]{1,0:T(8,128)(2,1)S(1)} %collective-permute-done.7.refs_5_), channel_id=1, source_target_pairs={{0,1},{1,0},{2,3},{3,2},{4,5},{5,4},{6,7},{7,6},{8,9},{9,8},{10,11... | collective-permute-start | bytes 1572872 | tf_op jit(solution)/shard_map/ppermute | solution.py:390
  34.5 8.3 %collective-permute-start.11 = (bf16[1024,256]{1,0:T(8,128)(2,1)S(1)}, bf16[1024,256]{1,0:T(8,128)(2,1)S(1)}, u32[]{:S(2)}, u32[]{:S(2)}) collective-permute-start(bf16[1024,256]{1,0:T(8,128)(2,1)S(1)} %collective-permute-done.refs_2_), channel_id=1, source_target_pairs={{0,1},{1,0},{2,3},{3,2},{4,5},{5,4},{6,7},{7,6},{8,9},{9,8},{10,11... | collective-permute-start | bytes 1572872 | tf_op jit(solution)/shard_map/ppermute | solution.py:390
  39.6 3.2 %collective-permute-start.12 = (bf16[1024,256]{1,0:T(8,128)(2,1)S(1)}, bf16[1024,256]{1,0:T(8,128)(2,1)S(1)}, u32[]{:S(2)}, u32[]{:S(2)}) collective-permute-start(bf16[1024,256]{1,0:T(8,128)(2,1)S(1)} %collective-permute-done.1.refs_3_), channel_id=1, source_target_pairs={{0,1},{1,0},{2,3},{3,2},{4,5},{5,4},{6,7},{7,6},{8,9},{9,8},{10,11... | collective-permute-start | bytes 1572872 | tf_op jit(solution)/shard_map/ppermute | solution.py:390
  40.4 4.5 %collective-permute-start.8 = (bf16[1024,256]{1,0:T(8,128)(2,1)S(1)}, bf16[1024,256]{1,0:T(8,128)(2,1)S(1)}, u32[]{:S(2)}, u32[]{:S(2)}) collective-permute-start(bf16[1024,256]{1,0:T(8,128)(2,1)S(1)} %collective-permute-done.5.refs_2_), channel_id=1, source_target_pairs={{0,1},{1,0},{2,3},{3,2},{4,5},{5,4},{6,7},{7,6},{8,9},{9,8},{10,11... | collective-permute-start | bytes 1572872 | tf_op jit(solution)/shard_map/ppermute | solution.py:390
  40.4 4.5 %collective-permute-start.9 = (bf16[1024,256]{1,0:T(8,128)(2,1)S(1)}, bf16[1024,256]{1,0:T(8,128)(2,1)S(1)}, u32[]{:S(2)}, u32[]{:S(2)}) collective-permute-start(bf16[1024,256]{1,0:T(8,128)(2,1)S(1)} %collective-permute-done.3.refs_3_), channel_id=1, source_target_pairs={{0,1},{1,0},{2,3},{3,2},{4,5},{5,4},{6,7},{7,6},{8,9},{9,8},{10,11... | collective-permute-start | bytes 1572872 | tf_op jit(solution)/shard_map/ppermute | solution.py:390
  40.9 4.0 %collective-permute-start.10 = (bf16[1024,256]{1,0:T(8,128)(2,1)S(1)}, bf16[1024,256]{1,0:T(8,128)(2,1)S(1)}, u32[]{:S(2)}, u32[]{:S(2)}) collective-permute-start(bf16[1024,256]{1,0:T(8,128)(2,1)S(1)} %collective-permute-done.4.refs_4_), channel_id=1, source_target_pairs={{0,1},{1,0},{2,3},{3,2},{4,5},{5,4},{6,7},{7,6},{8,9},{9,8},{10,11... | collective-permute-start | bytes 1572872 | tf_op jit(solution)/shard_map/ppermute | solution.py:390
  42.9 2.2 %slice-start = ((s8[6291456]{0:T(1024)(128)(4,1)}), s8[4194304]{0:T(1024)(128)(4,1)S(1)}, s32[]{:S(2)}) async-start(s8[6291456]{0:T(1024)(128)(4,1)} %bitcast.7), calls=%async_computation.1 | async-start | bytes 8388608
  42.9 2.9 %slice-start.1 = ((s8[6291456]{0:T(1024)(128)(4,1)}), s8[2097152]{0:T(1024)(128)(4,1)S(1)}, s32[]{:S(2)}) async-start(s8[6291456]{0:T(1024)(128)(4,1)} %bitcast.7), calls=%async_computation.2 | async-start | bytes 4194304
  53.7 23.2 %copy-start.1 = (bf16[4096,256]{1,0:T(8,128)(2,1)S(1)}, bf16[4096,256]{1,0:T(8,128)(2,1)}, u32[]{:S(2)}) copy-start(bf16[4096,256]{1,0:T(8,128)(2,1)} %refs_0_.9) | copy-start | bytes 6291460
  69.1 7.8 %collective-permute-start.17 = (bf16[1024,256]{1,0:T(8,128)(2,1)S(1)}, bf16[1024,256]{1,0:T(8,128)(2,1)S(1)}, u32[]{:S(2)}, u32[]{:S(2)}) collective-permute-start(bf16[1024,256]{1,0:T(8,128)(2,1)S(1)} %shard_map.79.refs_1_), channel_id=1, source_target_pairs={{0,1},{1,0},{2,3},{3,2},{4,5},{5,4},{6,7},{7,6},{8,9},{9,8},{10,11... | collective-permute-start | bytes 1572872 | tf_op jit(solution)/shard_map/ppermute | solution.py:390
  70.2 15.0 %collective-permute-start.16 = (bf16[1024,256]{1,0:T(8,128)(2,1)S(1)}, bf16[1024,256]{1,0:T(8,128)(2,1)S(1)}, u32[]{:S(2)}, u32[]{:S(2)}) collective-permute-start(bf16[1024,256]{1,0:T(8,128)(2,1)S(1)} %shard_map.79.refs_1_), channel_id=1, source_target_pairs={{0,8},{1,9},{2,10},{3,11},{4,12},{5,13},{6,14},{7,15},{8,0},{9,1},... | collective-permute-start | bytes 1572872 | tf_op jit(solution)/shard_map/ppermute | solution.py:390
  72.5 14.7 %collective-permute-start.15 = (bf16[1024,256]{1,0:T(8,128)(2,1)S(1)}, bf16[1024,256]{1,0:T(8,128)(2,1)S(1)}, u32[]{:S(2)}, u32[]{:S(2)}) collective-permute-start(bf16[1024,256]{1,0:T(8,128)(2,1)S(1)} %shard_map.79.refs_1_), channel_id=1, source_target_pairs={{0,2},{1,3},{2,0},{3,1},{4,6},{5,7},{6,4},{7,5},{8,10},{9,11},{10,... | collective-permute-start | bytes 1572872 | tf_op jit(solution)/shard_map/ppermute | solution.py:390
  75.3 21.1 %collective-permute-start.22 = (bf16[1024,256]{1,0:T(8,128)(2,1)S(1)}, bf16[1024,256]{1,0:T(8,128)(2,1)S(1)}, u32[]{:S(2)}, u32[]{:S(2)}) collective-permute-start(bf16[1024,256]{1,0:T(8,128)(2,1)S(1)} %shard_map.79.refs_1_), channel_id=1, source_target_pairs={{0,12},{1,13},{2,14},{3,15},{4,0},{5,1},{6,2},{7,3},{8,4},{9,5},{1... | collective-permute-start | bytes 1572872 | tf_op jit(solution)/shard_map/ppermute | solution.py:390
  76.9 21.0 %collective-permute-start.21 = (bf16[1024,256]{1,0:T(8,128)(2,1)S(1)}, bf16[1024,256]{1,0:T(8,128)(2,1)S(1)}, u32[]{:S(2)}, u32[]{:S(2)}) collective-permute-start(bf16[1024,256]{1,0:T(8,128)(2,1)S(1)} %shard_map.79.refs_1_), channel_id=1, source_target_pairs={{0,4},{1,5},{2,6},{3,7},{4,8},{5,9},{6,10},{7,11},{8,12},{9,13},{1... | collective-permute-start | bytes 1572872 | tf_op jit(solution)/shard_map/ppermute | solution.py:390
  87.2 13.7 %collective-permute-start.20 = (bf16[1024,256]{1,0:T(8,128)(2,1)S(1)}, bf16[1024,256]{1,0:T(8,128)(2,1)S(1)}, u32[]{:S(2)}, u32[]{:S(2)}) collective-permute-start(bf16[1024,256]{1,0:T(8,128)(2,1)S(1)} %collective-permute-done.16.refs_2_), channel_id=1, source_target_pairs={{0,2},{1,3},{2,0},{3,1},{4,6},{5,7},{6,4},{7,5},{8,10},{9,11},{10,... | collective-permute-start | bytes 1572872 | tf_op jit(solution)/shard_map/ppermute | solution.py:390
  90.0 17.7 %collective-permute-start.19 = (bf16[1024,256]{1,0:T(8,128)(2,1)S(1)}, bf16[1024,256]{1,0:T(8,128)(2,1)S(1)}, u32[]{:S(2)}, u32[]{:S(2)}) collective-permute-start(bf16[1024,256]{1,0:T(8,128)(2,1)S(1)} %collective-permute-done.15.refs_1_), channel_id=1, source_target_pairs={{0,12},{1,13},{2,14},{3,15},{4,0},{5,1},{6,2},{7,3},{8,4},{9,5},{1... | collective-permute-start | bytes 1572872 | tf_op jit(solution)/shard_map/ppermute | solution.py:390
  91.5 17.1 %collective-permute-start.18 = (bf16[1024,256]{1,0:T(8,128)(2,1)S(1)}, bf16[1024,256]{1,0:T(8,128)(2,1)S(1)}, u32[]{:S(2)}, u32[]{:S(2)}) collective-permute-start(bf16[1024,256]{1,0:T(8,128)(2,1)S(1)} %collective-permute-done.15.refs_1_), channel_id=1, source_target_pairs={{0,4},{1,5},{2,6},{3,7},{4,8},{5,9},{6,10},{7,11},{8,12},{9,13},{1... | collective-permute-start | bytes 1572872 | tf_op jit(solution)/shard_map/ppermute | solution.py:390
  96.5 12.1 %collective-permute-start.29 = (bf16[1024,256]{1,0:T(8,128)(2,1)S(1)}, bf16[1024,256]{1,0:T(8,128)(2,1)S(1)}, u32[]{:S(2)}, u32[]{:S(2)}) collective-permute-start(bf16[1024,256]{1,0:T(8,128)(2,1)S(1)} %collective-permute-done.22.refs_4_), channel_id=1, source_target_pairs={{0,1},{1,0},{2,3},{3,2},{4,5},{5,4},{6,7},{7,6},{8,9},{9,8},{10,11... | collective-permute-start | bytes 1572872 | tf_op jit(solution)/shard_map/ppermute | solution.py:390
  97.8 11.3 %collective-permute-start.28 = (bf16[1024,256]{1,0:T(8,128)(2,1)S(1)}, bf16[1024,256]{1,0:T(8,128)(2,1)S(1)}, u32[]{:S(2)}, u32[]{:S(2)}) collective-permute-start(bf16[1024,256]{1,0:T(8,128)(2,1)S(1)} %collective-permute-done.21.refs_3_), channel_id=1, source_target_pairs={{0,1},{1,0},{2,3},{3,2},{4,5},{5,4},{6,7},{7,6},{8,9},{9,8},{10,11... | collective-permute-start | bytes 1572872 | tf_op jit(solution)/shard_map/ppermute | solution.py:390
  100.9 8.9 %collective-permute-start.26 = (bf16[1024,256]{1,0:T(8,128)(2,1)S(1)}, bf16[1024,256]{1,0:T(8,128)(2,1)S(1)}, u32[]{:S(2)}, u32[]{:S(2)}) collective-permute-start(bf16[1024,256]{1,0:T(8,128)(2,1)S(1)} %collective-permute-done.15.refs_1_), channel_id=1, source_target_pairs={{0,1},{1,0},{2,3},{3,2},{4,5},{5,4},{6,7},{7,6},{8,9},{9,8},{10,11... | collective-permute-start | bytes 1572872 | tf_op jit(solution)/shard_map/ppermute | solution.py:390
  107.7 2.4 %collective-permute-start.27 = (bf16[1024,256]{1,0:T(8,128)(2,1)S(1)}, bf16[1024,256]{1,0:T(8,128)(2,1)S(1)}, u32[]{:S(2)}, u32[]{:S(2)}) collective-permute-start(bf16[1024,256]{1,0:T(8,128)(2,1)S(1)} %collective-permute-done.16.refs_2_), channel_id=1, source_target_pairs={{0,1},{1,0},{2,3},{3,2},{4,5},{5,4},{6,7},{7,6},{8,9},{9,8},{10,11... | collective-permute-start | bytes 1572872 | tf_op jit(solution)/shard_map/ppermute | solution.py:390
  108.6 2.3 %collective-permute-start.23 = (bf16[1024,256]{1,0:T(8,128)(2,1)S(1)}, bf16[1024,256]{1,0:T(8,128)(2,1)S(1)}, u32[]{:S(2)}, u32[]{:S(2)}) collective-permute-start(bf16[1024,256]{1,0:T(8,128)(2,1)S(1)} %collective-permute-done.20.refs_1_), channel_id=1, source_target_pairs={{0,1},{1,0},{2,3},{3,2},{4,5},{5,4},{6,7},{7,6},{8,9},{9,8},{10,11... | collective-permute-start | bytes 1572872 | tf_op jit(solution)/shard_map/ppermute | solution.py:390
  108.6 3.0 %collective-permute-start.24 = (bf16[1024,256]{1,0:T(8,128)(2,1)S(1)}, bf16[1024,256]{1,0:T(8,128)(2,1)S(1)}, u32[]{:S(2)}, u32[]{:S(2)}) collective-permute-start(bf16[1024,256]{1,0:T(8,128)(2,1)S(1)} %collective-permute-done.18.refs_2_), channel_id=1, source_target_pairs={{0,1},{1,0},{2,3},{3,2},{4,5},{5,4},{6,7},{7,6},{8,9},{9,8},{10,11... | collective-permute-start | bytes 1572872 | tf_op jit(solution)/shard_map/ppermute | solution.py:390
  109.1 3.3 %collective-permute-start.25 = (bf16[1024,256]{1,0:T(8,128)(2,1)S(1)}, bf16[1024,256]{1,0:T(8,128)(2,1)S(1)}, u32[]{:S(2)}, u32[]{:S(2)}) collective-permute-start(bf16[1024,256]{1,0:T(8,128)(2,1)S(1)} %collective-permute-done.19.refs_3_), channel_id=1, source_target_pairs={{0,1},{1,0},{2,3},{3,2},{4,5},{5,4},{6,7},{7,6},{8,9},{9,8},{10,11... | collective-permute-start | bytes 1572872 | tf_op jit(solution)/shard_map/ppermute | solution.py:390

commit v4 on v3

--- a/solution.py
+++ b/solution.py
@@ -17,6 +17,8 @@
 SMEM = pl.BlockSpec(memory_space=pltpu.SMEM)
 MIB = 1024 * 1024
 TILE = 512
+GROUP = 4
+PAD = 8
 
 
 def call(kernel, outs, ins, specs, scratch, limit, aliases=None):
@@ -46,6 +48,12 @@
 ):
     TABLE[_name] = (sum(rows for _, rows in TABLE.values()), _rows)
 TABLE_ROWS = sum(rows for _, rows in TABLE.values())
+
+def add_up(terms):
+    while len(terms) > 1:
+        terms = [a + b for a, b in zip(terms[::2], terms[1::2])] + terms[len(terms) & ~1 :]
+    return terms[0]
+
 
 def part(table, name):
     begin, rows = TABLE[name]
@@ -162,7 +170,8 @@
     width = gate.shape[1]
     rows_all = acc.shape[0]
     halves = width // LANES
-    proj[:, 0:8, :] = jnp.zeros((3 * halves, 8, LANES), F32)
+    pitch = chunk + PAD
+    proj[:, 0:PAD, :] = jnp.zeros((3 * halves, PAD, LANES), F32)
     for r in range(rows_all // tile):
         rows = pl.ds(r * tile, tile)
         total, squares = add_pieces(layout, gain, w, pieces, r, tile)
@@ -173,63 +182,62 @@
             value = (acc[rows, cols] + total[s]) * scale
             value = value.astype(BF16).astype(F32)
             for g in range(halves):
-                proj[s * halves + g, pl.ds(8 + r * tile, tile), :] = value[:, g * LANES : (g + 1) * LANES]
+                for k in range(tile // chunk):
+                    run = r * (tile // chunk) + k
+                    piece = value[k * chunk : (k + 1) * chunk, g * LANES : (g + 1) * LANES]
+                    proj[s * halves + g, pl.ds(run * pitch + PAD, chunk), :] = piece
+                    if run + 1 < SUBS:
+                        proj[s * halves + g, pl.ds((run + 1) * pitch, PAD), :] = piece[chunk - PAD :]
     head = lax.broadcasted_iota(jnp.int32, (SUBS, LANES), 0) == 0
     for g in range(width // LANES):
         lanes = slice(g * LANES, (g + 1) * LANES)
 
         def strided(s, t):
-            return proj[s * halves + g, pl.ds(8 + t, SUBS, stride=chunk), :]
-
-        def step(t, carry, masked):
-            windows, states = carry
+            return proj[s * halves + g, pl.ds(PAD + t, SUBS, stride=pitch), :]
+
+        unroll = 8
+
+        def steps(i, states, masked=False):
+            begin = i * unroll
             short = []
-            moved = []
             for s in range(3):
-                newest = strided(s, t)
-                line = windows[s] + [newest]
-                value = None
-                for j in range(SPAN):
-                    at = (j * 3 + s) * SUBS
-                    term = taps[at : at + SUBS, lanes] * line[REACH - j]
-                    value = term if value is None else value + term
-                short.append(value)
-                moved.append(line[1:])
-            kv = (short[1] * short[2]).astype(BF16).astype(F32)
+                rows = [strided(s, begin + u) for u in range(-REACH, unroll)]
+                weights = [
+                    taps[(j * 3 + s) * SUBS : (j * 3 + s + 1) * SUBS, lanes] for j in range(SPAN)
+                ]
+                short.append(
+                    [
+                        add_up([weights[j] * rows[REACH + u - j] for j in range(SPAN)])
+                        for u in range(unroll)
+                    ]
+                )
+            kv = [(short[1][u] * short[2][u]).astype(BF16).astype(F32) for u in range(unroll)]
             if masked:
-                kv = jnp.where(head, 0.0, kv)
-            out = None
+                kv = [jnp.where(head, 0.0, v) if u < REACH else v for u, v in enumerate(kv)]
+            outs = [None] * unroll
             later = []
-            for n in range(MODES):
-                at = n * SUBS
-                state = decay[at : at + SUBS, lanes] * states[n] + kv
-                later.append(state)
-                term = weight[at : at + SUBS, lanes] * state
-                out = term if out is None else out + term
-            place = pl.ds(pl.multiple_of(t * SUBS, SUBS), SUBS)
-            gate[place, lanes] = short[0].astype(BF16).astype(F32)
-            local[place, lanes] = out
-            return moved, later
-
-        windows = [
-            [strided(s, t) for t in range(-REACH, 0)]
-            for s in range(3)
-        ]
-        carry = (windows, [jnp.zeros((SUBS, LANES), F32)] * MODES)
-        unroll = 8
-        for t in range(unroll):
-            carry = step(t, carry, t < REACH)
-
-        def steps(i, carry):
+            for first in range(0, MODES, GROUP):
+                some = range(first, first + GROUP)
+                decays = [decay[n * SUBS : (n + 1) * SUBS, lanes] for n in some]
+                weights = [weight[n * SUBS : (n + 1) * SUBS, lanes] for n in some]
+                now = [states[n] for n in some]
+                for u in range(unroll):
+                    now = [decays[k] * now[k] + kv[u] for k in range(GROUP)]
+                    term = add_up([weights[k] * now[k] for k in range(GROUP)])
+                    outs[u] = term if outs[u] is None else outs[u] + term
+                later.extend(now)
             for u in range(unroll):
-                carry = step(i * unroll + u, carry, False)
-            return carry
-
-        carry = lax.fori_loop(1, chunk // unroll, steps, carry)
+                place = pl.ds(pl.multiple_of((begin + u) * SUBS, SUBS), SUBS)
+                gate[place, lanes] = short[0][u].astype(BF16).astype(F32)
+                local[place, lanes] = outs[u]
+            return later
+
+        states = steps(0, [jnp.zeros((SUBS, LANES), F32)] * MODES, True)
+        states = lax.fori_loop(1, chunk // unroll, steps, states)
         place = lax.broadcasted_iota(jnp.int32, (SUBS, LANES), 0)
         for n in range(MODES):
             at = n * SUBS
-            state = carry[1][n]
+            state = states[n]
             for level, hop in enumerate((1, 2, 4)):
                 moved = jnp.where(place >= hop, pltpu.roll(state, hop, 0), 0.0)
                 jump = jumps[level * MODES + n : level * MODES + n + 1, lanes]
@@ -242,8 +250,8 @@
     for s in range(3):
         sides = []
         for g in range(halves):
-            tail = proj[s * halves + g, rows_all : rows_all + 8, :]
-            sides.append(jnp.concatenate([tail, proj[s * halves + g, 8:16, :]], axis=0))
+            tail = proj[s * halves + g, SUBS * pitch - PAD : SUBS * pitch, :]
+            sides.append(jnp.concatenate([tail, proj[s * halves + g, PAD : 2 * PAD, :]], axis=0))
         ends.append(jnp.concatenate(sides, axis=1).astype(BF16))
     for i, value in enumerate(ends):
         for d in range(8):
@@ -254,7 +262,7 @@
     loads, gate, local, before, table, mixed, held, whole, start = refs
     names = ("taps", "decay", "weight", "power", "power_less", "ahead", "early", "late")
     taps, decay, weight, power, power_less, ahead, early, late = (part(table, n) for n in names)
-    step_rows = 64
+    step_rows = 64 + PAD
     width = mixed.shape[1]
     me = lax.axis_index("ctx")
     for d in range(9):
@@ -265,10 +273,10 @@
             value = jnp.concatenate([value[0:16] + value[16:32], value[32:]], axis=0)
             value = jnp.where(me >= d, value, 0.0)
         for g in range(width // LANES):
-            piece = jnp.zeros((step_rows, LANES), F32)
+            piece = jnp.zeros((64, LANES), F32)
             if d < 8:
                 piece = value[:, g * LANES : (g + 1) * LANES]
-            held[g, d * step_rows : (d + 1) * step_rows, :] = piece
+            held[g, d * step_rows : d * step_rows + 64, :] = piece
     place = lax.broadcasted_iota(jnp.int32, (SUBS, LANES), 0)
     head = place == 0
     for g in range(width // LANES):
@@ -306,21 +314,21 @@
             state = state + power_less[at : at + SUBS, lanes] * own[0:1, :]
             start[at : at + SUBS, lanes] = state * weight[at : at + SUBS, lanes]
 
+        decays = [decay[n * SUBS : (n + 1) * SUBS, lanes] for n in range(MODES)]
+
         def step(t, states, extra, fixed):
-            out = None
             later = []
             for n in range(MODES):
-                at = n * SUBS
-                state = decay[at : at + SUBS, lanes] * states[n]
+                state = decays[n] * states[n]
                 if extra is not None:
-                    state = state + weight[at : at + SUBS, lanes] * extra
+                    state = state + weight[n * SUBS : (n + 1) * SUBS, lanes] * extra
                 later.append(state)
-                out = state if out is None else out + state
+            out = add_up(later)
             rows = pl.ds(pl.multiple_of(t * SUBS, SUBS), SUBS)
             q_now = gate[rows, lanes]
             if fixed is not None:
                 q_now = jnp.where(head, fixed, q_now)
-            whole[g, pl.ds(t, SUBS, stride=chunk), :] = q_now * (out + local[rows, lanes])
+            whole[g, pl.ds(t, SUBS, stride=chunk + PAD), :] = q_now * (out + local[rows, lanes])
             return later
 
         states = [start[n * SUBS : (n + 1) * SUBS, lanes] for n in range(MODES)]
@@ -337,7 +345,9 @@
 
         lax.fori_loop(1, chunk // unroll, steps, states)
     for g in range(width // LANES):
-        mixed[:, g * LANES : (g + 1) * LANES] = whole[g].astype(BF16)
+        for k in range(SUBS):
+            rows = whole[g, k * (chunk + PAD) : k * (chunk + PAD) + chunk, :]
+            mixed[k * chunk : (k + 1) * chunk, g * LANES : (g + 1) * LANES] = rows.astype(BF16)
 
 
 def out_kernel(layout, fresh, last, w, *refs):
@@ -403,11 +413,11 @@
         return shifted(tie(p, *after) if after else p, 0, 0, 1)
 
     def gather(x, start, add):
-        up = shifted(x, 0, 1, 0)
         far = shifted(x, 2, 0, 0)
         left = shifted(x, 1, 0, 0)
         right = shifted(x, -1, 0, 0)
         x_other = other(x)
+        up = shifted(tie(x, x_other), 0, 1, 0)
         if start is not None:
             x_other = tie(x_other, start)
         state, mark = add([(x, 0, (0, 0, 0)), (x_other, 0, (0, 0, 1))], None)
@@ -465,7 +475,7 @@
         ins,
         [VMEM] * len(ins),
         [
-            pltpu.VMEM((3 * chans // LANES, length + 8, LANES), F32),
+            pltpu.VMEM((3 * chans // LANES, length + SUBS * PAD, LANES), F32),
             pltpu.VMEM((MODES, chans), F32),
         ],
         20,
@@ -482,8 +492,8 @@
         ins,
         [VMEM] * len(ins),
         [
-            pltpu.VMEM((chans // LANES, 9 * 64, LANES), F32),
-            pltpu.VMEM((chans // LANES, length, LANES), F32),
+            pltpu.VMEM((chans // LANES, 9 * (64 + PAD), LANES), F32),
+            pltpu.VMEM((chans // LANES, length + SUBS * PAD, LANES), F32),
             pltpu.VMEM((MODES * SUBS, chans), F32),
         ],
         12,

time: 114 us -> 112 us (0.982)
  Pallas kernels: 21.8 us -> 19.6 us
    pallas_call x12, Pallas kernels: 21.8 us -> 19.6 us  [call(): pl.pallas_call(kernel, out_shape=outs, in_specs=specs, out_specs=[VMEM] *...]
where the time goes in v4:
time: 112 us
  starting transfers between devices  36.5 us (33%)
  waiting for transfers between devices  34.4 us (31%)
  Pallas kernels  19.6 us (18%)
  blocking collectives  13.3 us (12%)
  local copies, waits for them, and re-layouts  7.52 us (7%)
    ppermute x30, starting transfers between devices, shifted(): return lax.ppermute(x, 'tp', pairs)  36.5 us
    ppermute x30, waiting for transfers between devices, shifted(): return lax.ppermute(x, 'tp', pairs)  34.4 us
    pallas_call x12, Pallas kernels, call(): pl.pallas_call(kernel, out_shape=outs, in_specs=specs, out_specs=[VMEM] *...  19.6 us
    all_to_all x1, blocking collectives, body(): loads = lax.all_to_all(load, 'ctx', 0, 0, tiled=True)  13.3 us
    unnamed x15, local copies, waits for them, and re-layouts  6.79 us
  transfers between devices with their start and end apart: 30, of which 12 were waited for; matrix products, arithmetic and copies ran while one was open for 1% of the time, Pallas kernels for 9%

profile of v4, /device:TPU:1, one launch (start us, length us, event | category | flops | bytes accessed | tf_op | source)
XLA Modules:
  0.0 111.5 jit_solution(18077046389284563274)
XLA Ops:
  0.0 1.4 %collective-permute-start = (bf16[1024,256]{1,0:T(8,128)(2,1)}, bf16[1024,256]{1,0:T(8,128)(2,1)S(1)}, u32[]{:S(2)}, u32[]{:S(2)}) collective-permute-start(bf16[1024,256]{1,0:T(8,128)(2,1)} %refs_5_.1), channel_id=1, source_target_pairs={{0,1},{1,0},{2,3},{3,2},{4,5},{5,4},{6,7},{7,6},{8,9},{9,8},{10,11... | collective-permute-start | bytes 1572872 | tf_op jit(solution)/shard_map/ppermute | solution.py:400
  1.4 3.0 %collective-permute-start.2 = (bf16[1024,256]{1,0:T(8,128)(2,1)}, bf16[1024,256]{1,0:T(8,128)(2,1)S(1)}, u32[]{:S(2)}, u32[]{:S(2)}) collective-permute-start(bf16[1024,256]{1,0:T(8,128)(2,1)} %refs_5_.1), channel_id=1, source_target_pairs={{0,8},{1,9},{2,10},{3,11},{4,12},{5,13},{6,14},{7,15},{8,0},{9,1},... | collective-permute-start | bytes 1572872 | tf_op jit(solution)/shard_map/ppermute | solution.py:400
  4.4 3.6 %collective-permute-start.1 = (bf16[1024,256]{1,0:T(8,128)(2,1)}, bf16[1024,256]{1,0:T(8,128)(2,1)S(1)}, u32[]{:S(2)}, u32[]{:S(2)}) collective-permute-start(bf16[1024,256]{1,0:T(8,128)(2,1)} %refs_5_.1), channel_id=1, source_target_pairs={{0,2},{1,3},{2,0},{3,1},{4,6},{5,7},{6,4},{7,5},{8,10},{9,11},{10,... | collective-permute-start | bytes 1572872 | tf_op jit(solution)/shard_map/ppermute | solution.py:400
  8.4 2.3 %collective-permute-start.7 = (bf16[1024,256]{1,0:T(8,128)(2,1)}, bf16[1024,256]{1,0:T(8,128)(2,1)S(1)}, u32[]{:S(2)}, u32[]{:S(2)}) collective-permute-start(bf16[1024,256]{1,0:T(8,128)(2,1)} %refs_5_.1), channel_id=1, source_target_pairs={{0,12},{1,13},{2,14},{3,15},{4,0},{5,1},{6,2},{7,3},{8,4},{9,5},{1... | collective-permute-start | bytes 1572872 | tf_op jit(solution)/shard_map/ppermute | solution.py:400
  10.7 0.7 copy.17.refs_2_
  11.5 0.7 copy-done.3
  12.2 0.7 copy-done.4
  13.0 0.7 reshape.3.refs_0_
  13.7 2.8 %copy-done = bf16[4096,3,256]{2,0,1:T(8,128)(2,1)S(1)} copy-done((bf16[4096,3,256]{2,0,1:T(8,128)(2,1)S(1)}, bf16[4096,3,256]{2,0,1:T(8,128)(2,1)}, u32[]{:S(2)}) %copy-start) | copy-done | bytes 6291480
  16.5 1.0 copy-done.2
  17.6 1.0 shard_map.74
  18.6 1.8 %collective-permute-done.1.refs_2_ = bf16[1024,256]{1,0:T(8,128)(2,1)S(1)} collective-permute-done((bf16[1024,256]{1,0:T(8,128)(2,1)}, bf16[1024,256]{1,0:T(8,128)(2,1)S(1)}, u32[]{:S(2)}, u32[]{:S(2)}) %collective-permute-start.1) | collective-permute-done | bytes 524320 | tf_op jit(solution)/shard_map/ppermute | solution.py:400
  20.4 2.7 %collective-permute-start.5 = (bf16[1024,256]{1,0:T(8,128)(2,1)S(1)}, bf16[1024,256]{1,0:T(8,128)(2,1)S(1)}, u32[]{:S(2)}, u32[]{:S(2)}) collective-permute-start(bf16[1024,256]{1,0:T(8,128)(2,1)S(1)} %collective-permute-done.2.refs_3_), channel_id=1, source_target_pairs={{0,2},{1,3},{2,0},{3,1},{4,6},{5,7},{6,4},{7,5},{8,10},{9,11},{10,... | collective-permute-start | bytes 1572872 | tf_op jit(solution)/shard_map/ppermute | solution.py:400
  23.1 1.4 %collective-permute-start.4 = (bf16[1024,256]{1,0:T(8,128)(2,1)S(1)}, bf16[1024,256]{1,0:T(8,128)(2,1)S(1)}, u32[]{:S(2)}, u32[]{:S(2)}) collective-permute-start(bf16[1024,256]{1,0:T(8,128)(2,1)S(1)} %collective-permute-done.1.refs_2_), channel_id=1, source_target_pairs={{0,12},{1,13},{2,14},{3,15},{4,0},{5,1},{6,2},{7,3},{8,4},{9,5},{1... | collective-permute-start | bytes 1572872 | tf_op jit(solution)/shard_map/ppermute | solution.py:400
  24.5 3.8 %collective-permute-done.6.refs_4_ = bf16[1024,256]{1,0:T(8,128)(2,1)} collective-permute-done((bf16[1024,256]{1,0:T(8,128)(2,1)}, bf16[1024,256]{1,0:T(8,128)(2,1)}, u32[]{:S(2)}, u32[]{:S(2)}) %collective-permute-start.6) | collective-permute-done | bytes 524320 | tf_op jit(solution)/shard_map/ppermute | solution.py:400
  28.9 0.7 collective-permute-start.14
  29.6 3.1 %shard_map.75 = (f32[1024,768]{1,0:T(8,128)S(1)}, f32[1024,128]{1,0:T(8,128)S(1)}) custom-call(f32[16,256]{1,0:T(8,128)S(1)} %reshape.3.refs_0_, bf16[3,4096,256]{2,1,0:T(8,128)(2,1)S(1)} %bitcast.4, bf16[1024,256]{1,0:T(8,128)(2,1)S(1)} %collective-permute-done.1.refs_2_, ...), custom_call_target="tpu_custom_call", output_to_operand_aliasing={{0}: (6, {}), {1}: (7, {})} | custom-call | flops 1 | bytes 1 | tf_op jit(solution)/shard_map/pallas_call | solution.py:25
  32.7 1.9 %collective-permute-done.5.refs_2_ = bf16[1024,256]{1,0:T(8,128)(2,1)S(1)} collective-permute-done((bf16[1024,256]{1,0:T(8,128)(2,1)S(1)}, bf16[1024,256]{1,0:T(8,128)(2,1)S(1)}, u32[]{:S(2)}, u32[]{:S(2)}) %collective-permute-start.5) | collective-permute-done | bytes 524320 | tf_op jit(solution)/shard_map/ppermute | solution.py:400
  34.5 1.7 %collective-permute-start.11 = (bf16[1024,256]{1,0:T(8,128)(2,1)S(1)}, bf16[1024,256]{1,0:T(8,128)(2,1)S(1)}, u32[]{:S(2)}, u32[]{:S(2)}) collective-permute-start(bf16[1024,256]{1,0:T(8,128)(2,1)S(1)} %collective-permute-done.1.refs_2_), channel_id=1, source_target_pairs={{0,1},{1,0},{2,3},{3,2},{4,5},{5,4},{6,7},{7,6},{8,9},{9,8},{10,11... | collective-permute-start | bytes 1572872 | tf_op jit(solution)/shard_map/ppermute | solution.py:400
  36.2 3.4 %collective-permute-done.4.refs_4_ = bf16[1024,256]{1,0:T(8,128)(2,1)S(1)} collective-permute-done((bf16[1024,256]{1,0:T(8,128)(2,1)S(1)}, bf16[1024,256]{1,0:T(8,128)(2,1)S(1)}, u32[]{:S(2)}, u32[]{:S(2)}) %collective-permute-start.4) | collective-permute-done | bytes 524320 | tf_op jit(solution)/shard_map/ppermute | solution.py:400
  39.6 0.8 collective-permute-start.12
  40.4 0.5 collective-permute-start.9
  41.2 1.6 %shard_map.76 = (f32[1024,768]{1,0:T(8,128)S(1)}, f32[1024,128]{1,0:T(8,128)S(1)}) custom-call(f32[16,256]{1,0:T(8,128)S(1)} %reshape.3.refs_0_, bf16[3,4096,256]{2,1,0:T(8,128)(2,1)S(1)} %bitcast.5, bf16[1024,256]{1,0:T(8,128)(2,1)S(1)} %collective-permute-done.5.refs_2_, ...), custom_call_target="tpu_custom_call", output_to_operand_aliasing={{0}: (5, {}), {1}: (6, {})} | custom-call | flops 1 | bytes 1 | tf_op jit(solution)/shard_map/pallas_call | solution.py:25
  42.9 2.0 %shard_map.77 = (f32[1024,768]{1,0:T(8,128)S(1)}, f32[1024,128]{1,0:T(8,128)S(1)}) custom-call(f32[16,256]{1,0:T(8,128)S(1)} %reshape.3.refs_0_, bf16[3,4096,256]{2,1,0:T(8,128)(2,1)S(1)} %bitcast.6, bf16[1024,256]{1,0:T(8,128)(2,1)S(1)} %collective-permute-done.11.refs_2_, ...), custom_call_target="tpu_custom_call", output_to_operand_aliasing={{0}: (6, {}), {1}: (7, {})} | custom-call | flops 1 | bytes 1 | tf_op jit(solution)/shard_map/pallas_call | solution.py:25
  45.0 0.7 slice-done.1
  45.7 6.1 %shard_map.78 = (f32[1024,256]{1,0:T(8,128)S(1)}, f32[1024,256]{1,0:T(8,128)S(1)}, f32[128,256]{1,0:T(8,128)S(1)}, bf16[8,80,256]{2,1,0:T(8,128)(2,1)S(1)}) custom-call(f32[16,256]{1,0:T(8,128)S(1)} %reshape.3.refs_0_, bf16[3,4096,256]{2,1,0:T(8,128)(2,1)S(1)} %bitcast.9, bf16[1024,256]{1,0:T(8,128)(2,1)S(1)} %collective-permute-done.8.refs_2_, ...), custom_call_target="tpu_custom_call" | custom-call | flops 1 | bytes 1 | tf_op jit(solution)/shard_map/pallas_call | solution.py:25
  51.9 13.3 %all_to_all.5.refs_0_ = bf16[8,80,256]{2,1,0:T(8,128)(2,1)S(1)} all-to-all(bf16[8,80,256]{2,1,0:T(8,128)(2,1)S(1)} %get-tuple-element.51), channel_id=1, replica_groups=mesh['ctx'=8,'tp'=16] {'ctx'}, dimensions={0} | all-to-all | bytes 655360 | tf_op jit(solution)/shard_map/all_to_all | solution.py:483
  65.1 1.7 %shard_map.79.refs_1_ = bf16[1024,256]{1,0:T(8,128)(2,1)S(1)} custom-call(bf16[8,80,256]{2,1,0:T(8,128)(2,1)S(1)} %all_to_all.5.refs_0_, f32[1024,256]{1,0:T(8,128)S(1)} %get-tuple-element.52.refs_1_, f32[1024,256]{1,0:T(8,128)S(1)} %get-tuple-element.53.refs_2_, f32[128,256]{1,0:T(8,128)S(1)} %get-tuple-element.54.refs_3_, ...), custom_call_target="tpu_custom_call" | custom-call | flops 1 | bytes 1 | tf_op jit(solution)/shard_map/pallas_call | solution.py:25
  66.9 1.2 %collective-permute-start.15 = (bf16[1024,256]{1,0:T(8,128)(2,1)S(1)}, bf16[1024,256]{1,0:T(8,128)(2,1)S(1)}, u32[]{:S(2)}, u32[]{:S(2)}) collective-permute-start(bf16[1024,256]{1,0:T(8,128)(2,1)S(1)} %shard_map.79.refs_1_), channel_id=1, source_target_pairs={{0,1},{1,0},{2,3},{3,2},{4,5},{5,4},{6,7},{7,6},{8,9},{9,8},{10,11... | collective-permute-start | bytes 1572872 | tf_op jit(solution)/shard_map/ppermute | solution.py:400
  68.0 2.3 %collective-permute-start.17 = (bf16[1024,256]{1,0:T(8,128)(2,1)S(1)}, bf16[1024,256]{1,0:T(8,128)(2,1)S(1)}, u32[]{:S(2)}, u32[]{:S(2)}) collective-permute-start(bf16[1024,256]{1,0:T(8,128)(2,1)S(1)} %shard_map.79.refs_1_), channel_id=1, source_target_pairs={{0,8},{1,9},{2,10},{3,11},{4,12},{5,13},{6,14},{7,15},{8,0},{9,1},... | collective-permute-start | bytes 1572872 | tf_op jit(solution)/shard_map/ppermute | solution.py:400
  70.3 3.3 %collective-permute-start.16 = (bf16[1024,256]{1,0:T(8,128)(2,1)S(1)}, bf16[1024,256]{1,0:T(8,128)(2,1)S(1)}, u32[]{:S(2)}, u32[]{:S(2)}) collective-permute-start(bf16[1024,256]{1,0:T(8,128)(2,1)S(1)} %shard_map.79.refs_1_), channel_id=1, source_target_pairs={{0,2},{1,3},{2,0},{3,1},{4,6},{5,7},{6,4},{7,5},{8,10},{9,11},{10,... | collective-permute-start | bytes 1572872 | tf_op jit(solution)/shard_map/ppermute | solution.py:400
  73.6 1.6 %collective-permute-start.22 = (bf16[1024,256]{1,0:T(8,128)(2,1)S(1)}, bf16[1024,256]{1,0:T(8,128)(2,1)S(1)}, u32[]{:S(2)}, u32[]{:S(2)}) collective-permute-start(bf16[1024,256]{1,0:T(8,128)(2,1)S(1)} %shard_map.79.refs_1_), channel_id=1, source_target_pairs={{0,12},{1,13},{2,14},{3,15},{4,0},{5,1},{6,2},{7,3},{8,4},{9,5},{1... | collective-permute-start | bytes 1572872 | tf_op jit(solution)/shard_map/ppermute | solution.py:400
  75.7 7.4 %collective-permute-done.17.refs_2_ = bf16[1024,256]{1,0:T(8,128)(2,1)S(1)} collective-permute-done((bf16[1024,256]{1,0:T(8,128)(2,1)S(1)}, bf16[1024,256]{1,0:T(8,128)(2,1)S(1)}, u32[]{:S(2)}, u32[]{:S(2)}) %collective-permute-start.17) | collective-permute-done | bytes 524320 | tf_op jit(solution)/shard_map/ppermute | solution.py:400
  83.1 2.6 %collective-permute-done.16.refs_1_ = bf16[1024,256]{1,0:T(8,128)(2,1)S(1)} collective-permute-done((bf16[1024,256]{1,0:T(8,128)(2,1)S(1)}, bf16[1024,256]{1,0:T(8,128)(2,1)S(1)}, u32[]{:S(2)}, u32[]{:S(2)}) %collective-permute-start.16) | collective-permute-done | bytes 524320 | tf_op jit(solution)/shard_map/ppermute | solution.py:400
  85.6 2.6 %collective-permute-start.20 = (bf16[1024,256]{1,0:T(8,128)(2,1)S(1)}, bf16[1024,256]{1,0:T(8,128)(2,1)S(1)}, u32[]{:S(2)}, u32[]{:S(2)}) collective-permute-start(bf16[1024,256]{1,0:T(8,128)(2,1)S(1)} %collective-permute-done.17.refs_2_), channel_id=1, source_target_pairs={{0,2},{1,3},{2,0},{3,1},{4,6},{5,7},{6,4},{7,5},{8,10},{9,11},{10,... | collective-permute-start | bytes 1572872 | tf_op jit(solution)/shard_map/ppermute | solution.py:400
  88.3 1.6 %collective-permute-start.19 = (bf16[1024,256]{1,0:T(8,128)(2,1)S(1)}, bf16[1024,256]{1,0:T(8,128)(2,1)S(1)}, u32[]{:S(2)}, u32[]{:S(2)}) collective-permute-start(bf16[1024,256]{1,0:T(8,128)(2,1)S(1)} %collective-permute-done.16.refs_1_), channel_id=1, source_target_pairs={{0,12},{1,13},{2,14},{3,15},{4,0},{5,1},{6,2},{7,3},{8,4},{9,5},{1... | collective-permute-start | bytes 1572872 | tf_op jit(solution)/shard_map/ppermute | solution.py:400
  89.9 4.4 %collective-permute-done.22.refs_4_ = bf16[1024,256]{1,0:T(8,128)(2,1)S(1)} collective-permute-done((bf16[1024,256]{1,0:T(8,128)(2,1)S(1)}, bf16[1024,256]{1,0:T(8,128)(2,1)S(1)}, u32[]{:S(2)}, u32[]{:S(2)}) %collective-permute-start.22) | collective-permute-done | bytes 524320 | tf_op jit(solution)/shard_map/ppermute | solution.py:400
  94.2 1.3 %collective-permute-start.29 = (bf16[1024,256]{1,0:T(8,128)(2,1)S(1)}, bf16[1024,256]{1,0:T(8,128)(2,1)S(1)}, u32[]{:S(2)}, u32[]{:S(2)}) collective-permute-start(bf16[1024,256]{1,0:T(8,128)(2,1)S(1)} %collective-permute-done.22.refs_4_), channel_id=1, source_target_pairs={{0,1},{1,0},{2,3},{3,2},{4,5},{5,4},{6,7},{7,6},{8,9},{9,8},{10,11... | collective-permute-start | bytes 1572872 | tf_op jit(solution)/shard_map/ppermute | solution.py:400
  95.6 0.7 shard_map.81.refs_4_
  96.3 3.3 %collective-permute-done.20.refs_1_ = bf16[1024,256]{1,0:T(8,128)(2,1)S(1)} collective-permute-done((bf16[1024,256]{1,0:T(8,128)(2,1)S(1)}, bf16[1024,256]{1,0:T(8,128)(2,1)S(1)}, u32[]{:S(2)}, u32[]{:S(2)}) %collective-permute-start.20) | collective-permute-done | bytes 524320 | tf_op jit(solution)/shard_map/ppermute | solution.py:400
  99.7 1.8 %collective-permute-start.26 = (bf16[1024,256]{1,0:T(8,128)(2,1)S(1)}, bf16[1024,256]{1,0:T(8,128)(2,1)S(1)}, u32[]{:S(2)}, u32[]{:S(2)}) collective-permute-start(bf16[1024,256]{1,0:T(8,128)(2,1)S(1)} %collective-permute-done.16.refs_1_), channel_id=1, source_target_pairs={{0,1},{1,0},{2,3},{3,2},{4,5},{5,4},{6,7},{7,6},{8,9},{9,8},{10,11... | collective-permute-start | bytes 1572872 | tf_op jit(solution)/shard_map/ppermute | solution.py:400
  101.5 4.0 %collective-permute-done.19.refs_3_ = bf16[1024,256]{1,0:T(8,128)(2,1)S(1)} collective-permute-done((bf16[1024,256]{1,0:T(8,128)(2,1)S(1)}, bf16[1024,256]{1,0:T(8,128)(2,1)S(1)}, u32[]{:S(2)}, u32[]{:S(2)}) %collective-permute-start.19) | collective-permute-done | bytes 524320 | tf_op jit(solution)/shard_map/ppermute | solution.py:400
  105.5 0.9 collective-permute-start.27
  107.0 0.6 shard_map.82.refs_5_
  107.9 0.7 shard_map.83.refs_4_
  108.6 0.7 collective-permute-done.24.refs_2_
  109.4 0.7 collective-permute-done.25.refs_3_
  110.1 1.4 %shard_map.84 = bf16[1024,256]{1,0:T(8,128)(2,1)} custom-call(bf16[4096,256]{1,0:T(8,128)(2,1)S(1)} %copy-done.1, bf16[1024,256]{1,0:T(8,128)(2,1)S(1)} %collective-permute-done.23.refs_1_, bf16[1024,256]{1,0:T(8,128)(2,1)S(1)} %collective-permute-done.24.refs_2_, bf16[1024,256]{1,0:T(8,128)(2,1)S(1)} %collective-permute-done.25.refs_3_, ...), custom_call_target="tpu_custom_call" | custom-call | flops 1 | bytes 1 | tf_op jit(solution)/shard_map/pallas_call | solution.py:25
  (42 shorter events, 2.9 us)
Async XLA Ops:
  0.0 4.4 %collective-permute-start = (bf16[1024,256]{1,0:T(8,128)(2,1)}, bf16[1024,256]{1,0:T(8,128)(2,1)S(1)}, u32[]{:S(2)}, u32[]{:S(2)}) collective-permute-start(bf16[1024,256]{1,0:T(8,128)(2,1)} %refs_5_.1), channel_id=1, source_target_pairs={{0,1},{1,0},{2,3},{3,2},{4,5},{5,4},{6,7},{7,6},{8,9},{9,8},{10,11... | collective-permute-start | bytes 1572872 | tf_op jit(solution)/shard_map/ppermute | solution.py:400
  1.4 17.2 %collective-permute-start.2 = (bf16[1024,256]{1,0:T(8,128)(2,1)}, bf16[1024,256]{1,0:T(8,128)(2,1)S(1)}, u32[]{:S(2)}, u32[]{:S(2)}) collective-permute-start(bf16[1024,256]{1,0:T(8,128)(2,1)} %refs_5_.1), channel_id=1, source_target_pairs={{0,8},{1,9},{2,10},{3,11},{4,12},{5,13},{6,14},{7,15},{8,0},{9,1},... | collective-permute-start | bytes 1572872 | tf_op jit(solution)/shard_map/ppermute | solution.py:400
  4.4 15.9 %collective-permute-start.1 = (bf16[1024,256]{1,0:T(8,128)(2,1)}, bf16[1024,256]{1,0:T(8,128)(2,1)S(1)}, u32[]{:S(2)}, u32[]{:S(2)}) collective-permute-start(bf16[1024,256]{1,0:T(8,128)(2,1)} %refs_5_.1), channel_id=1, source_target_pairs={{0,2},{1,3},{2,0},{3,1},{4,6},{5,7},{6,4},{7,5},{8,10},{9,11},{10,... | collective-permute-start | bytes 1572872 | tf_op jit(solution)/shard_map/ppermute | solution.py:400
  8.0 20.3 %collective-permute-start.6 = (bf16[1024,256]{1,0:T(8,128)(2,1)}, bf16[1024,256]{1,0:T(8,128)(2,1)}, u32[]{:S(2)}, u32[]{:S(2)}) collective-permute-start(bf16[1024,256]{1,0:T(8,128)(2,1)} %refs_5_.1), channel_id=1, source_target_pairs={{0,4},{1,5},{2,6},{3,7},{4,8},{5,9},{6,10},{7,11},{8,12},{9,13},{1... | collective-permute-start | bytes 1572872 | tf_op jit(solution)/shard_map/ppermute | solution.py:400
  8.4 20.4 %collective-permute-start.7 = (bf16[1024,256]{1,0:T(8,128)(2,1)}, bf16[1024,256]{1,0:T(8,128)(2,1)S(1)}, u32[]{:S(2)}, u32[]{:S(2)}) collective-permute-start(bf16[1024,256]{1,0:T(8,128)(2,1)} %refs_5_.1), channel_id=1, source_target_pairs={{0,12},{1,13},{2,14},{3,15},{4,0},{5,1},{6,2},{7,3},{8,4},{9,5},{1... | collective-permute-start | bytes 1572872 | tf_op jit(solution)/shard_map/ppermute | solution.py:400
  11.5 0.7 copy-start.3
  12.2 0.7 copy-start.4
  13.7 2.8 %copy-start = (bf16[4096,3,256]{2,0,1:T(8,128)(2,1)S(1)}, bf16[4096,3,256]{2,0,1:T(8,128)(2,1)}, u32[]{:S(2)}) copy-start(bf16[4096,3,256]{2,0,1:T(8,128)(2,1)} %param.9) | copy-start | bytes 18874372
  16.5 1.0 copy-start.2
  20.4 14.2 %collective-permute-start.5 = (bf16[1024,256]{1,0:T(8,128)(2,1)S(1)}, bf16[1024,256]{1,0:T(8,128)(2,1)S(1)}, u32[]{:S(2)}, u32[]{:S(2)}) collective-permute-start(bf16[1024,256]{1,0:T(8,128)(2,1)S(1)} %collective-permute-done.2.refs_3_), channel_id=1, source_target_pairs={{0,2},{1,3},{2,0},{3,1},{4,6},{5,7},{6,4},{7,5},{8,10},{9,11},{10,... | collective-permute-start | bytes 1572872 | tf_op jit(solution)/shard_map/ppermute | solution.py:400
  23.1 16.6 %collective-permute-start.4 = (bf16[1024,256]{1,0:T(8,128)(2,1)S(1)}, bf16[1024,256]{1,0:T(8,128)(2,1)S(1)}, u32[]{:S(2)}, u32[]{:S(2)}) collective-permute-start(bf16[1024,256]{1,0:T(8,128)(2,1)S(1)} %collective-permute-done.1.refs_2_), channel_id=1, source_target_pairs={{0,12},{1,13},{2,14},{3,15},{4,0},{5,1},{6,2},{7,3},{8,4},{9,5},{1... | collective-permute-start | bytes 1572872 | tf_op jit(solution)/shard_map/ppermute | solution.py:400
  24.4 16.0 %collective-permute-start.3 = (bf16[1024,256]{1,0:T(8,128)(2,1)S(1)}, bf16[1024,256]{1,0:T(8,128)(2,1)S(1)}, u32[]{:S(2)}, u32[]{:S(2)}) collective-permute-start(bf16[1024,256]{1,0:T(8,128)(2,1)S(1)} %collective-permute-done.1.refs_2_), channel_id=1, source_target_pairs={{0,4},{1,5},{2,6},{3,7},{4,8},{5,9},{6,10},{7,11},{8,12},{9,13},{1... | collective-permute-start | bytes 1572872 | tf_op jit(solution)/shard_map/ppermute | solution.py:400
  28.4 12.1 %collective-permute-start.13 = (bf16[1024,256]{1,0:T(8,128)(2,1)}, bf16[1024,256]{1,0:T(8,128)(2,1)S(1)}, u32[]{:S(2)}, u32[]{:S(2)}) collective-permute-start(bf16[1024,256]{1,0:T(8,128)(2,1)} %collective-permute-done.6.refs_4_), channel_id=1, source_target_pairs={{0,1},{1,0},{2,3},{3,2},{4,5},{5,4},{6,7},{7,6},{8,9},{9,8},{10,11... | collective-permute-start | bytes 1572872 | tf_op jit(solution)/shard_map/ppermute | solution.py:400
  28.9 12.1 %collective-permute-start.14 = (bf16[1024,256]{1,0:T(8,128)(2,1)S(1)}, bf16[1024,256]{1,0:T(8,128)(2,1)S(1)}, u32[]{:S(2)}, u32[]{:S(2)}) collective-permute-start(bf16[1024,256]{1,0:T(8,128)(2,1)S(1)} %collective-permute-done.7.refs_5_), channel_id=1, source_target_pairs={{0,1},{1,0},{2,3},{3,2},{4,5},{5,4},{6,7},{7,6},{8,9},{9,8},{10,11... | collective-permute-start | bytes 1572872 | tf_op jit(solution)/shard_map/ppermute | solution.py:400
  34.5 8.3 %collective-permute-start.11 = (bf16[1024,256]{1,0:T(8,128)(2,1)S(1)}, bf16[1024,256]{1,0:T(8,128)(2,1)S(1)}, u32[]{:S(2)}, u32[]{:S(2)}) collective-permute-start(bf16[1024,256]{1,0:T(8,128)(2,1)S(1)} %collective-permute-done.1.refs_2_), channel_id=1, source_target_pairs={{0,1},{1,0},{2,3},{3,2},{4,5},{5,4},{6,7},{7,6},{8,9},{9,8},{10,11... | collective-permute-start | bytes 1572872 | tf_op jit(solution)/shard_map/ppermute | solution.py:400
  39.6 3.2 %collective-permute-start.12 = (bf16[1024,256]{1,0:T(8,128)(2,1)S(1)}, bf16[1024,256]{1,0:T(8,128)(2,1)S(1)}, u32[]{:S(2)}, u32[]{:S(2)}) collective-permute-start(bf16[1024,256]{1,0:T(8,128)(2,1)S(1)} %collective-permute-done.2.refs_3_), channel_id=1, source_target_pairs={{0,1},{1,0},{2,3},{3,2},{4,5},{5,4},{6,7},{7,6},{8,9},{9,8},{10,11... | collective-permute-start | bytes 1572872 | tf_op jit(solution)/shard_map/ppermute | solution.py:400
  40.4 4.5 %collective-permute-start.8 = (bf16[1024,256]{1,0:T(8,128)(2,1)S(1)}, bf16[1024,256]{1,0:T(8,128)(2,1)S(1)}, u32[]{:S(2)}, u32[]{:S(2)}) collective-permute-start(bf16[1024,256]{1,0:T(8,128)(2,1)S(1)} %collective-permute-done.5.refs_2_), channel_id=1, source_target_pairs={{0,1},{1,0},{2,3},{3,2},{4,5},{5,4},{6,7},{7,6},{8,9},{9,8},{10,11... | collective-permute-start | bytes 1572872 | tf_op jit(solution)/shard_map/ppermute | solution.py:400
  40.4 4.5 %collective-permute-start.9 = (bf16[1024,256]{1,0:T(8,128)(2,1)S(1)}, bf16[1024,256]{1,0:T(8,128)(2,1)S(1)}, u32[]{:S(2)}, u32[]{:S(2)}) collective-permute-start(bf16[1024,256]{1,0:T(8,128)(2,1)S(1)} %collective-permute-done.3.refs_3_), channel_id=1, source_target_pairs={{0,1},{1,0},{2,3},{3,2},{4,5},{5,4},{6,7},{7,6},{8,9},{9,8},{10,11... | collective-permute-start | bytes 1572872 | tf_op jit(solution)/shard_map/ppermute | solution.py:400
  40.9 4.0 %collective-permute-start.10 = (bf16[1024,256]{1,0:T(8,128)(2,1)S(1)}, bf16[1024,256]{1,0:T(8,128)(2,1)S(1)}, u32[]{:S(2)}, u32[]{:S(2)}) collective-permute-start(bf16[1024,256]{1,0:T(8,128)(2,1)S(1)} %collective-permute-done.4.refs_4_), channel_id=1, source_target_pairs={{0,1},{1,0},{2,3},{3,2},{4,5},{5,4},{6,7},{7,6},{8,9},{9,8},{10,11... | collective-permute-start | bytes 1572872 | tf_op jit(solution)/shard_map/ppermute | solution.py:400
  42.9 2.2 %slice-start = ((s8[6291456]{0:T(1024)(128)(4,1)}), s8[4194304]{0:T(1024)(128)(4,1)S(1)}, s32[]{:S(2)}) async-start(s8[6291456]{0:T(1024)(128)(4,1)} %bitcast.7), calls=%async_computation.1 | async-start | bytes 8388608
  42.9 2.9 %slice-start.1 = ((s8[6291456]{0:T(1024)(128)(4,1)}), s8[2097152]{0:T(1024)(128)(4,1)S(1)}, s32[]{:S(2)}) async-start(s8[6291456]{0:T(1024)(128)(4,1)} %bitcast.7), calls=%async_computation.2 | async-start | bytes 4194304
  51.9 23.4 %copy-start.1 = (bf16[4096,256]{1,0:T(8,128)(2,1)S(1)}, bf16[4096,256]{1,0:T(8,128)(2,1)}, u32[]{:S(2)}) copy-start(bf16[4096,256]{1,0:T(8,128)(2,1)} %refs_0_.9) | copy-start | bytes 6291460
  66.9 3.4 %collective-permute-start.15 = (bf16[1024,256]{1,0:T(8,128)(2,1)S(1)}, bf16[1024,256]{1,0:T(8,128)(2,1)S(1)}, u32[]{:S(2)}, u32[]{:S(2)}) collective-permute-start(bf16[1024,256]{1,0:T(8,128)(2,1)S(1)} %shard_map.79.refs_1_), channel_id=1, source_target_pairs={{0,1},{1,0},{2,3},{3,2},{4,5},{5,4},{6,7},{7,6},{8,9},{9,8},{10,11... | collective-permute-start | bytes 1572872 | tf_op jit(solution)/shard_map/ppermute | solution.py:400
  68.0 15.0 %collective-permute-start.17 = (bf16[1024,256]{1,0:T(8,128)(2,1)S(1)}, bf16[1024,256]{1,0:T(8,128)(2,1)S(1)}, u32[]{:S(2)}, u32[]{:S(2)}) collective-permute-start(bf16[1024,256]{1,0:T(8,128)(2,1)S(1)} %shard_map.79.refs_1_), channel_id=1, source_target_pairs={{0,8},{1,9},{2,10},{3,11},{4,12},{5,13},{6,14},{7,15},{8,0},{9,1},... | collective-permute-start | bytes 1572872 | tf_op jit(solution)/shard_map/ppermute | solution.py:400
  70.3 15.3 %collective-permute-start.16 = (bf16[1024,256]{1,0:T(8,128)(2,1)S(1)}, bf16[1024,256]{1,0:T(8,128)(2,1)S(1)}, u32[]{:S(2)}, u32[]{:S(2)}) collective-permute-start(bf16[1024,256]{1,0:T(8,128)(2,1)S(1)} %shard_map.79.refs_1_), channel_id=1, source_target_pairs={{0,2},{1,3},{2,0},{3,1},{4,6},{5,7},{6,4},{7,5},{8,10},{9,11},{10,... | collective-permute-start | bytes 1572872 | tf_op jit(solution)/shard_map/ppermute | solution.py:400
  73.6 20.6 %collective-permute-start.22 = (bf16[1024,256]{1,0:T(8,128)(2,1)S(1)}, bf16[1024,256]{1,0:T(8,128)(2,1)S(1)}, u32[]{:S(2)}, u32[]{:S(2)}) collective-permute-start(bf16[1024,256]{1,0:T(8,128)(2,1)S(1)} %shard_map.79.refs_1_), channel_id=1, source_target_pairs={{0,12},{1,13},{2,14},{3,15},{4,0},{5,1},{6,2},{7,3},{8,4},{9,5},{1... | collective-permute-start | bytes 1572872 | tf_op jit(solution)/shard_map/ppermute | solution.py:400
  75.2 20.4 %collective-permute-start.21 = (bf16[1024,256]{1,0:T(8,128)(2,1)S(1)}, bf16[1024,256]{1,0:T(8,128)(2,1)S(1)}, u32[]{:S(2)}, u32[]{:S(2)}) collective-permute-start(bf16[1024,256]{1,0:T(8,128)(2,1)S(1)} %shard_map.79.refs_1_), channel_id=1, source_target_pairs={{0,4},{1,5},{2,6},{3,7},{4,8},{5,9},{6,10},{7,11},{8,12},{9,13},{1... | collective-permute-start | bytes 1572872 | tf_op jit(solution)/shard_map/ppermute | solution.py:400
  85.6 14.1 %collective-permute-start.20 = (bf16[1024,256]{1,0:T(8,128)(2,1)S(1)}, bf16[1024,256]{1,0:T(8,128)(2,1)S(1)}, u32[]{:S(2)}, u32[]{:S(2)}) collective-permute-start(bf16[1024,256]{1,0:T(8,128)(2,1)S(1)} %collective-permute-done.17.refs_2_), channel_id=1, source_target_pairs={{0,2},{1,3},{2,0},{3,1},{4,6},{5,7},{6,4},{7,5},{8,10},{9,11},{10,... | collective-permute-start | bytes 1572872 | tf_op jit(solution)/shard_map/ppermute | solution.py:400
  88.3 17.2 %collective-permute-start.19 = (bf16[1024,256]{1,0:T(8,128)(2,1)S(1)}, bf16[1024,256]{1,0:T(8,128)(2,1)S(1)}, u32[]{:S(2)}, u32[]{:S(2)}) collective-permute-start(bf16[1024,256]{1,0:T(8,128)(2,1)S(1)} %collective-permute-done.16.refs_1_), channel_id=1, source_target_pairs={{0,12},{1,13},{2,14},{3,15},{4,0},{5,1},{6,2},{7,3},{8,4},{9,5},{1... | collective-permute-start | bytes 1572872 | tf_op jit(solution)/shard_map/ppermute | solution.py:400
  89.9 16.5 %collective-permute-start.18 = (bf16[1024,256]{1,0:T(8,128)(2,1)S(1)}, bf16[1024,256]{1,0:T(8,128)(2,1)S(1)}, u32[]{:S(2)}, u32[]{:S(2)}) collective-permute-start(bf16[1024,256]{1,0:T(8,128)(2,1)S(1)} %collective-permute-done.16.refs_1_), channel_id=1, source_target_pairs={{0,4},{1,5},{2,6},{3,7},{4,8},{5,9},{6,10},{7,11},{8,12},{9,13},{1... | collective-permute-start | bytes 1572872 | tf_op jit(solution)/shard_map/ppermute | solution.py:400
  94.2 12.1 %collective-permute-start.29 = (bf16[1024,256]{1,0:T(8,128)(2,1)S(1)}, bf16[1024,256]{1,0:T(8,128)(2,1)S(1)}, u32[]{:S(2)}, u32[]{:S(2)}) collective-permute-start(bf16[1024,256]{1,0:T(8,128)(2,1)S(1)} %collective-permute-done.22.refs_4_), channel_id=1, source_target_pairs={{0,1},{1,0},{2,3},{3,2},{4,5},{5,4},{6,7},{7,6},{8,9},{9,8},{10,11... | collective-permute-start | bytes 1572872 | tf_op jit(solution)/shard_map/ppermute | solution.py:400
  95.6 11.3 %collective-permute-start.28 = (bf16[1024,256]{1,0:T(8,128)(2,1)S(1)}, bf16[1024,256]{1,0:T(8,128)(2,1)S(1)}, u32[]{:S(2)}, u32[]{:S(2)}) collective-permute-start(bf16[1024,256]{1,0:T(8,128)(2,1)S(1)} %collective-permute-done.21.refs_3_), channel_id=1, source_target_pairs={{0,1},{1,0},{2,3},{3,2},{4,5},{5,4},{6,7},{7,6},{8,9},{9,8},{10,11... | collective-permute-start | bytes 1572872 | tf_op jit(solution)/shard_map/ppermute | solution.py:400
  99.7 7.9 %collective-permute-start.26 = (bf16[1024,256]{1,0:T(8,128)(2,1)S(1)}, bf16[1024,256]{1,0:T(8,128)(2,1)S(1)}, u32[]{:S(2)}, u32[]{:S(2)}) collective-permute-start(bf16[1024,256]{1,0:T(8,128)(2,1)S(1)} %collective-permute-done.16.refs_1_), channel_id=1, source_target_pairs={{0,1},{1,0},{2,3},{3,2},{4,5},{5,4},{6,7},{7,6},{8,9},{9,8},{10,11... | collective-permute-start | bytes 1572872 | tf_op jit(solution)/shard_map/ppermute | solution.py:400
  105.5 2.4 %collective-permute-start.27 = (bf16[1024,256]{1,0:T(8,128)(2,1)S(1)}, bf16[1024,256]{1,0:T(8,128)(2,1)S(1)}, u32[]{:S(2)}, u32[]{:S(2)}) collective-permute-start(bf16[1024,256]{1,0:T(8,128)(2,1)S(1)} %collective-permute-done.17.refs_2_), channel_id=1, source_target_pairs={{0,1},{1,0},{2,3},{3,2},{4,5},{5,4},{6,7},{7,6},{8,9},{9,8},{10,11... | collective-permute-start | bytes 1572872 | tf_op jit(solution)/shard_map/ppermute | solution.py:400
  106.4 2.3 %collective-permute-start.23 = (bf16[1024,256]{1,0:T(8,128)(2,1)S(1)}, bf16[1024,256]{1,0:T(8,128)(2,1)S(1)}, u32[]{:S(2)}, u32[]{:S(2)}) collective-permute-start(bf16[1024,256]{1,0:T(8,128)(2,1)S(1)} %collective-permute-done.20.refs_1_), channel_id=1, source_target_pairs={{0,1},{1,0},{2,3},{3,2},{4,5},{5,4},{6,7},{7,6},{8,9},{9,8},{10,11... | collective-permute-start | bytes 1572872 | tf_op jit(solution)/shard_map/ppermute | solution.py:400
  106.4 3.0 %collective-permute-start.24 = (bf16[1024,256]{1,0:T(8,128)(2,1)S(1)}, bf16[1024,256]{1,0:T(8,128)(2,1)S(1)}, u32[]{:S(2)}, u32[]{:S(2)}) collective-permute-start(bf16[1024,256]{1,0:T(8,128)(2,1)S(1)} %collective-permute-done.18.refs_2_), channel_id=1, source_target_pairs={{0,1},{1,0},{2,3},{3,2},{4,5},{5,4},{6,7},{7,6},{8,9},{9,8},{10,11... | collective-permute-start | bytes 1572872 | tf_op jit(solution)/shard_map/ppermute | solution.py:400
  106.9 3.3 %collective-permute-start.25 = (bf16[1024,256]{1,0:T(8,128)(2,1)S(1)}, bf16[1024,256]{1,0:T(8,128)(2,1)S(1)}, u32[]{:S(2)}, u32[]{:S(2)}) collective-permute-start(bf16[1024,256]{1,0:T(8,128)(2,1)S(1)} %collective-permute-done.19.refs_3_), channel_id=1, source_target_pairs={{0,1},{1,0},{2,3},{3,2},{4,5},{5,4},{6,7},{7,6},{8,9},{9,8},{10,11... | collective-permute-start | bytes 1572872 | tf_op jit(solution)/shard_map/ppermute | solution.py:400

commit v5 on v4

--- a/solution.py
+++ b/solution.py
@@ -413,29 +413,31 @@
         return shifted(tie(p, *after) if after else p, 0, 0, 1)
 
     def gather(x, start, add):
+        up = shifted(x, 0, 1, 0)
         far = shifted(x, 2, 0, 0)
         left = shifted(x, 1, 0, 0)
         right = shifted(x, -1, 0, 0)
         x_other = other(x)
-        up = shifted(tie(x, x_other), 0, 1, 0)
         if start is not None:
             x_other = tie(x_other, start)
         state, mark = add([(x, 0, (0, 0, 0)), (x_other, 0, (0, 0, 1))], None)
-        up, far, mark = lax.optimization_barrier((up, far, mark))
+        far, mark = lax.optimization_barrier((far, mark))
+        up, far = lax.optimization_barrier((up, far))
         up_left = shifted(up, 1, 0, 0)
         up_right = shifted(up, -1, 0, 0)
         up_far = shifted(far, 0, 1, 0)
-        up_other, far_other = other(up, left, right), other(far, left, right)
-        left_other, right_other = other(left), other(right)
-        pieces = [(up, 0, (0, 1, 0)), (far, 0, (2, 0, 0)), (left, 0, (-1, 0, 0)), (right, 0, (1, 0, 0))]
+        pair = jnp.concatenate([up, far], axis=0)
+        sides = jnp.concatenate([left, right], axis=0)
+        pair_other, sides_other = other(pair, sides), other(sides)
+        pieces = [(pair, 0, (0, 1, 0)), (pair, length, (2, 0, 0))]
+        pieces += [(sides, 0, (-1, 0, 0)), (sides, length, (1, 0, 0))]
         state, mark = add(pieces, state)
+        others = [(pair_other, 0, (0, 1, 1)), (pair_other, length, (2, 0, 1))]
+        others += [(sides_other, 0, (-1, 0, 1)), (sides_other, length, (1, 0, 1))]
         up_left, up_right, up_far, mark = lax.optimization_barrier((up_left, up_right, up_far, mark))
         up_far_other, up_left_other, up_right_other = other(up_far), other(up_left), other(up_right)
         pieces = [(up_far, 0, (2, 1, 0)), (up_left, 0, (-1, 1, 0)), (up_right, 0, (1, 1, 0))]
-        state, mark = add(pieces, state)
-        pieces = [(up_other, 0, (0, 1, 1)), (far_other, 0, (2, 0, 1))]
-        pieces += [(left_other, 0, (-1, 0, 1)), (right_other, 0, (1, 0, 1))]
-        state, mark = add(pieces, state)
+        state, mark = add(others + pieces, state)
         pieces = [(up_far_other, 0, (2, 1, 1)), (up_left_other, 0, (-1, 1, 1))]
         return pieces + [(up_right_other, 0, (1, 1, 1))], state
 

time: 112 us -> 110 us (0.982)
  Pallas kernels: 19.6 us -> 17.9 us
  starting transfers between devices: 36.5 us -> 34.9 us
    pallas_call x12 -> x10, Pallas kernels: 19.6 us -> 17.9 us  [call(): pl.pallas_call(kernel, out_shape=outs, in_specs=specs, out_specs=[VMEM] *...]
    ppermute x30 -> x26, starting transfers between devices: 36.5 us -> 34.9 us  [shifted(): return lax.ppermute(x, 'tp', pairs)]
    ppermute x30 -> x26, waiting for transfers between devices: 34.4 us -> 34.9 us  [shifted(): return lax.ppermute(x, 'tp', pairs)]
    unnamed x15 -> x19, local copies, waits for them, and re-layouts: 6.79 us -> 7.19 us
  transfers between devices with their start and end apart: 30 -> 26, of which waited for: 12 -> 10; matrix products, arithmetic and copies ran while one was open for 1% -> 3% of each run, Pallas kernels for 9% -> 8%
where the time goes in v5:
time: 110 us; the launch traced here: 109 us
  starting transfers between devices  34.9 us (32%)
  waiting for transfers between devices  34.9 us (32%)
  Pallas kernels  17.9 us (16%)
  blocking collectives  13.3 us (12%)
  local copies, waits for them, and re-layouts  8.07 us (7%)
    ppermute x26, starting transfers between devices, shifted(): return lax.ppermute(x, 'tp', pairs)  34.9 us
    ppermute x26, waiting for transfers between devices, shifted(): return lax.ppermute(x, 'tp', pairs)  34.9 us
    pallas_call x10, Pallas kernels, call(): pl.pallas_call(kernel, out_shape=outs, in_specs=specs, out_specs=[VMEM] *...  17.9 us
    all_to_all x1, blocking collectives, body(): loads = lax.all_to_all(load, 'ctx', 0, 0, tiled=True)  13.3 us
    unnamed x19, local copies, waits for them, and re-layouts  7.19 us
  transfers between devices with their start and end apart: 26, of which 10 were waited for; matrix products, arithmetic and copies ran while one was open for 3% of the time, Pallas kernels for 8%

profile of v5, /device:TPU:1, one launch (start us, length us, event | category | flops | bytes accessed | tf_op | source)
XLA Modules:
  0.0 109.3 jit_solution(8790867456486914516)
XLA Ops:
  0.0 1.4 %collective-permute-start.2 = (bf16[1024,256]{1,0:T(8,128)(2,1)}, bf16[1024,256]{1,0:T(8,128)(2,1)S(1)}, u32[]{:S(2)}, u32[]{:S(2)}) collective-permute-start(bf16[1024,256]{1,0:T(8,128)(2,1)} %refs_5_.1), channel_id=1, source_target_pairs={{0,1},{1,0},{2,3},{3,2},{4,5},{5,4},{6,7},{7,6},{8,9},{9,8},{10,11... | collective-permute-start | bytes 1572872 | tf_op jit(solution)/shard_map/ppermute | solution.py:400
  1.4 3.0 %collective-permute-start.1 = (bf16[1024,256]{1,0:T(8,128)(2,1)}, bf16[1024,256]{1,0:T(8,128)(2,1)S(1)}, u32[]{:S(2)}, u32[]{:S(2)}) collective-permute-start(bf16[1024,256]{1,0:T(8,128)(2,1)} %refs_5_.1), channel_id=1, source_target_pairs={{0,8},{1,9},{2,10},{3,11},{4,12},{5,13},{6,14},{7,15},{8,0},{9,1},... | collective-permute-start | bytes 1572872 | tf_op jit(solution)/shard_map/ppermute | solution.py:400
  4.4 3.6 %collective-permute-start = (bf16[1024,256]{1,0:T(8,128)(2,1)}, bf16[1024,256]{1,0:T(8,128)(2,1)S(1)}, u32[]{:S(2)}, u32[]{:S(2)}) collective-permute-start(bf16[1024,256]{1,0:T(8,128)(2,1)} %refs_5_.1), channel_id=1, source_target_pairs={{0,2},{1,3},{2,0},{3,1},{4,6},{5,7},{6,4},{7,5},{8,10},{9,11},{10,... | collective-permute-start | bytes 1572872 | tf_op jit(solution)/shard_map/ppermute | solution.py:400
  8.0 0.4 collective-permute-start.6
  8.4 2.3 %collective-permute-start.7 = (bf16[1024,256]{1,0:T(8,128)(2,1)}, bf16[1024,256]{1,0:T(8,128)(2,1)S(1)}, u32[]{:S(2)}, u32[]{:S(2)}) collective-permute-start(bf16[1024,256]{1,0:T(8,128)(2,1)} %refs_5_.1), channel_id=1, source_target_pairs={{0,12},{1,13},{2,14},{3,15},{4,0},{5,1},{6,2},{7,3},{8,4},{9,5},{1... | collective-permute-start | bytes 1572872 | tf_op jit(solution)/shard_map/ppermute | solution.py:400
  10.7 0.7 copy.14.refs_2_
  11.5 0.7 copy-done.3
  12.2 0.7 copy-done.4
  13.0 0.7 reshape.3.refs_0_
  13.7 2.8 %copy-done = bf16[4096,3,256]{2,0,1:T(8,128)(2,1)S(1)} copy-done((bf16[4096,3,256]{2,0,1:T(8,128)(2,1)S(1)}, bf16[4096,3,256]{2,0,1:T(8,128)(2,1)}, u32[]{:S(2)}) %copy-start) | copy-done | bytes 6291480
  16.5 1.0 copy-done.2
  17.6 1.0 shard_map.74
  18.6 1.8 %collective-permute-done = bf16[1024,256]{1,0:T(8,128)(2,1)S(1)} collective-permute-done((bf16[1024,256]{1,0:T(8,128)(2,1)}, bf16[1024,256]{1,0:T(8,128)(2,1)S(1)}, u32[]{:S(2)}, u32[]{:S(2)}) %collective-permute-start) | collective-permute-done | bytes 524320 | tf_op jit(solution)/shard_map/ppermute | solution.py:400
  20.4 0.4 collective-permute-start.3
  20.8 2.3 %collective-permute-start.4 = (bf16[1024,256]{1,0:T(8,128)(2,1)S(1)}, bf16[1024,256]{1,0:T(8,128)(2,1)S(1)}, u32[]{:S(2)}, u32[]{:S(2)}) collective-permute-start(bf16[1024,256]{1,0:T(8,128)(2,1)S(1)} %collective-permute-done), channel_id=1, source_target_pairs={{0,12},{1,13},{2,14},{3,15},{4,0},{5,1},{6,2},{7,3},{8,4},{9,5},{1... | collective-permute-start | bytes 1572872 | tf_op jit(solution)/shard_map/ppermute | solution.py:400
  23.0 2.7 %collective-permute-start.5 = (bf16[1024,256]{1,0:T(8,128)(2,1)S(1)}, bf16[1024,256]{1,0:T(8,128)(2,1)S(1)}, u32[]{:S(2)}, u32[]{:S(2)}) collective-permute-start(bf16[1024,256]{1,0:T(8,128)(2,1)S(1)} %collective-permute-done.1), channel_id=1, source_target_pairs={{0,2},{1,3},{2,0},{3,1},{4,6},{5,7},{6,4},{7,5},{8,10},{9,11},{10,... | collective-permute-start | bytes 1572872 | tf_op jit(solution)/shard_map/ppermute | solution.py:400
  25.8 2.5 %collective-permute-done.6 = bf16[1024,256]{1,0:T(8,128)(2,1)} collective-permute-done((bf16[1024,256]{1,0:T(8,128)(2,1)}, bf16[1024,256]{1,0:T(8,128)(2,1)}, u32[]{:S(2)}, u32[]{:S(2)}) %collective-permute-start.6) | collective-permute-done | bytes 524320 | tf_op jit(solution)/shard_map/ppermute | solution.py:400
  28.4 1.1 constant_dynamic-update-slice_fusion.3
  29.5 0.7 collective-permute-start.11
  30.2 2.0 %shard_map.75 = (f32[1024,768]{1,0:T(8,128)S(1)}, f32[1024,128]{1,0:T(8,128)S(1)}) custom-call(f32[16,256]{1,0:T(8,128)S(1)} %reshape.3.refs_0_, bf16[3,4096,256]{2,1,0:T(8,128)(2,1)S(1)} %bitcast.4, bf16[2048,256]{1,0:T(8,128)(2,1)S(1)} %constant_dynamic-update-slice_fusion.refs_2_, ...), custom_call_target="tpu_custom_call", output_to_operand_aliasing={{0}: (4, {}), {1}: (5, {})} | custom-call | flops 1 | bytes 1 | tf_op jit(solution)/shard_map/pallas_call | solution.py:25
  32.3 7.2 %collective-permute-done.3.refs_5_ = bf16[1024,256]{1,0:T(8,128)(2,1)S(1)} collective-permute-done((bf16[1024,256]{1,0:T(8,128)(2,1)S(1)}, bf16[1024,256]{1,0:T(8,128)(2,1)S(1)}, u32[]{:S(2)}, u32[]{:S(2)}) %collective-permute-start.3) | collective-permute-done | bytes 524320 | tf_op jit(solution)/shard_map/ppermute | solution.py:400
  39.6 0.8 collective-permute-start.10
  40.4 0.5 collective-permute-start.9
  41.0 3.3 %shard_map.76 = (f32[1024,768]{1,0:T(8,128)S(1)}, f32[1024,128]{1,0:T(8,128)S(1)}) custom-call(f32[16,256]{1,0:T(8,128)S(1)} %reshape.3.refs_0_, bf16[3,4096,256]{2,1,0:T(8,128)(2,1)S(1)} %bitcast.5, bf16[2048,256]{1,0:T(8,128)(2,1)S(1)} %collective-permute-done.11.refs_2_, ...), custom_call_target="tpu_custom_call", output_to_operand_aliasing={{0}: (7, {}), {1}: (8, {})} | custom-call | flops 1 | bytes 1 | tf_op jit(solution)/shard_map/pallas_call | solution.py:25
  44.3 6.1 %shard_map.77 = (f32[1024,256]{1,0:T(8,128)S(1)}, f32[1024,256]{1,0:T(8,128)S(1)}, f32[128,256]{1,0:T(8,128)S(1)}, bf16[8,80,256]{2,1,0:T(8,128)(2,1)S(1)}) custom-call(f32[16,256]{1,0:T(8,128)S(1)} %reshape.3.refs_0_, bf16[3,4096,256]{2,1,0:T(8,128)(2,1)S(1)} %bitcast.8, bf16[1024,256]{1,0:T(8,128)(2,1)S(1)} %collective-permute-done.8.refs_2_, ...), custom_call_target="tpu_custom_call" | custom-call | flops 1 | bytes 1 | tf_op jit(solution)/shard_map/pallas_call | solution.py:25
  50.4 13.3 %all_to_all.5.refs_0_ = bf16[8,80,256]{2,1,0:T(8,128)(2,1)S(1)} all-to-all(bf16[8,80,256]{2,1,0:T(8,128)(2,1)S(1)} %get-tuple-element.44), channel_id=1, replica_groups=mesh['ctx'=8,'tp'=16] {'ctx'}, dimensions={0} | all-to-all | bytes 655360 | tf_op jit(solution)/shard_map/all_to_all | solution.py:485
  63.8 1.7 %shard_map.78.refs_1_ = bf16[1024,256]{1,0:T(8,128)(2,1)S(1)} custom-call(bf16[8,80,256]{2,1,0:T(8,128)(2,1)S(1)} %all_to_all.5.refs_0_, f32[1024,256]{1,0:T(8,128)S(1)} %get-tuple-element.45.refs_1_, f32[1024,256]{1,0:T(8,128)S(1)} %get-tuple-element.46.refs_2_, f32[128,256]{1,0:T(8,128)S(1)} %get-tuple-element.47.refs_3_, ...), custom_call_target="tpu_custom_call" | custom-call | flops 1 | bytes 1 | tf_op jit(solution)/shard_map/pallas_call | solution.py:25
  65.5 1.1 %collective-permute-start.15 = (bf16[1024,256]{1,0:T(8,128)(2,1)S(1)}, bf16[1024,256]{1,0:T(8,128)(2,1)S(1)}, u32[]{:S(2)}, u32[]{:S(2)}) collective-permute-start(bf16[1024,256]{1,0:T(8,128)(2,1)S(1)} %shard_map.78.refs_1_), channel_id=1, source_target_pairs={{0,1},{1,0},{2,3},{3,2},{4,5},{5,4},{6,7},{7,6},{8,9},{9,8},{10,11... | collective-permute-start | bytes 1572872 | tf_op jit(solution)/shard_map/ppermute | solution.py:400
  66.6 2.6 %collective-permute-start.14 = (bf16[1024,256]{1,0:T(8,128)(2,1)S(1)}, bf16[1024,256]{1,0:T(8,128)(2,1)S(1)}, u32[]{:S(2)}, u32[]{:S(2)}) collective-permute-start(bf16[1024,256]{1,0:T(8,128)(2,1)S(1)} %shard_map.78.refs_1_), channel_id=1, source_target_pairs={{0,8},{1,9},{2,10},{3,11},{4,12},{5,13},{6,14},{7,15},{8,0},{9,1},... | collective-permute-start | bytes 1572872 | tf_op jit(solution)/shard_map/ppermute | solution.py:400
  69.2 2.8 %collective-permute-start.13 = (bf16[1024,256]{1,0:T(8,128)(2,1)S(1)}, bf16[1024,256]{1,0:T(8,128)(2,1)S(1)}, u32[]{:S(2)}, u32[]{:S(2)}) collective-permute-start(bf16[1024,256]{1,0:T(8,128)(2,1)S(1)} %shard_map.78.refs_1_), channel_id=1, source_target_pairs={{0,2},{1,3},{2,0},{3,1},{4,6},{5,7},{6,4},{7,5},{8,10},{9,11},{10,... | collective-permute-start | bytes 1572872 | tf_op jit(solution)/shard_map/ppermute | solution.py:400
  72.0 0.9 collective-permute-start.19
  72.8 1.8 %collective-permute-start.20 = (bf16[1024,256]{1,0:T(8,128)(2,1)S(1)}, bf16[1024,256]{1,0:T(8,128)(2,1)S(1)}, u32[]{:S(2)}, u32[]{:S(2)}) collective-permute-start(bf16[1024,256]{1,0:T(8,128)(2,1)S(1)} %shard_map.78.refs_1_), channel_id=1, source_target_pairs={{0,12},{1,13},{2,14},{3,15},{4,0},{5,1},{6,2},{7,3},{8,4},{9,5},{1... | collective-permute-start | bytes 1572872 | tf_op jit(solution)/shard_map/ppermute | solution.py:400
  74.7 0.5 shard_map.79.refs_3_
  75.1 6.5 %collective-permute-done.14 = bf16[1024,256]{1,0:T(8,128)(2,1)S(1)} collective-permute-done((bf16[1024,256]{1,0:T(8,128)(2,1)S(1)}, bf16[1024,256]{1,0:T(8,128)(2,1)S(1)}, u32[]{:S(2)}, u32[]{:S(2)}) %collective-permute-start.14) | collective-permute-done | bytes 524320 | tf_op jit(solution)/shard_map/ppermute | solution.py:400
  81.6 2.2 %collective-permute-done.13 = bf16[1024,256]{1,0:T(8,128)(2,1)S(1)} collective-permute-done((bf16[1024,256]{1,0:T(8,128)(2,1)S(1)}, bf16[1024,256]{1,0:T(8,128)(2,1)S(1)}, u32[]{:S(2)}, u32[]{:S(2)}) %collective-permute-start.13) | collective-permute-done | bytes 524320 | tf_op jit(solution)/shard_map/ppermute | solution.py:400
  83.8 1.0 collective-permute-start.16
  84.8 1.7 %collective-permute-start.17 = (bf16[1024,256]{1,0:T(8,128)(2,1)S(1)}, bf16[1024,256]{1,0:T(8,128)(2,1)S(1)}, u32[]{:S(2)}, u32[]{:S(2)}) collective-permute-start(bf16[1024,256]{1,0:T(8,128)(2,1)S(1)} %collective-permute-done.13), channel_id=1, source_target_pairs={{0,12},{1,13},{2,14},{3,15},{4,0},{5,1},{6,2},{7,3},{8,4},{9,5},{1... | collective-permute-start | bytes 1572872 | tf_op jit(solution)/shard_map/ppermute | solution.py:400
  86.5 2.8 %collective-permute-start.18 = (bf16[1024,256]{1,0:T(8,128)(2,1)S(1)}, bf16[1024,256]{1,0:T(8,128)(2,1)S(1)}, u32[]{:S(2)}, u32[]{:S(2)}) collective-permute-start(bf16[1024,256]{1,0:T(8,128)(2,1)S(1)} %collective-permute-done.14), channel_id=1, source_target_pairs={{0,2},{1,3},{2,0},{3,1},{4,6},{5,7},{6,4},{7,5},{8,10},{9,11},{10,... | collective-permute-start | bytes 1572872 | tf_op jit(solution)/shard_map/ppermute | solution.py:400
  89.4 3.8 %collective-permute-done.19 = bf16[1024,256]{1,0:T(8,128)(2,1)S(1)} collective-permute-done((bf16[1024,256]{1,0:T(8,128)(2,1)S(1)}, bf16[1024,256]{1,0:T(8,128)(2,1)S(1)}, u32[]{:S(2)}, u32[]{:S(2)}) %collective-permute-start.19) | collective-permute-done | bytes 524320 | tf_op jit(solution)/shard_map/ppermute | solution.py:400
  93.3 1.0 collective-permute-start.24
  94.4 0.7 shard_map.80.refs_6_
  95.1 9.3 %collective-permute-done.16.refs_4_ = bf16[1024,256]{1,0:T(8,128)(2,1)S(1)} collective-permute-done((bf16[1024,256]{1,0:T(8,128)(2,1)S(1)}, bf16[1024,256]{1,0:T(8,128)(2,1)S(1)}, u32[]{:S(2)}, u32[]{:S(2)}) %collective-permute-start.16) | collective-permute-done | bytes 524320 | tf_op jit(solution)/shard_map/ppermute | solution.py:400
  104.4 0.5 collective-permute-start.21
  105.0 0.4 collective-permute-start.23
  105.5 1.1 %shard_map.81.refs_4_ = f32[1024,256]{1,0:T(8,128)S(1)} custom-call(bf16[4096,256]{1,0:T(8,128)(2,1)S(1)} %copy-done.1, bf16[2048,256]{1,0:T(8,128)(2,1)S(1)} %collective-permute-done.24.refs_1_, bf16[2048,256]{1,0:T(8,128)(2,1)S(1)} %collective-permute-done.25.refs_2_, ...), custom_call_target="tpu_custom_call", output_to_operand_aliasing={{}: (6, {})} | custom-call | flops 1 | bytes 1 | tf_op jit(solution)/shard_map/pallas_call | solution.py:25
  106.6 0.6 collective-permute-done.22.refs_2_
  107.2 0.7 collective-permute-done.23.refs_3_
  108.0 1.4 %shard_map.82 = bf16[1024,256]{1,0:T(8,128)(2,1)} custom-call(bf16[4096,256]{1,0:T(8,128)(2,1)S(1)} %copy-done.1, bf16[1024,256]{1,0:T(8,128)(2,1)S(1)} %collective-permute-done.21.refs_1_, bf16[1024,256]{1,0:T(8,128)(2,1)S(1)} %collective-permute-done.22.refs_2_, bf16[1024,256]{1,0:T(8,128)(2,1)S(1)} %collective-permute-done.23.refs_3_, ...), custom_call_target="tpu_custom_call" | custom-call | flops 1 | bytes 1 | tf_op jit(solution)/shard_map/pallas_call | solution.py:25
  (40 shorter events, 0.8 us)
Async XLA Ops:
  0.0 13.7 %collective-permute-start.2 = (bf16[1024,256]{1,0:T(8,128)(2,1)}, bf16[1024,256]{1,0:T(8,128)(2,1)S(1)}, u32[]{:S(2)}, u32[]{:S(2)}) collective-permute-start(bf16[1024,256]{1,0:T(8,128)(2,1)} %refs_5_.1), channel_id=1, source_target_pairs={{0,1},{1,0},{2,3},{3,2},{4,5},{5,4},{6,7},{7,6},{8,9},{9,8},{10,11... | collective-permute-start | bytes 1572872 | tf_op jit(solution)/shard_map/ppermute | solution.py:400
  1.4 17.1 %collective-permute-start.1 = (bf16[1024,256]{1,0:T(8,128)(2,1)}, bf16[1024,256]{1,0:T(8,128)(2,1)S(1)}, u32[]{:S(2)}, u32[]{:S(2)}) collective-permute-start(bf16[1024,256]{1,0:T(8,128)(2,1)} %refs_5_.1), channel_id=1, source_target_pairs={{0,8},{1,9},{2,10},{3,11},{4,12},{5,13},{6,14},{7,15},{8,0},{9,1},... | collective-permute-start | bytes 1572872 | tf_op jit(solution)/shard_map/ppermute | solution.py:400
  4.4 15.9 %collective-permute-start = (bf16[1024,256]{1,0:T(8,128)(2,1)}, bf16[1024,256]{1,0:T(8,128)(2,1)S(1)}, u32[]{:S(2)}, u32[]{:S(2)}) collective-permute-start(bf16[1024,256]{1,0:T(8,128)(2,1)} %refs_5_.1), channel_id=1, source_target_pairs={{0,2},{1,3},{2,0},{3,1},{4,6},{5,7},{6,4},{7,5},{8,10},{9,11},{10,... | collective-permute-start | bytes 1572872 | tf_op jit(solution)/shard_map/ppermute | solution.py:400
  8.0 20.3 %collective-permute-start.6 = (bf16[1024,256]{1,0:T(8,128)(2,1)}, bf16[1024,256]{1,0:T(8,128)(2,1)}, u32[]{:S(2)}, u32[]{:S(2)}) collective-permute-start(bf16[1024,256]{1,0:T(8,128)(2,1)} %refs_5_.1), channel_id=1, source_target_pairs={{0,4},{1,5},{2,6},{3,7},{4,8},{5,9},{6,10},{7,11},{8,12},{9,13},{1... | collective-permute-start | bytes 1572872 | tf_op jit(solution)/shard_map/ppermute | solution.py:400
  8.4 21.0 %collective-permute-start.7 = (bf16[1024,256]{1,0:T(8,128)(2,1)}, bf16[1024,256]{1,0:T(8,128)(2,1)S(1)}, u32[]{:S(2)}, u32[]{:S(2)}) collective-permute-start(bf16[1024,256]{1,0:T(8,128)(2,1)} %refs_5_.1), channel_id=1, source_target_pairs={{0,12},{1,13},{2,14},{3,15},{4,0},{5,1},{6,2},{7,3},{8,4},{9,5},{1... | collective-permute-start | bytes 1572872 | tf_op jit(solution)/shard_map/ppermute | solution.py:400
  11.4 0.7 copy-start.3
  12.2 0.7 copy-start.4
  13.7 2.8 %copy-start = (bf16[4096,3,256]{2,0,1:T(8,128)(2,1)S(1)}, bf16[4096,3,256]{2,0,1:T(8,128)(2,1)}, u32[]{:S(2)}) copy-start(bf16[4096,3,256]{2,0,1:T(8,128)(2,1)} %param.9) | copy-start | bytes 18874372
  16.5 1.0 copy-start.2
  20.4 19.1 %collective-permute-start.3 = (bf16[1024,256]{1,0:T(8,128)(2,1)S(1)}, bf16[1024,256]{1,0:T(8,128)(2,1)S(1)}, u32[]{:S(2)}, u32[]{:S(2)}) collective-permute-start(bf16[1024,256]{1,0:T(8,128)(2,1)S(1)} %collective-permute-done), channel_id=1, source_target_pairs={{0,4},{1,5},{2,6},{3,7},{4,8},{5,9},{6,10},{7,11},{8,12},{9,13},{1... | collective-permute-start | bytes 1572872 | tf_op jit(solution)/shard_map/ppermute | solution.py:400
  20.8 18.9 %collective-permute-start.4 = (bf16[1024,256]{1,0:T(8,128)(2,1)S(1)}, bf16[1024,256]{1,0:T(8,128)(2,1)S(1)}, u32[]{:S(2)}, u32[]{:S(2)}) collective-permute-start(bf16[1024,256]{1,0:T(8,128)(2,1)S(1)} %collective-permute-done), channel_id=1, source_target_pairs={{0,12},{1,13},{2,14},{3,15},{4,0},{5,1},{6,2},{7,3},{8,4},{9,5},{1... | collective-permute-start | bytes 1572872 | tf_op jit(solution)/shard_map/ppermute | solution.py:400
  23.0 16.6 %collective-permute-start.5 = (bf16[1024,256]{1,0:T(8,128)(2,1)S(1)}, bf16[1024,256]{1,0:T(8,128)(2,1)S(1)}, u32[]{:S(2)}, u32[]{:S(2)}) collective-permute-start(bf16[1024,256]{1,0:T(8,128)(2,1)S(1)} %collective-permute-done.1), channel_id=1, source_target_pairs={{0,2},{1,3},{2,0},{3,1},{4,6},{5,7},{6,4},{7,5},{8,10},{9,11},{10,... | collective-permute-start | bytes 1572872 | tf_op jit(solution)/shard_map/ppermute | solution.py:400
  29.5 11.4 %collective-permute-start.11 = (bf16[2048,256]{1,0:T(8,128)(2,1)S(1)}, bf16[2048,256]{1,0:T(8,128)(2,1)S(1)}, u32[]{:S(2)}, u32[]{:S(2)}) collective-permute-start(bf16[2048,256]{1,0:T(8,128)(2,1)S(1)} %constant_dynamic-update-slice_fusion.refs_2_), channel_id=1, source_target_pairs={{0,1},{1,0},{2,3},{3,2},{4,5},{5,4},{6,7},{7,6},{8,9},{9,8},{10,11... | collective-permute-start | bytes 3145736 | tf_op jit(solution)/shard_map/ppermute | solution.py:400
  30.2 10.8 %collective-permute-start.12 = (bf16[2048,256]{1,0:T(8,128)(2,1)S(1)}, bf16[2048,256]{1,0:T(8,128)(2,1)S(1)}, u32[]{:S(2)}, u32[]{:S(2)}) collective-permute-start(bf16[2048,256]{1,0:T(8,128)(2,1)S(1)} %constant_dynamic-update-slice_fusion.2.refs_3_), channel_id=1, source_target_pairs={{0,1},{1,0},{2,3},{3,2},{4,5},{5,4},{6,7},{7,6},{8,9},{9,8},{10,11... | collective-permute-start | bytes 3145736 | tf_op jit(solution)/shard_map/ppermute | solution.py:400
  39.6 4.6 %collective-permute-start.10 = (bf16[1024,256]{1,0:T(8,128)(2,1)S(1)}, bf16[1024,256]{1,0:T(8,128)(2,1)S(1)}, u32[]{:S(2)}, u32[]{:S(2)}) collective-permute-start(bf16[1024,256]{1,0:T(8,128)(2,1)S(1)} %collective-permute-done.4.refs_6_), channel_id=1, source_target_pairs={{0,1},{1,0},{2,3},{3,2},{4,5},{5,4},{6,7},{7,6},{8,9},{9,8},{10,11... | collective-permute-start | bytes 1572872 | tf_op jit(solution)/shard_map/ppermute | solution.py:400
  40.4 3.8 %collective-permute-start.8 = (bf16[1024,256]{1,0:T(8,128)(2,1)S(1)}, bf16[1024,256]{1,0:T(8,128)(2,1)S(1)}, u32[]{:S(2)}, u32[]{:S(2)}) collective-permute-start(bf16[1024,256]{1,0:T(8,128)(2,1)S(1)} %collective-permute-done.5.refs_4_), channel_id=1, source_target_pairs={{0,1},{1,0},{2,3},{3,2},{4,5},{5,4},{6,7},{7,6},{8,9},{9,8},{10,11... | collective-permute-start | bytes 1572872 | tf_op jit(solution)/shard_map/ppermute | solution.py:400
  40.4 3.8 %collective-permute-start.9 = (bf16[1024,256]{1,0:T(8,128)(2,1)S(1)}, bf16[1024,256]{1,0:T(8,128)(2,1)S(1)}, u32[]{:S(2)}, u32[]{:S(2)}) collective-permute-start(bf16[1024,256]{1,0:T(8,128)(2,1)S(1)} %collective-permute-done.3.refs_5_), channel_id=1, source_target_pairs={{0,1},{1,0},{2,3},{3,2},{4,5},{5,4},{6,7},{7,6},{8,9},{9,8},{10,11... | collective-permute-start | bytes 1572872 | tf_op jit(solution)/shard_map/ppermute | solution.py:400
  40.9 3.3 %slice-start = ((s8[6291456]{0:T(1024)(128)(4,1)}), s8[4194304]{0:T(1024)(128)(4,1)S(1)}, s32[]{:S(2)}) async-start(s8[6291456]{0:T(1024)(128)(4,1)} %bitcast.6), calls=%async_computation.1 | async-start | bytes 8388608
  40.9 3.3 %slice-start.1 = ((s8[6291456]{0:T(1024)(128)(4,1)}), s8[2097152]{0:T(1024)(128)(4,1)S(1)}, s32[]{:S(2)}) async-start(s8[6291456]{0:T(1024)(128)(4,1)} %bitcast.6), calls=%async_computation.2 | async-start | bytes 4194304
  50.4 24.2 %copy-start.1 = (bf16[4096,256]{1,0:T(8,128)(2,1)S(1)}, bf16[4096,256]{1,0:T(8,128)(2,1)}, u32[]{:S(2)}) copy-start(bf16[4096,256]{1,0:T(8,128)(2,1)} %refs_0_.7) | copy-start | bytes 6291460
  65.5 9.2 %collective-permute-start.15 = (bf16[1024,256]{1,0:T(8,128)(2,1)S(1)}, bf16[1024,256]{1,0:T(8,128)(2,1)S(1)}, u32[]{:S(2)}, u32[]{:S(2)}) collective-permute-start(bf16[1024,256]{1,0:T(8,128)(2,1)S(1)} %shard_map.78.refs_1_), channel_id=1, source_target_pairs={{0,1},{1,0},{2,3},{3,2},{4,5},{5,4},{6,7},{7,6},{8,9},{9,8},{10,11... | collective-permute-start | bytes 1572872 | tf_op jit(solution)/shard_map/ppermute | solution.py:400
  66.6 15.0 %collective-permute-start.14 = (bf16[1024,256]{1,0:T(8,128)(2,1)S(1)}, bf16[1024,256]{1,0:T(8,128)(2,1)S(1)}, u32[]{:S(2)}, u32[]{:S(2)}) collective-permute-start(bf16[1024,256]{1,0:T(8,128)(2,1)S(1)} %shard_map.78.refs_1_), channel_id=1, source_target_pairs={{0,8},{1,9},{2,10},{3,11},{4,12},{5,13},{6,14},{7,15},{8,0},{9,1},... | collective-permute-start | bytes 1572872 | tf_op jit(solution)/shard_map/ppermute | solution.py:400
  69.2 14.7 %collective-permute-start.13 = (bf16[1024,256]{1,0:T(8,128)(2,1)S(1)}, bf16[1024,256]{1,0:T(8,128)(2,1)S(1)}, u32[]{:S(2)}, u32[]{:S(2)}) collective-permute-start(bf16[1024,256]{1,0:T(8,128)(2,1)S(1)} %shard_map.78.refs_1_), channel_id=1, source_target_pairs={{0,2},{1,3},{2,0},{3,1},{4,6},{5,7},{6,4},{7,5},{8,10},{9,11},{10,... | collective-permute-start | bytes 1572872 | tf_op jit(solution)/shard_map/ppermute | solution.py:400
  72.0 21.2 %collective-permute-start.19 = (bf16[1024,256]{1,0:T(8,128)(2,1)S(1)}, bf16[1024,256]{1,0:T(8,128)(2,1)S(1)}, u32[]{:S(2)}, u32[]{:S(2)}) collective-permute-start(bf16[1024,256]{1,0:T(8,128)(2,1)S(1)} %shard_map.78.refs_1_), channel_id=1, source_target_pairs={{0,4},{1,5},{2,6},{3,7},{4,8},{5,9},{6,10},{7,11},{8,12},{9,13},{1... | collective-permute-start | bytes 1572872 | tf_op jit(solution)/shard_map/ppermute | solution.py:400
  72.8 20.4 %collective-permute-start.20 = (bf16[1024,256]{1,0:T(8,128)(2,1)S(1)}, bf16[1024,256]{1,0:T(8,128)(2,1)S(1)}, u32[]{:S(2)}, u32[]{:S(2)}) collective-permute-start(bf16[1024,256]{1,0:T(8,128)(2,1)S(1)} %shard_map.78.refs_1_), channel_id=1, source_target_pairs={{0,12},{1,13},{2,14},{3,15},{4,0},{5,1},{6,2},{7,3},{8,4},{9,5},{1... | collective-permute-start | bytes 1572872 | tf_op jit(solution)/shard_map/ppermute | solution.py:400
  83.8 20.6 %collective-permute-start.16 = (bf16[1024,256]{1,0:T(8,128)(2,1)S(1)}, bf16[1024,256]{1,0:T(8,128)(2,1)S(1)}, u32[]{:S(2)}, u32[]{:S(2)}) collective-permute-start(bf16[1024,256]{1,0:T(8,128)(2,1)S(1)} %collective-permute-done.13), channel_id=1, source_target_pairs={{0,4},{1,5},{2,6},{3,7},{4,8},{5,9},{6,10},{7,11},{8,12},{9,13},{1... | collective-permute-start | bytes 1572872 | tf_op jit(solution)/shard_map/ppermute | solution.py:400
  84.8 19.6 %collective-permute-start.17 = (bf16[1024,256]{1,0:T(8,128)(2,1)S(1)}, bf16[1024,256]{1,0:T(8,128)(2,1)S(1)}, u32[]{:S(2)}, u32[]{:S(2)}) collective-permute-start(bf16[1024,256]{1,0:T(8,128)(2,1)S(1)} %collective-permute-done.13), channel_id=1, source_target_pairs={{0,12},{1,13},{2,14},{3,15},{4,0},{5,1},{6,2},{7,3},{8,4},{9,5},{1... | collective-permute-start | bytes 1572872 | tf_op jit(solution)/shard_map/ppermute | solution.py:400
  86.5 17.9 %collective-permute-start.18 = (bf16[1024,256]{1,0:T(8,128)(2,1)S(1)}, bf16[1024,256]{1,0:T(8,128)(2,1)S(1)}, u32[]{:S(2)}, u32[]{:S(2)}) collective-permute-start(bf16[1024,256]{1,0:T(8,128)(2,1)S(1)} %collective-permute-done.14), channel_id=1, source_target_pairs={{0,2},{1,3},{2,0},{3,1},{4,6},{5,7},{6,4},{7,5},{8,10},{9,11},{10,... | collective-permute-start | bytes 1572872 | tf_op jit(solution)/shard_map/ppermute | solution.py:400
  93.3 12.2 %collective-permute-start.24 = (bf16[2048,256]{1,0:T(8,128)(2,1)S(1)}, bf16[2048,256]{1,0:T(8,128)(2,1)S(1)}, u32[]{:S(2)}, u32[]{:S(2)}) collective-permute-start(bf16[2048,256]{1,0:T(8,128)(2,1)S(1)} %constant_dynamic-update-slice_fusion.4.refs_1_), channel_id=1, source_target_pairs={{0,1},{1,0},{2,3},{3,2},{4,5},{5,4},{6,7},{7,6},{8,9},{9,8},{10,11... | collective-permute-start | bytes 3145736 | tf_op jit(solution)/shard_map/ppermute | solution.py:400
  94.3 11.2 %collective-permute-start.25 = (bf16[2048,256]{1,0:T(8,128)(2,1)S(1)}, bf16[2048,256]{1,0:T(8,128)(2,1)S(1)}, u32[]{:S(2)}, u32[]{:S(2)}) collective-permute-start(bf16[2048,256]{1,0:T(8,128)(2,1)S(1)} %constant_dynamic-update-slice_fusion.6.refs_2_), channel_id=1, source_target_pairs={{0,1},{1,0},{2,3},{3,2},{4,5},{5,4},{6,7},{7,6},{8,9},{9,8},{10,11... | collective-permute-start | bytes 3145736 | tf_op jit(solution)/shard_map/ppermute | solution.py:400
  104.4 2.2 %collective-permute-start.21 = (bf16[1024,256]{1,0:T(8,128)(2,1)S(1)}, bf16[1024,256]{1,0:T(8,128)(2,1)S(1)}, u32[]{:S(2)}, u32[]{:S(2)}) collective-permute-start(bf16[1024,256]{1,0:T(8,128)(2,1)S(1)} %collective-permute-done.18.refs_3_), channel_id=1, source_target_pairs={{0,1},{1,0},{2,3},{3,2},{4,5},{5,4},{6,7},{7,6},{8,9},{9,8},{10,11... | collective-permute-start | bytes 1572872 | tf_op jit(solution)/shard_map/ppermute | solution.py:400
  104.9 2.3 %collective-permute-start.22 = (bf16[1024,256]{1,0:T(8,128)(2,1)S(1)}, bf16[1024,256]{1,0:T(8,128)(2,1)S(1)}, u32[]{:S(2)}, u32[]{:S(2)}) collective-permute-start(bf16[1024,256]{1,0:T(8,128)(2,1)S(1)} %collective-permute-done.16.refs_4_), channel_id=1, source_target_pairs={{0,1},{1,0},{2,3},{3,2},{4,5},{5,4},{6,7},{7,6},{8,9},{9,8},{10,11... | collective-permute-start | bytes 1572872 | tf_op jit(solution)/shard_map/ppermute | solution.py:400
  105.0 3.0 %collective-permute-start.23 = (bf16[1024,256]{1,0:T(8,128)(2,1)S(1)}, bf16[1024,256]{1,0:T(8,128)(2,1)S(1)}, u32[]{:S(2)}, u32[]{:S(2)}) collective-permute-start(bf16[1024,256]{1,0:T(8,128)(2,1)S(1)} %collective-permute-done.17.refs_5_), channel_id=1, source_target_pairs={{0,1},{1,0},{2,3},{3,2},{4,5},{5,4},{6,7},{7,6},{8,9},{9,8},{10,11... | collective-permute-start | bytes 1572872 | tf_op jit(solution)/shard_map/ppermute | solution.py:400

commit v6 on v5

--- a/solution.py
+++ b/solution.py
@@ -211,7 +211,7 @@
                         for u in range(unroll)
                     ]
                 )
-            kv = [(short[1][u] * short[2][u]).astype(BF16).astype(F32) for u in range(unroll)]
+            kv = [short[1][u] * short[2][u] for u in range(unroll)]
             if masked:
                 kv = [jnp.where(head, 0.0, v) if u < REACH else v for u, v in enumerate(kv)]
             outs = [None] * unroll
@@ -228,7 +228,7 @@
                 later.extend(now)
             for u in range(unroll):
                 place = pl.ds(pl.multiple_of((begin + u) * SUBS, SUBS), SUBS)
-                gate[place, lanes] = short[0][u].astype(BF16).astype(F32)
+                gate[place, lanes] = short[0][u]
                 local[place, lanes] = outs[u]
             return later
 
@@ -298,8 +298,8 @@
                     value = term if value is None else value + term
                 values.append(value)
             short.append(values)
-        kv = [(short[1][t] * short[2][t]).astype(BF16).astype(F32) for t in range(REACH)]
-        q = [short[0][t].astype(BF16).astype(F32) for t in range(REACH)]
+        kv = [short[1][t] * short[2][t] for t in range(REACH)]
+        q = short[0]
         for n in range(MODES):
             at = n * SUBS
             full = strided(n)

time: 110 us -> 110 us (level)
  no operation moved by 1% of the time
where the time goes in v6:
time: 110 us; the launch traced here: 109 us
  starting transfers between devices  34.9 us (32%)
  waiting for transfers between devices  34.9 us (32%)
  Pallas kernels  17.7 us (16%)
  blocking collectives  13.3 us (12%)
  local copies, waits for them, and re-layouts  8.07 us (7%)
    ppermute x26, starting transfers between devices, shifted(): return lax.ppermute(x, 'tp', pairs)  34.9 us
    ppermute x26, waiting for transfers between devices, shifted(): return lax.ppermute(x, 'tp', pairs)  34.9 us
    pallas_call x10, Pallas kernels, call(): pl.pallas_call(kernel, out_shape=outs, in_specs=specs, out_specs=[VMEM] *...  17.7 us
    all_to_all x1, blocking collectives, body(): loads = lax.all_to_all(load, 'ctx', 0, 0, tiled=True)  13.3 us
    unnamed x19, local copies, waits for them, and re-layouts  7.19 us
  transfers between devices with their start and end apart: 26, of which 10 were waited for; matrix products, arithmetic and copies ran while one was open for 3% of the time, Pallas kernels for 8%

profile of v6, /device:TPU:1, one launch (start us, length us, event | category | flops | bytes accessed | tf_op | source)
XLA Modules:
  0.0 109.1 jit_solution(16232535655126025031)
XLA Ops:
  0.0 1.4 %collective-permute-start.2 = (bf16[1024,256]{1,0:T(8,128)(2,1)}, bf16[1024,256]{1,0:T(8,128)(2,1)S(1)}, u32[]{:S(2)}, u32[]{:S(2)}) collective-permute-start(bf16[1024,256]{1,0:T(8,128)(2,1)} %refs_5_.1), channel_id=1, source_target_pairs={{0,1},{1,0},{2,3},{3,2},{4,5},{5,4},{6,7},{7,6},{8,9},{9,8},{10,11... | collective-permute-start | bytes 1572872 | tf_op jit(solution)/shard_map/ppermute | solution.py:400
  1.4 3.0 %collective-permute-start.1 = (bf16[1024,256]{1,0:T(8,128)(2,1)}, bf16[1024,256]{1,0:T(8,128)(2,1)S(1)}, u32[]{:S(2)}, u32[]{:S(2)}) collective-permute-start(bf16[1024,256]{1,0:T(8,128)(2,1)} %refs_5_.1), channel_id=1, source_target_pairs={{0,8},{1,9},{2,10},{3,11},{4,12},{5,13},{6,14},{7,15},{8,0},{9,1},... | collective-permute-start | bytes 1572872 | tf_op jit(solution)/shard_map/ppermute | solution.py:400
  4.4 3.6 %collective-permute-start = (bf16[1024,256]{1,0:T(8,128)(2,1)}, bf16[1024,256]{1,0:T(8,128)(2,1)S(1)}, u32[]{:S(2)}, u32[]{:S(2)}) collective-permute-start(bf16[1024,256]{1,0:T(8,128)(2,1)} %refs_5_.1), channel_id=1, source_target_pairs={{0,2},{1,3},{2,0},{3,1},{4,6},{5,7},{6,4},{7,5},{8,10},{9,11},{10,... | collective-permute-start | bytes 1572872 | tf_op jit(solution)/shard_map/ppermute | solution.py:400
  8.0 0.4 collective-permute-start.6
  8.4 2.3 %collective-permute-start.7 = (bf16[1024,256]{1,0:T(8,128)(2,1)}, bf16[1024,256]{1,0:T(8,128)(2,1)S(1)}, u32[]{:S(2)}, u32[]{:S(2)}) collective-permute-start(bf16[1024,256]{1,0:T(8,128)(2,1)} %refs_5_.1), channel_id=1, source_target_pairs={{0,12},{1,13},{2,14},{3,15},{4,0},{5,1},{6,2},{7,3},{8,4},{9,5},{1... | collective-permute-start | bytes 1572872 | tf_op jit(solution)/shard_map/ppermute | solution.py:400
  10.7 0.7 copy.14.refs_2_
  11.5 0.7 copy-done.3
  12.2 0.7 copy-done.4
  13.0 0.7 reshape.3.refs_0_
  13.7 2.8 %copy-done = bf16[4096,3,256]{2,0,1:T(8,128)(2,1)S(1)} copy-done((bf16[4096,3,256]{2,0,1:T(8,128)(2,1)S(1)}, bf16[4096,3,256]{2,0,1:T(8,128)(2,1)}, u32[]{:S(2)}) %copy-start) | copy-done | bytes 6291480
  16.5 1.0 copy-done.2
  17.6 1.0 shard_map.74
  18.6 1.8 %collective-permute-done = bf16[1024,256]{1,0:T(8,128)(2,1)S(1)} collective-permute-done((bf16[1024,256]{1,0:T(8,128)(2,1)}, bf16[1024,256]{1,0:T(8,128)(2,1)S(1)}, u32[]{:S(2)}, u32[]{:S(2)}) %collective-permute-start) | collective-permute-done | bytes 524320 | tf_op jit(solution)/shard_map/ppermute | solution.py:400
  20.4 0.4 collective-permute-start.3
  20.8 2.3 %collective-permute-start.4 = (bf16[1024,256]{1,0:T(8,128)(2,1)S(1)}, bf16[1024,256]{1,0:T(8,128)(2,1)S(1)}, u32[]{:S(2)}, u32[]{:S(2)}) collective-permute-start(bf16[1024,256]{1,0:T(8,128)(2,1)S(1)} %collective-permute-done), channel_id=1, source_target_pairs={{0,12},{1,13},{2,14},{3,15},{4,0},{5,1},{6,2},{7,3},{8,4},{9,5},{1... | collective-permute-start | bytes 1572872 | tf_op jit(solution)/shard_map/ppermute | solution.py:400
  23.0 2.7 %collective-permute-start.5 = (bf16[1024,256]{1,0:T(8,128)(2,1)S(1)}, bf16[1024,256]{1,0:T(8,128)(2,1)S(1)}, u32[]{:S(2)}, u32[]{:S(2)}) collective-permute-start(bf16[1024,256]{1,0:T(8,128)(2,1)S(1)} %collective-permute-done.1), channel_id=1, source_target_pairs={{0,2},{1,3},{2,0},{3,1},{4,6},{5,7},{6,4},{7,5},{8,10},{9,11},{10,... | collective-permute-start | bytes 1572872 | tf_op jit(solution)/shard_map/ppermute | solution.py:400
  25.8 2.5 %collective-permute-done.6 = bf16[1024,256]{1,0:T(8,128)(2,1)} collective-permute-done((bf16[1024,256]{1,0:T(8,128)(2,1)}, bf16[1024,256]{1,0:T(8,128)(2,1)}, u32[]{:S(2)}, u32[]{:S(2)}) %collective-permute-start.6) | collective-permute-done | bytes 524320 | tf_op jit(solution)/shard_map/ppermute | solution.py:400
  28.4 1.1 constant_dynamic-update-slice_fusion.3
  29.5 0.7 collective-permute-start.11
  30.2 2.0 %shard_map.75 = (f32[1024,768]{1,0:T(8,128)S(1)}, f32[1024,128]{1,0:T(8,128)S(1)}) custom-call(f32[16,256]{1,0:T(8,128)S(1)} %reshape.3.refs_0_, bf16[3,4096,256]{2,1,0:T(8,128)(2,1)S(1)} %bitcast.4, bf16[2048,256]{1,0:T(8,128)(2,1)S(1)} %constant_dynamic-update-slice_fusion.refs_2_, ...), custom_call_target="tpu_custom_call", output_to_operand_aliasing={{0}: (4, {}), {1}: (5, {})} | custom-call | flops 1 | bytes 1 | tf_op jit(solution)/shard_map/pallas_call | solution.py:25
  32.3 7.2 %collective-permute-done.3.refs_5_ = bf16[1024,256]{1,0:T(8,128)(2,1)S(1)} collective-permute-done((bf16[1024,256]{1,0:T(8,128)(2,1)S(1)}, bf16[1024,256]{1,0:T(8,128)(2,1)S(1)}, u32[]{:S(2)}, u32[]{:S(2)}) %collective-permute-start.3) | collective-permute-done | bytes 524320 | tf_op jit(solution)/shard_map/ppermute | solution.py:400
  39.6 0.8 collective-permute-start.10
  40.4 0.5 collective-permute-start.9
  41.0 3.3 %shard_map.76 = (f32[1024,768]{1,0:T(8,128)S(1)}, f32[1024,128]{1,0:T(8,128)S(1)}) custom-call(f32[16,256]{1,0:T(8,128)S(1)} %reshape.3.refs_0_, bf16[3,4096,256]{2,1,0:T(8,128)(2,1)S(1)} %bitcast.5, bf16[2048,256]{1,0:T(8,128)(2,1)S(1)} %collective-permute-done.11.refs_2_, ...), custom_call_target="tpu_custom_call", output_to_operand_aliasing={{0}: (7, {}), {1}: (8, {})} | custom-call | flops 1 | bytes 1 | tf_op jit(solution)/shard_map/pallas_call | solution.py:25
  44.3 5.9 %shard_map.77 = (f32[1024,256]{1,0:T(8,128)S(1)}, f32[1024,256]{1,0:T(8,128)S(1)}, f32[128,256]{1,0:T(8,128)S(1)}, bf16[8,80,256]{2,1,0:T(8,128)(2,1)S(1)}) custom-call(f32[16,256]{1,0:T(8,128)S(1)} %reshape.3.refs_0_, bf16[3,4096,256]{2,1,0:T(8,128)(2,1)S(1)} %bitcast.8, bf16[1024,256]{1,0:T(8,128)(2,1)S(1)} %collective-permute-done.8.refs_2_, ...), custom_call_target="tpu_custom_call" | custom-call | flops 1 | bytes 1 | tf_op jit(solution)/shard_map/pallas_call | solution.py:25
  50.2 13.3 %all_to_all.5.refs_0_ = bf16[8,80,256]{2,1,0:T(8,128)(2,1)S(1)} all-to-all(bf16[8,80,256]{2,1,0:T(8,128)(2,1)S(1)} %get-tuple-element.44), channel_id=1, replica_groups=mesh['ctx'=8,'tp'=16] {'ctx'}, dimensions={0} | all-to-all | bytes 655360 | tf_op jit(solution)/shard_map/all_to_all | solution.py:485
  63.5 1.7 %shard_map.78.refs_1_ = bf16[1024,256]{1,0:T(8,128)(2,1)S(1)} custom-call(bf16[8,80,256]{2,1,0:T(8,128)(2,1)S(1)} %all_to_all.5.refs_0_, f32[1024,256]{1,0:T(8,128)S(1)} %get-tuple-element.45.refs_1_, f32[1024,256]{1,0:T(8,128)S(1)} %get-tuple-element.46.refs_2_, f32[128,256]{1,0:T(8,128)S(1)} %get-tuple-element.47.refs_3_, ...), custom_call_target="tpu_custom_call" | custom-call | flops 1 | bytes 1 | tf_op jit(solution)/shard_map/pallas_call | solution.py:25
  65.3 1.1 %collective-permute-start.15 = (bf16[1024,256]{1,0:T(8,128)(2,1)S(1)}, bf16[1024,256]{1,0:T(8,128)(2,1)S(1)}, u32[]{:S(2)}, u32[]{:S(2)}) collective-permute-start(bf16[1024,256]{1,0:T(8,128)(2,1)S(1)} %shard_map.78.refs_1_), channel_id=1, source_target_pairs={{0,1},{1,0},{2,3},{3,2},{4,5},{5,4},{6,7},{7,6},{8,9},{9,8},{10,11... | collective-permute-start | bytes 1572872 | tf_op jit(solution)/shard_map/ppermute | solution.py:400
  66.4 2.6 %collective-permute-start.14 = (bf16[1024,256]{1,0:T(8,128)(2,1)S(1)}, bf16[1024,256]{1,0:T(8,128)(2,1)S(1)}, u32[]{:S(2)}, u32[]{:S(2)}) collective-permute-start(bf16[1024,256]{1,0:T(8,128)(2,1)S(1)} %shard_map.78.refs_1_), channel_id=1, source_target_pairs={{0,8},{1,9},{2,10},{3,11},{4,12},{5,13},{6,14},{7,15},{8,0},{9,1},... | collective-permute-start | bytes 1572872 | tf_op jit(solution)/shard_map/ppermute | solution.py:400
  69.0 2.8 %collective-permute-start.13 = (bf16[1024,256]{1,0:T(8,128)(2,1)S(1)}, bf16[1024,256]{1,0:T(8,128)(2,1)S(1)}, u32[]{:S(2)}, u32[]{:S(2)}) collective-permute-start(bf16[1024,256]{1,0:T(8,128)(2,1)S(1)} %shard_map.78.refs_1_), channel_id=1, source_target_pairs={{0,2},{1,3},{2,0},{3,1},{4,6},{5,7},{6,4},{7,5},{8,10},{9,11},{10,... | collective-permute-start | bytes 1572872 | tf_op jit(solution)/shard_map/ppermute | solution.py:400
  71.8 0.9 collective-permute-start.19
  72.6 1.8 %collective-permute-start.20 = (bf16[1024,256]{1,0:T(8,128)(2,1)S(1)}, bf16[1024,256]{1,0:T(8,128)(2,1)S(1)}, u32[]{:S(2)}, u32[]{:S(2)}) collective-permute-start(bf16[1024,256]{1,0:T(8,128)(2,1)S(1)} %shard_map.78.refs_1_), channel_id=1, source_target_pairs={{0,12},{1,13},{2,14},{3,15},{4,0},{5,1},{6,2},{7,3},{8,4},{9,5},{1... | collective-permute-start | bytes 1572872 | tf_op jit(solution)/shard_map/ppermute | solution.py:400
  74.4 0.5 shard_map.79.refs_3_
  74.9 6.5 %collective-permute-done.14 = bf16[1024,256]{1,0:T(8,128)(2,1)S(1)} collective-permute-done((bf16[1024,256]{1,0:T(8,128)(2,1)S(1)}, bf16[1024,256]{1,0:T(8,128)(2,1)S(1)}, u32[]{:S(2)}, u32[]{:S(2)}) %collective-permute-start.14) | collective-permute-done | bytes 524320 | tf_op jit(solution)/shard_map/ppermute | solution.py:400
  81.4 2.2 %collective-permute-done.13 = bf16[1024,256]{1,0:T(8,128)(2,1)S(1)} collective-permute-done((bf16[1024,256]{1,0:T(8,128)(2,1)S(1)}, bf16[1024,256]{1,0:T(8,128)(2,1)S(1)}, u32[]{:S(2)}, u32[]{:S(2)}) %collective-permute-start.13) | collective-permute-done | bytes 524320 | tf_op jit(solution)/shard_map/ppermute | solution.py:400
  83.6 1.0 collective-permute-start.16
  84.6 1.7 %collective-permute-start.17 = (bf16[1024,256]{1,0:T(8,128)(2,1)S(1)}, bf16[1024,256]{1,0:T(8,128)(2,1)S(1)}, u32[]{:S(2)}, u32[]{:S(2)}) collective-permute-start(bf16[1024,256]{1,0:T(8,128)(2,1)S(1)} %collective-permute-done.13), channel_id=1, source_target_pairs={{0,12},{1,13},{2,14},{3,15},{4,0},{5,1},{6,2},{7,3},{8,4},{9,5},{1... | collective-permute-start | bytes 1572872 | tf_op jit(solution)/shard_map/ppermute | solution.py:400
  86.3 2.8 %collective-permute-start.18 = (bf16[1024,256]{1,0:T(8,128)(2,1)S(1)}, bf16[1024,256]{1,0:T(8,128)(2,1)S(1)}, u32[]{:S(2)}, u32[]{:S(2)}) collective-permute-start(bf16[1024,256]{1,0:T(8,128)(2,1)S(1)} %collective-permute-done.14), channel_id=1, source_target_pairs={{0,2},{1,3},{2,0},{3,1},{4,6},{5,7},{6,4},{7,5},{8,10},{9,11},{10,... | collective-permute-start | bytes 1572872 | tf_op jit(solution)/shard_map/ppermute | solution.py:400
  89.2 3.8 %collective-permute-done.19 = bf16[1024,256]{1,0:T(8,128)(2,1)S(1)} collective-permute-done((bf16[1024,256]{1,0:T(8,128)(2,1)S(1)}, bf16[1024,256]{1,0:T(8,128)(2,1)S(1)}, u32[]{:S(2)}, u32[]{:S(2)}) %collective-permute-start.19) | collective-permute-done | bytes 524320 | tf_op jit(solution)/shard_map/ppermute | solution.py:400
  93.1 1.0 collective-permute-start.24
  94.2 0.7 shard_map.80.refs_6_
  94.9 9.3 %collective-permute-done.16.refs_4_ = bf16[1024,256]{1,0:T(8,128)(2,1)S(1)} collective-permute-done((bf16[1024,256]{1,0:T(8,128)(2,1)S(1)}, bf16[1024,256]{1,0:T(8,128)(2,1)S(1)}, u32[]{:S(2)}, u32[]{:S(2)}) %collective-permute-start.16) | collective-permute-done | bytes 524320 | tf_op jit(solution)/shard_map/ppermute | solution.py:400
  104.2 0.5 collective-permute-start.21
  104.8 0.4 collective-permute-start.23
  105.2 1.1 %shard_map.81.refs_4_ = f32[1024,256]{1,0:T(8,128)S(1)} custom-call(bf16[4096,256]{1,0:T(8,128)(2,1)S(1)} %copy-done.1, bf16[2048,256]{1,0:T(8,128)(2,1)S(1)} %collective-permute-done.24.refs_1_, bf16[2048,256]{1,0:T(8,128)(2,1)S(1)} %collective-permute-done.25.refs_2_, ...), custom_call_target="tpu_custom_call", output_to_operand_aliasing={{}: (6, {})} | custom-call | flops 1 | bytes 1 | tf_op jit(solution)/shard_map/pallas_call | solution.py:25
  106.4 0.6 collective-permute-done.22.refs_2_
  107.0 0.7 collective-permute-done.23.refs_3_
  107.8 1.4 %shard_map.82 = bf16[1024,256]{1,0:T(8,128)(2,1)} custom-call(bf16[4096,256]{1,0:T(8,128)(2,1)S(1)} %copy-done.1, bf16[1024,256]{1,0:T(8,128)(2,1)S(1)} %collective-permute-done.21.refs_1_, bf16[1024,256]{1,0:T(8,128)(2,1)S(1)} %collective-permute-done.22.refs_2_, bf16[1024,256]{1,0:T(8,128)(2,1)S(1)} %collective-permute-done.23.refs_3_, ...), custom_call_target="tpu_custom_call" | custom-call | flops 1 | bytes 1 | tf_op jit(solution)/shard_map/pallas_call | solution.py:25
  (40 shorter events, 0.8 us)
Async XLA Ops:
  0.0 13.7 %collective-permute-start.2 = (bf16[1024,256]{1,0:T(8,128)(2,1)}, bf16[1024,256]{1,0:T(8,128)(2,1)S(1)}, u32[]{:S(2)}, u32[]{:S(2)}) collective-permute-start(bf16[1024,256]{1,0:T(8,128)(2,1)} %refs_5_.1), channel_id=1, source_target_pairs={{0,1},{1,0},{2,3},{3,2},{4,5},{5,4},{6,7},{7,6},{8,9},{9,8},{10,11... | collective-permute-start | bytes 1572872 | tf_op jit(solution)/shard_map/ppermute | solution.py:400
  1.4 17.1 %collective-permute-start.1 = (bf16[1024,256]{1,0:T(8,128)(2,1)}, bf16[1024,256]{1,0:T(8,128)(2,1)S(1)}, u32[]{:S(2)}, u32[]{:S(2)}) collective-permute-start(bf16[1024,256]{1,0:T(8,128)(2,1)} %refs_5_.1), channel_id=1, source_target_pairs={{0,8},{1,9},{2,10},{3,11},{4,12},{5,13},{6,14},{7,15},{8,0},{9,1},... | collective-permute-start | bytes 1572872 | tf_op jit(solution)/shard_map/ppermute | solution.py:400
  4.4 15.9 %collective-permute-start = (bf16[1024,256]{1,0:T(8,128)(2,1)}, bf16[1024,256]{1,0:T(8,128)(2,1)S(1)}, u32[]{:S(2)}, u32[]{:S(2)}) collective-permute-start(bf16[1024,256]{1,0:T(8,128)(2,1)} %refs_5_.1), channel_id=1, source_target_pairs={{0,2},{1,3},{2,0},{3,1},{4,6},{5,7},{6,4},{7,5},{8,10},{9,11},{10,... | collective-permute-start | bytes 1572872 | tf_op jit(solution)/shard_map/ppermute | solution.py:400
  8.0 20.3 %collective-permute-start.6 = (bf16[1024,256]{1,0:T(8,128)(2,1)}, bf16[1024,256]{1,0:T(8,128)(2,1)}, u32[]{:S(2)}, u32[]{:S(2)}) collective-permute-start(bf16[1024,256]{1,0:T(8,128)(2,1)} %refs_5_.1), channel_id=1, source_target_pairs={{0,4},{1,5},{2,6},{3,7},{4,8},{5,9},{6,10},{7,11},{8,12},{9,13},{1... | collective-permute-start | bytes 1572872 | tf_op jit(solution)/shard_map/ppermute | solution.py:400
  8.4 21.0 %collective-permute-start.7 = (bf16[1024,256]{1,0:T(8,128)(2,1)}, bf16[1024,256]{1,0:T(8,128)(2,1)S(1)}, u32[]{:S(2)}, u32[]{:S(2)}) collective-permute-start(bf16[1024,256]{1,0:T(8,128)(2,1)} %refs_5_.1), channel_id=1, source_target_pairs={{0,12},{1,13},{2,14},{3,15},{4,0},{5,1},{6,2},{7,3},{8,4},{9,5},{1... | collective-permute-start | bytes 1572872 | tf_op jit(solution)/shard_map/ppermute | solution.py:400
  11.4 0.7 copy-start.3
  12.2 0.7 copy-start.4
  13.7 2.8 %copy-start = (bf16[4096,3,256]{2,0,1:T(8,128)(2,1)S(1)}, bf16[4096,3,256]{2,0,1:T(8,128)(2,1)}, u32[]{:S(2)}) copy-start(bf16[4096,3,256]{2,0,1:T(8,128)(2,1)} %param.9) | copy-start | bytes 18874372
  16.5 1.0 copy-start.2
  20.4 19.1 %collective-permute-start.3 = (bf16[1024,256]{1,0:T(8,128)(2,1)S(1)}, bf16[1024,256]{1,0:T(8,128)(2,1)S(1)}, u32[]{:S(2)}, u32[]{:S(2)}) collective-permute-start(bf16[1024,256]{1,0:T(8,128)(2,1)S(1)} %collective-permute-done), channel_id=1, source_target_pairs={{0,4},{1,5},{2,6},{3,7},{4,8},{5,9},{6,10},{7,11},{8,12},{9,13},{1... | collective-permute-start | bytes 1572872 | tf_op jit(solution)/shard_map/ppermute | solution.py:400
  20.8 18.9 %collective-permute-start.4 = (bf16[1024,256]{1,0:T(8,128)(2,1)S(1)}, bf16[1024,256]{1,0:T(8,128)(2,1)S(1)}, u32[]{:S(2)}, u32[]{:S(2)}) collective-permute-start(bf16[1024,256]{1,0:T(8,128)(2,1)S(1)} %collective-permute-done), channel_id=1, source_target_pairs={{0,12},{1,13},{2,14},{3,15},{4,0},{5,1},{6,2},{7,3},{8,4},{9,5},{1... | collective-permute-start | bytes 1572872 | tf_op jit(solution)/shard_map/ppermute | solution.py:400
  23.0 16.6 %collective-permute-start.5 = (bf16[1024,256]{1,0:T(8,128)(2,1)S(1)}, bf16[1024,256]{1,0:T(8,128)(2,1)S(1)}, u32[]{:S(2)}, u32[]{:S(2)}) collective-permute-start(bf16[1024,256]{1,0:T(8,128)(2,1)S(1)} %collective-permute-done.1), channel_id=1, source_target_pairs={{0,2},{1,3},{2,0},{3,1},{4,6},{5,7},{6,4},{7,5},{8,10},{9,11},{10,... | collective-permute-start | bytes 1572872 | tf_op jit(solution)/shard_map/ppermute | solution.py:400
  29.5 11.4 %collective-permute-start.11 = (bf16[2048,256]{1,0:T(8,128)(2,1)S(1)}, bf16[2048,256]{1,0:T(8,128)(2,1)S(1)}, u32[]{:S(2)}, u32[]{:S(2)}) collective-permute-start(bf16[2048,256]{1,0:T(8,128)(2,1)S(1)} %constant_dynamic-update-slice_fusion.refs_2_), channel_id=1, source_target_pairs={{0,1},{1,0},{2,3},{3,2},{4,5},{5,4},{6,7},{7,6},{8,9},{9,8},{10,11... | collective-permute-start | bytes 3145736 | tf_op jit(solution)/shard_map/ppermute | solution.py:400
  30.2 10.8 %collective-permute-start.12 = (bf16[2048,256]{1,0:T(8,128)(2,1)S(1)}, bf16[2048,256]{1,0:T(8,128)(2,1)S(1)}, u32[]{:S(2)}, u32[]{:S(2)}) collective-permute-start(bf16[2048,256]{1,0:T(8,128)(2,1)S(1)} %constant_dynamic-update-slice_fusion.2.refs_3_), channel_id=1, source_target_pairs={{0,1},{1,0},{2,3},{3,2},{4,5},{5,4},{6,7},{7,6},{8,9},{9,8},{10,11... | collective-permute-start | bytes 3145736 | tf_op jit(solution)/shard_map/ppermute | solution.py:400
  39.6 4.6 %collective-permute-start.10 = (bf16[1024,256]{1,0:T(8,128)(2,1)S(1)}, bf16[1024,256]{1,0:T(8,128)(2,1)S(1)}, u32[]{:S(2)}, u32[]{:S(2)}) collective-permute-start(bf16[1024,256]{1,0:T(8,128)(2,1)S(1)} %collective-permute-done.4.refs_6_), channel_id=1, source_target_pairs={{0,1},{1,0},{2,3},{3,2},{4,5},{5,4},{6,7},{7,6},{8,9},{9,8},{10,11... | collective-permute-start | bytes 1572872 | tf_op jit(solution)/shard_map/ppermute | solution.py:400
  40.4 3.8 %collective-permute-start.8 = (bf16[1024,256]{1,0:T(8,128)(2,1)S(1)}, bf16[1024,256]{1,0:T(8,128)(2,1)S(1)}, u32[]{:S(2)}, u32[]{:S(2)}) collective-permute-start(bf16[1024,256]{1,0:T(8,128)(2,1)S(1)} %collective-permute-done.5.refs_4_), channel_id=1, source_target_pairs={{0,1},{1,0},{2,3},{3,2},{4,5},{5,4},{6,7},{7,6},{8,9},{9,8},{10,11... | collective-permute-start | bytes 1572872 | tf_op jit(solution)/shard_map/ppermute | solution.py:400
  40.4 3.8 %collective-permute-start.9 = (bf16[1024,256]{1,0:T(8,128)(2,1)S(1)}, bf16[1024,256]{1,0:T(8,128)(2,1)S(1)}, u32[]{:S(2)}, u32[]{:S(2)}) collective-permute-start(bf16[1024,256]{1,0:T(8,128)(2,1)S(1)} %collective-permute-done.3.refs_5_), channel_id=1, source_target_pairs={{0,1},{1,0},{2,3},{3,2},{4,5},{5,4},{6,7},{7,6},{8,9},{9,8},{10,11... | collective-permute-start | bytes 1572872 | tf_op jit(solution)/shard_map/ppermute | solution.py:400
  40.9 3.3 %slice-start = ((s8[6291456]{0:T(1024)(128)(4,1)}), s8[4194304]{0:T(1024)(128)(4,1)S(1)}, s32[]{:S(2)}) async-start(s8[6291456]{0:T(1024)(128)(4,1)} %bitcast.6), calls=%async_computation.1 | async-start | bytes 8388608
  40.9 3.3 %slice-start.1 = ((s8[6291456]{0:T(1024)(128)(4,1)}), s8[2097152]{0:T(1024)(128)(4,1)S(1)}, s32[]{:S(2)}) async-start(s8[6291456]{0:T(1024)(128)(4,1)} %bitcast.6), calls=%async_computation.2 | async-start | bytes 4194304
  50.2 24.2 %copy-start.1 = (bf16[4096,256]{1,0:T(8,128)(2,1)S(1)}, bf16[4096,256]{1,0:T(8,128)(2,1)}, u32[]{:S(2)}) copy-start(bf16[4096,256]{1,0:T(8,128)(2,1)} %refs_0_.7) | copy-start | bytes 6291460
  65.3 9.2 %collective-permute-start.15 = (bf16[1024,256]{1,0:T(8,128)(2,1)S(1)}, bf16[1024,256]{1,0:T(8,128)(2,1)S(1)}, u32[]{:S(2)}, u32[]{:S(2)}) collective-permute-start(bf16[1024,256]{1,0:T(8,128)(2,1)S(1)} %shard_map.78.refs_1_), channel_id=1, source_target_pairs={{0,1},{1,0},{2,3},{3,2},{4,5},{5,4},{6,7},{7,6},{8,9},{9,8},{10,11... | collective-permute-start | bytes 1572872 | tf_op jit(solution)/shard_map/ppermute | solution.py:400
  66.4 15.0 %collective-permute-start.14 = (bf16[1024,256]{1,0:T(8,128)(2,1)S(1)}, bf16[1024,256]{1,0:T(8,128)(2,1)S(1)}, u32[]{:S(2)}, u32[]{:S(2)}) collective-permute-start(bf16[1024,256]{1,0:T(8,128)(2,1)S(1)} %shard_map.78.refs_1_), channel_id=1, source_target_pairs={{0,8},{1,9},{2,10},{3,11},{4,12},{5,13},{6,14},{7,15},{8,0},{9,1},... | collective-permute-start | bytes 1572872 | tf_op jit(solution)/shard_map/ppermute | solution.py:400
  69.0 14.7 %collective-permute-start.13 = (bf16[1024,256]{1,0:T(8,128)(2,1)S(1)}, bf16[1024,256]{1,0:T(8,128)(2,1)S(1)}, u32[]{:S(2)}, u32[]{:S(2)}) collective-permute-start(bf16[1024,256]{1,0:T(8,128)(2,1)S(1)} %shard_map.78.refs_1_), channel_id=1, source_target_pairs={{0,2},{1,3},{2,0},{3,1},{4,6},{5,7},{6,4},{7,5},{8,10},{9,11},{10,... | collective-permute-start | bytes 1572872 | tf_op jit(solution)/shard_map/ppermute | solution.py:400
  71.8 21.2 %collective-permute-start.19 = (bf16[1024,256]{1,0:T(8,128)(2,1)S(1)}, bf16[1024,256]{1,0:T(8,128)(2,1)S(1)}, u32[]{:S(2)}, u32[]{:S(2)}) collective-permute-start(bf16[1024,256]{1,0:T(8,128)(2,1)S(1)} %shard_map.78.refs_1_), channel_id=1, source_target_pairs={{0,4},{1,5},{2,6},{3,7},{4,8},{5,9},{6,10},{7,11},{8,12},{9,13},{1... | collective-permute-start | bytes 1572872 | tf_op jit(solution)/shard_map/ppermute | solution.py:400
  72.6 20.4 %collective-permute-start.20 = (bf16[1024,256]{1,0:T(8,128)(2,1)S(1)}, bf16[1024,256]{1,0:T(8,128)(2,1)S(1)}, u32[]{:S(2)}, u32[]{:S(2)}) collective-permute-start(bf16[1024,256]{1,0:T(8,128)(2,1)S(1)} %shard_map.78.refs_1_), channel_id=1, source_target_pairs={{0,12},{1,13},{2,14},{3,15},{4,0},{5,1},{6,2},{7,3},{8,4},{9,5},{1... | collective-permute-start | bytes 1572872 | tf_op jit(solution)/shard_map/ppermute | solution.py:400
  83.6 20.6 %collective-permute-start.16 = (bf16[1024,256]{1,0:T(8,128)(2,1)S(1)}, bf16[1024,256]{1,0:T(8,128)(2,1)S(1)}, u32[]{:S(2)}, u32[]{:S(2)}) collective-permute-start(bf16[1024,256]{1,0:T(8,128)(2,1)S(1)} %collective-permute-done.13), channel_id=1, source_target_pairs={{0,4},{1,5},{2,6},{3,7},{4,8},{5,9},{6,10},{7,11},{8,12},{9,13},{1... | collective-permute-start | bytes 1572872 | tf_op jit(solution)/shard_map/ppermute | solution.py:400
  84.6 19.6 %collective-permute-start.17 = (bf16[1024,256]{1,0:T(8,128)(2,1)S(1)}, bf16[1024,256]{1,0:T(8,128)(2,1)S(1)}, u32[]{:S(2)}, u32[]{:S(2)}) collective-permute-start(bf16[1024,256]{1,0:T(8,128)(2,1)S(1)} %collective-permute-done.13), channel_id=1, source_target_pairs={{0,12},{1,13},{2,14},{3,15},{4,0},{5,1},{6,2},{7,3},{8,4},{9,5},{1... | collective-permute-start | bytes 1572872 | tf_op jit(solution)/shard_map/ppermute | solution.py:400
  86.3 17.9 %collective-permute-start.18 = (bf16[1024,256]{1,0:T(8,128)(2,1)S(1)}, bf16[1024,256]{1,0:T(8,128)(2,1)S(1)}, u32[]{:S(2)}, u32[]{:S(2)}) collective-permute-start(bf16[1024,256]{1,0:T(8,128)(2,1)S(1)} %collective-permute-done.14), channel_id=1, source_target_pairs={{0,2},{1,3},{2,0},{3,1},{4,6},{5,7},{6,4},{7,5},{8,10},{9,11},{10,... | collective-permute-start | bytes 1572872 | tf_op jit(solution)/shard_map/ppermute | solution.py:400
  93.1 12.2 %collective-permute-start.24 = (bf16[2048,256]{1,0:T(8,128)(2,1)S(1)}, bf16[2048,256]{1,0:T(8,128)(2,1)S(1)}, u32[]{:S(2)}, u32[]{:S(2)}) collective-permute-start(bf16[2048,256]{1,0:T(8,128)(2,1)S(1)} %constant_dynamic-update-slice_fusion.4.refs_1_), channel_id=1, source_target_pairs={{0,1},{1,0},{2,3},{3,2},{4,5},{5,4},{6,7},{7,6},{8,9},{9,8},{10,11... | collective-permute-start | bytes 3145736 | tf_op jit(solution)/shard_map/ppermute | solution.py:400
  94.1 11.2 %collective-permute-start.25 = (bf16[2048,256]{1,0:T(8,128)(2,1)S(1)}, bf16[2048,256]{1,0:T(8,128)(2,1)S(1)}, u32[]{:S(2)}, u32[]{:S(2)}) collective-permute-start(bf16[2048,256]{1,0:T(8,128)(2,1)S(1)} %constant_dynamic-update-slice_fusion.6.refs_2_), channel_id=1, source_target_pairs={{0,1},{1,0},{2,3},{3,2},{4,5},{5,4},{6,7},{7,6},{8,9},{9,8},{10,11... | collective-permute-start | bytes 3145736 | tf_op jit(solution)/shard_map/ppermute | solution.py:400
  104.2 2.2 %collective-permute-start.21 = (bf16[1024,256]{1,0:T(8,128)(2,1)S(1)}, bf16[1024,256]{1,0:T(8,128)(2,1)S(1)}, u32[]{:S(2)}, u32[]{:S(2)}) collective-permute-start(bf16[1024,256]{1,0:T(8,128)(2,1)S(1)} %collective-permute-done.18.refs_3_), channel_id=1, source_target_pairs={{0,1},{1,0},{2,3},{3,2},{4,5},{5,4},{6,7},{7,6},{8,9},{9,8},{10,11... | collective-permute-start | bytes 1572872 | tf_op jit(solution)/shard_map/ppermute | solution.py:400
  104.7 2.3 %collective-permute-start.22 = (bf16[1024,256]{1,0:T(8,128)(2,1)S(1)}, bf16[1024,256]{1,0:T(8,128)(2,1)S(1)}, u32[]{:S(2)}, u32[]{:S(2)}) collective-permute-start(bf16[1024,256]{1,0:T(8,128)(2,1)S(1)} %collective-permute-done.16.refs_4_), channel_id=1, source_target_pairs={{0,1},{1,0},{2,3},{3,2},{4,5},{5,4},{6,7},{7,6},{8,9},{9,8},{10,11... | collective-permute-start | bytes 1572872 | tf_op jit(solution)/shard_map/ppermute | solution.py:400
  104.8 3.0 %collective-permute-start.23 = (bf16[1024,256]{1,0:T(8,128)(2,1)S(1)}, bf16[1024,256]{1,0:T(8,128)(2,1)S(1)}, u32[]{:S(2)}, u32[]{:S(2)}) collective-permute-start(bf16[1024,256]{1,0:T(8,128)(2,1)S(1)} %collective-permute-done.17.refs_5_), channel_id=1, source_target_pairs={{0,1},{1,0},{2,3},{3,2},{4,5},{5,4},{6,7},{7,6},{8,9},{9,8},{10,11... | collective-permute-start | bytes 1572872 | tf_op jit(solution)/shard_map/ppermute | solution.py:400

commit v7 on v6

--- a/solution.py
+++ b/solution.py
@@ -195,7 +195,7 @@
         def strided(s, t):
             return proj[s * halves + g, pl.ds(PAD + t, SUBS, stride=pitch), :]
 
-        unroll = 8
+        unroll = 16
 
         def steps(i, states, masked=False):
             begin = i * unroll
@@ -214,6 +214,9 @@
             kv = [short[1][u] * short[2][u] for u in range(unroll)]
             if masked:
                 kv = [jnp.where(head, 0.0, v) if u < REACH else v for u, v in enumerate(kv)]
+            for u in range(unroll):
+                place = pl.ds(pl.multiple_of((begin + u) * SUBS, SUBS), SUBS)
+                gate[place, lanes] = short[0][u]
             outs = [None] * unroll
             later = []
             for first in range(0, MODES, GROUP):
@@ -228,7 +231,6 @@
                 later.extend(now)
             for u in range(unroll):
                 place = pl.ds(pl.multiple_of((begin + u) * SUBS, SUBS), SUBS)
-                gate[place, lanes] = short[0][u]
                 local[place, lanes] = outs[u]
             return later
 

time: 110 us -> 109 us (level)
  no operation moved by 1% of the time
where the time goes in v7:
time: 109 us
  starting transfers between devices  34.9 us (32%)
  waiting for transfers between devices  34.9 us (32%)
  Pallas kernels  17.5 us (16%)
  blocking collectives  13.3 us (12%)
  local copies, waits for them, and re-layouts  8.07 us (7%)
    ppermute x26, starting transfers between devices, shifted(): return lax.ppermute(x, 'tp', pairs)  34.9 us
    ppermute x26, waiting for transfers between devices, shifted(): return lax.ppermute(x, 'tp', pairs)  34.9 us
    pallas_call x10, Pallas kernels, call(): pl.pallas_call(kernel, out_shape=outs, in_specs=specs, out_specs=[VMEM] *...  17.5 us
    all_to_all x1, blocking collectives, body(): loads = lax.all_to_all(load, 'ctx', 0, 0, tiled=True)  13.3 us
    unnamed x19, local copies, waits for them, and re-layouts  7.19 us
  transfers between devices with their start and end apart: 26, of which 10 were waited for; matrix products, arithmetic and copies ran while one was open for 3% of the time, Pallas kernels for 8%

profile of v7, /device:TPU:1, one launch (start us, length us, event | category | flops | bytes accessed | tf_op | source)
XLA Modules:
  0.0 108.9 jit_solution(11643306636636629731)
XLA Ops:
  0.0 1.4 %collective-permute-start.2 = (bf16[1024,256]{1,0:T(8,128)(2,1)}, bf16[1024,256]{1,0:T(8,128)(2,1)S(1)}, u32[]{:S(2)}, u32[]{:S(2)}) collective-permute-start(bf16[1024,256]{1,0:T(8,128)(2,1)} %refs_5_.1), channel_id=1, source_target_pairs={{0,1},{1,0},{2,3},{3,2},{4,5},{5,4},{6,7},{7,6},{8,9},{9,8},{10,11... | collective-permute-start | bytes 1572872 | tf_op jit(solution)/shard_map/ppermute | solution.py:402
  1.4 3.0 %collective-permute-start.1 = (bf16[1024,256]{1,0:T(8,128)(2,1)}, bf16[1024,256]{1,0:T(8,128)(2,1)S(1)}, u32[]{:S(2)}, u32[]{:S(2)}) collective-permute-start(bf16[1024,256]{1,0:T(8,128)(2,1)} %refs_5_.1), channel_id=1, source_target_pairs={{0,8},{1,9},{2,10},{3,11},{4,12},{5,13},{6,14},{7,15},{8,0},{9,1},... | collective-permute-start | bytes 1572872 | tf_op jit(solution)/shard_map/ppermute | solution.py:402
  4.4 3.6 %collective-permute-start = (bf16[1024,256]{1,0:T(8,128)(2,1)}, bf16[1024,256]{1,0:T(8,128)(2,1)S(1)}, u32[]{:S(2)}, u32[]{:S(2)}) collective-permute-start(bf16[1024,256]{1,0:T(8,128)(2,1)} %refs_5_.1), channel_id=1, source_target_pairs={{0,2},{1,3},{2,0},{3,1},{4,6},{5,7},{6,4},{7,5},{8,10},{9,11},{10,... | collective-permute-start | bytes 1572872 | tf_op jit(solution)/shard_map/ppermute | solution.py:402
  8.0 0.4 collective-permute-start.6
  8.4 2.3 %collective-permute-start.7 = (bf16[1024,256]{1,0:T(8,128)(2,1)}, bf16[1024,256]{1,0:T(8,128)(2,1)S(1)}, u32[]{:S(2)}, u32[]{:S(2)}) collective-permute-start(bf16[1024,256]{1,0:T(8,128)(2,1)} %refs_5_.1), channel_id=1, source_target_pairs={{0,12},{1,13},{2,14},{3,15},{4,0},{5,1},{6,2},{7,3},{8,4},{9,5},{1... | collective-permute-start | bytes 1572872 | tf_op jit(solution)/shard_map/ppermute | solution.py:402
  10.7 0.7 copy.14.refs_2_
  11.5 0.7 copy-done.3
  12.2 0.7 copy-done.4
  13.0 0.7 reshape.3.refs_0_
  13.7 2.8 %copy-done = bf16[4096,3,256]{2,0,1:T(8,128)(2,1)S(1)} copy-done((bf16[4096,3,256]{2,0,1:T(8,128)(2,1)S(1)}, bf16[4096,3,256]{2,0,1:T(8,128)(2,1)}, u32[]{:S(2)}) %copy-start) | copy-done | bytes 6291480
  16.5 1.0 copy-done.2
  17.6 1.0 shard_map.74
  18.6 1.8 %collective-permute-done = bf16[1024,256]{1,0:T(8,128)(2,1)S(1)} collective-permute-done((bf16[1024,256]{1,0:T(8,128)(2,1)}, bf16[1024,256]{1,0:T(8,128)(2,1)S(1)}, u32[]{:S(2)}, u32[]{:S(2)}) %collective-permute-start) | collective-permute-done | bytes 524320 | tf_op jit(solution)/shard_map/ppermute | solution.py:402
  20.4 0.4 collective-permute-start.3
  20.8 2.3 %collective-permute-start.4 = (bf16[1024,256]{1,0:T(8,128)(2,1)S(1)}, bf16[1024,256]{1,0:T(8,128)(2,1)S(1)}, u32[]{:S(2)}, u32[]{:S(2)}) collective-permute-start(bf16[1024,256]{1,0:T(8,128)(2,1)S(1)} %collective-permute-done), channel_id=1, source_target_pairs={{0,12},{1,13},{2,14},{3,15},{4,0},{5,1},{6,2},{7,3},{8,4},{9,5},{1... | collective-permute-start | bytes 1572872 | tf_op jit(solution)/shard_map/ppermute | solution.py:402
  23.0 2.7 %collective-permute-start.5 = (bf16[1024,256]{1,0:T(8,128)(2,1)S(1)}, bf16[1024,256]{1,0:T(8,128)(2,1)S(1)}, u32[]{:S(2)}, u32[]{:S(2)}) collective-permute-start(bf16[1024,256]{1,0:T(8,128)(2,1)S(1)} %collective-permute-done.1), channel_id=1, source_target_pairs={{0,2},{1,3},{2,0},{3,1},{4,6},{5,7},{6,4},{7,5},{8,10},{9,11},{10,... | collective-permute-start | bytes 1572872 | tf_op jit(solution)/shard_map/ppermute | solution.py:402
  25.8 2.5 %collective-permute-done.6 = bf16[1024,256]{1,0:T(8,128)(2,1)} collective-permute-done((bf16[1024,256]{1,0:T(8,128)(2,1)}, bf16[1024,256]{1,0:T(8,128)(2,1)}, u32[]{:S(2)}, u32[]{:S(2)}) %collective-permute-start.6) | collective-permute-done | bytes 524320 | tf_op jit(solution)/shard_map/ppermute | solution.py:402
  28.4 1.1 constant_dynamic-update-slice_fusion.3
  29.5 0.7 collective-permute-start.11
  30.2 2.0 %shard_map.75 = (f32[1024,768]{1,0:T(8,128)S(1)}, f32[1024,128]{1,0:T(8,128)S(1)}) custom-call(f32[16,256]{1,0:T(8,128)S(1)} %reshape.3.refs_0_, bf16[3,4096,256]{2,1,0:T(8,128)(2,1)S(1)} %bitcast.4, bf16[2048,256]{1,0:T(8,128)(2,1)S(1)} %constant_dynamic-update-slice_fusion.refs_2_, ...), custom_call_target="tpu_custom_call", output_to_operand_aliasing={{0}: (4, {}), {1}: (5, {})} | custom-call | flops 1 | bytes 1 | tf_op jit(solution)/shard_map/pallas_call | solution.py:25
  32.3 7.2 %collective-permute-done.3.refs_5_ = bf16[1024,256]{1,0:T(8,128)(2,1)S(1)} collective-permute-done((bf16[1024,256]{1,0:T(8,128)(2,1)S(1)}, bf16[1024,256]{1,0:T(8,128)(2,1)S(1)}, u32[]{:S(2)}, u32[]{:S(2)}) %collective-permute-start.3) | collective-permute-done | bytes 524320 | tf_op jit(solution)/shard_map/ppermute | solution.py:402
  39.6 0.8 collective-permute-start.10
  40.4 0.5 collective-permute-start.9
  41.0 3.3 %shard_map.76 = (f32[1024,768]{1,0:T(8,128)S(1)}, f32[1024,128]{1,0:T(8,128)S(1)}) custom-call(f32[16,256]{1,0:T(8,128)S(1)} %reshape.3.refs_0_, bf16[3,4096,256]{2,1,0:T(8,128)(2,1)S(1)} %bitcast.5, bf16[2048,256]{1,0:T(8,128)(2,1)S(1)} %collective-permute-done.11.refs_2_, ...), custom_call_target="tpu_custom_call", output_to_operand_aliasing={{0}: (7, {}), {1}: (8, {})} | custom-call | flops 1 | bytes 1 | tf_op jit(solution)/shard_map/pallas_call | solution.py:25
  44.3 5.7 %shard_map.77 = (f32[1024,256]{1,0:T(8,128)S(1)}, f32[1024,256]{1,0:T(8,128)S(1)}, f32[128,256]{1,0:T(8,128)S(1)}, bf16[8,80,256]{2,1,0:T(8,128)(2,1)S(1)}) custom-call(f32[16,256]{1,0:T(8,128)S(1)} %reshape.3.refs_0_, bf16[3,4096,256]{2,1,0:T(8,128)(2,1)S(1)} %bitcast.8, bf16[1024,256]{1,0:T(8,128)(2,1)S(1)} %collective-permute-done.8.refs_2_, ...), custom_call_target="tpu_custom_call" | custom-call | flops 1 | bytes 1 | tf_op jit(solution)/shard_map/pallas_call | solution.py:25
  50.0 13.3 %all_to_all.5.refs_0_ = bf16[8,80,256]{2,1,0:T(8,128)(2,1)S(1)} all-to-all(bf16[8,80,256]{2,1,0:T(8,128)(2,1)S(1)} %get-tuple-element.44), channel_id=1, replica_groups=mesh['ctx'=8,'tp'=16] {'ctx'}, dimensions={0} | all-to-all | bytes 655360 | tf_op jit(solution)/shard_map/all_to_all | solution.py:487
  63.3 1.7 %shard_map.78.refs_1_ = bf16[1024,256]{1,0:T(8,128)(2,1)S(1)} custom-call(bf16[8,80,256]{2,1,0:T(8,128)(2,1)S(1)} %all_to_all.5.refs_0_, f32[1024,256]{1,0:T(8,128)S(1)} %get-tuple-element.45.refs_1_, f32[1024,256]{1,0:T(8,128)S(1)} %get-tuple-element.46.refs_2_, f32[128,256]{1,0:T(8,128)S(1)} %get-tuple-element.47.refs_3_, ...), custom_call_target="tpu_custom_call" | custom-call | flops 1 | bytes 1 | tf_op jit(solution)/shard_map/pallas_call | solution.py:25
  65.0 1.1 %collective-permute-start.15 = (bf16[1024,256]{1,0:T(8,128)(2,1)S(1)}, bf16[1024,256]{1,0:T(8,128)(2,1)S(1)}, u32[]{:S(2)}, u32[]{:S(2)}) collective-permute-start(bf16[1024,256]{1,0:T(8,128)(2,1)S(1)} %shard_map.78.refs_1_), channel_id=1, source_target_pairs={{0,1},{1,0},{2,3},{3,2},{4,5},{5,4},{6,7},{7,6},{8,9},{9,8},{10,11... | collective-permute-start | bytes 1572872 | tf_op jit(solution)/shard_map/ppermute | solution.py:402
  66.1 2.6 %collective-permute-start.14 = (bf16[1024,256]{1,0:T(8,128)(2,1)S(1)}, bf16[1024,256]{1,0:T(8,128)(2,1)S(1)}, u32[]{:S(2)}, u32[]{:S(2)}) collective-permute-start(bf16[1024,256]{1,0:T(8,128)(2,1)S(1)} %shard_map.78.refs_1_), channel_id=1, source_target_pairs={{0,8},{1,9},{2,10},{3,11},{4,12},{5,13},{6,14},{7,15},{8,0},{9,1},... | collective-permute-start | bytes 1572872 | tf_op jit(solution)/shard_map/ppermute | solution.py:402
  68.7 2.8 %collective-permute-start.13 = (bf16[1024,256]{1,0:T(8,128)(2,1)S(1)}, bf16[1024,256]{1,0:T(8,128)(2,1)S(1)}, u32[]{:S(2)}, u32[]{:S(2)}) collective-permute-start(bf16[1024,256]{1,0:T(8,128)(2,1)S(1)} %shard_map.78.refs_1_), channel_id=1, source_target_pairs={{0,2},{1,3},{2,0},{3,1},{4,6},{5,7},{6,4},{7,5},{8,10},{9,11},{10,... | collective-permute-start | bytes 1572872 | tf_op jit(solution)/shard_map/ppermute | solution.py:402
  71.5 0.8 collective-permute-start.19
  72.4 1.8 %collective-permute-start.20 = (bf16[1024,256]{1,0:T(8,128)(2,1)S(1)}, bf16[1024,256]{1,0:T(8,128)(2,1)S(1)}, u32[]{:S(2)}, u32[]{:S(2)}) collective-permute-start(bf16[1024,256]{1,0:T(8,128)(2,1)S(1)} %shard_map.78.refs_1_), channel_id=1, source_target_pairs={{0,12},{1,13},{2,14},{3,15},{4,0},{5,1},{6,2},{7,3},{8,4},{9,5},{1... | collective-permute-start | bytes 1572872 | tf_op jit(solution)/shard_map/ppermute | solution.py:402
  74.2 0.5 shard_map.79.refs_3_
  74.7 6.5 %collective-permute-done.14 = bf16[1024,256]{1,0:T(8,128)(2,1)S(1)} collective-permute-done((bf16[1024,256]{1,0:T(8,128)(2,1)S(1)}, bf16[1024,256]{1,0:T(8,128)(2,1)S(1)}, u32[]{:S(2)}, u32[]{:S(2)}) %collective-permute-start.14) | collective-permute-done | bytes 524320 | tf_op jit(solution)/shard_map/ppermute | solution.py:402
  81.2 2.2 %collective-permute-done.13 = bf16[1024,256]{1,0:T(8,128)(2,1)S(1)} collective-permute-done((bf16[1024,256]{1,0:T(8,128)(2,1)S(1)}, bf16[1024,256]{1,0:T(8,128)(2,1)S(1)}, u32[]{:S(2)}, u32[]{:S(2)}) %collective-permute-start.13) | collective-permute-done | bytes 524320 | tf_op jit(solution)/shard_map/ppermute | solution.py:402
  83.3 1.0 collective-permute-start.16
  84.4 1.7 %collective-permute-start.17 = (bf16[1024,256]{1,0:T(8,128)(2,1)S(1)}, bf16[1024,256]{1,0:T(8,128)(2,1)S(1)}, u32[]{:S(2)}, u32[]{:S(2)}) collective-permute-start(bf16[1024,256]{1,0:T(8,128)(2,1)S(1)} %collective-permute-done.13), channel_id=1, source_target_pairs={{0,12},{1,13},{2,14},{3,15},{4,0},{5,1},{6,2},{7,3},{8,4},{9,5},{1... | collective-permute-start | bytes 1572872 | tf_op jit(solution)/shard_map/ppermute | solution.py:402
  86.0 2.8 %collective-permute-start.18 = (bf16[1024,256]{1,0:T(8,128)(2,1)S(1)}, bf16[1024,256]{1,0:T(8,128)(2,1)S(1)}, u32[]{:S(2)}, u32[]{:S(2)}) collective-permute-start(bf16[1024,256]{1,0:T(8,128)(2,1)S(1)} %collective-permute-done.14), channel_id=1, source_target_pairs={{0,2},{1,3},{2,0},{3,1},{4,6},{5,7},{6,4},{7,5},{8,10},{9,11},{10,... | collective-permute-start | bytes 1572872 | tf_op jit(solution)/shard_map/ppermute | solution.py:402
  88.9 3.8 %collective-permute-done.19 = bf16[1024,256]{1,0:T(8,128)(2,1)S(1)} collective-permute-done((bf16[1024,256]{1,0:T(8,128)(2,1)S(1)}, bf16[1024,256]{1,0:T(8,128)(2,1)S(1)}, u32[]{:S(2)}, u32[]{:S(2)}) %collective-permute-start.19) | collective-permute-done | bytes 524320 | tf_op jit(solution)/shard_map/ppermute | solution.py:402
  92.8 1.0 collective-permute-start.24
  93.9 0.7 shard_map.80.refs_6_
  94.6 9.3 %collective-permute-done.16.refs_4_ = bf16[1024,256]{1,0:T(8,128)(2,1)S(1)} collective-permute-done((bf16[1024,256]{1,0:T(8,128)(2,1)S(1)}, bf16[1024,256]{1,0:T(8,128)(2,1)S(1)}, u32[]{:S(2)}, u32[]{:S(2)}) %collective-permute-start.16) | collective-permute-done | bytes 524320 | tf_op jit(solution)/shard_map/ppermute | solution.py:402
  104.0 0.5 collective-permute-start.21
  104.6 0.4 collective-permute-start.23
  105.0 1.1 %shard_map.81.refs_4_ = f32[1024,256]{1,0:T(8,128)S(1)} custom-call(bf16[4096,256]{1,0:T(8,128)(2,1)S(1)} %copy-done.1, bf16[2048,256]{1,0:T(8,128)(2,1)S(1)} %collective-permute-done.24.refs_1_, bf16[2048,256]{1,0:T(8,128)(2,1)S(1)} %collective-permute-done.25.refs_2_, ...), custom_call_target="tpu_custom_call", output_to_operand_aliasing={{}: (6, {})} | custom-call | flops 1 | bytes 1 | tf_op jit(solution)/shard_map/pallas_call | solution.py:25
  106.1 0.6 collective-permute-done.22.refs_2_
  106.8 0.7 collective-permute-done.23.refs_3_
  107.5 1.4 %shard_map.82 = bf16[1024,256]{1,0:T(8,128)(2,1)} custom-call(bf16[4096,256]{1,0:T(8,128)(2,1)S(1)} %copy-done.1, bf16[1024,256]{1,0:T(8,128)(2,1)S(1)} %collective-permute-done.21.refs_1_, bf16[1024,256]{1,0:T(8,128)(2,1)S(1)} %collective-permute-done.22.refs_2_, bf16[1024,256]{1,0:T(8,128)(2,1)S(1)} %collective-permute-done.23.refs_3_, ...), custom_call_target="tpu_custom_call" | custom-call | flops 1 | bytes 1 | tf_op jit(solution)/shard_map/pallas_call | solution.py:25
  (40 shorter events, 0.8 us)
Async XLA Ops:
  0.0 13.7 %collective-permute-start.2 = (bf16[1024,256]{1,0:T(8,128)(2,1)}, bf16[1024,256]{1,0:T(8,128)(2,1)S(1)}, u32[]{:S(2)}, u32[]{:S(2)}) collective-permute-start(bf16[1024,256]{1,0:T(8,128)(2,1)} %refs_5_.1), channel_id=1, source_target_pairs={{0,1},{1,0},{2,3},{3,2},{4,5},{5,4},{6,7},{7,6},{8,9},{9,8},{10,11... | collective-permute-start | bytes 1572872 | tf_op jit(solution)/shard_map/ppermute | solution.py:402
  1.4 17.1 %collective-permute-start.1 = (bf16[1024,256]{1,0:T(8,128)(2,1)}, bf16[1024,256]{1,0:T(8,128)(2,1)S(1)}, u32[]{:S(2)}, u32[]{:S(2)}) collective-permute-start(bf16[1024,256]{1,0:T(8,128)(2,1)} %refs_5_.1), channel_id=1, source_target_pairs={{0,8},{1,9},{2,10},{3,11},{4,12},{5,13},{6,14},{7,15},{8,0},{9,1},... | collective-permute-start | bytes 1572872 | tf_op jit(solution)/shard_map/ppermute | solution.py:402
  4.4 15.9 %collective-permute-start = (bf16[1024,256]{1,0:T(8,128)(2,1)}, bf16[1024,256]{1,0:T(8,128)(2,1)S(1)}, u32[]{:S(2)}, u32[]{:S(2)}) collective-permute-start(bf16[1024,256]{1,0:T(8,128)(2,1)} %refs_5_.1), channel_id=1, source_target_pairs={{0,2},{1,3},{2,0},{3,1},{4,6},{5,7},{6,4},{7,5},{8,10},{9,11},{10,... | collective-permute-start | bytes 1572872 | tf_op jit(solution)/shard_map/ppermute | solution.py:402
  8.0 20.3 %collective-permute-start.6 = (bf16[1024,256]{1,0:T(8,128)(2,1)}, bf16[1024,256]{1,0:T(8,128)(2,1)}, u32[]{:S(2)}, u32[]{:S(2)}) collective-permute-start(bf16[1024,256]{1,0:T(8,128)(2,1)} %refs_5_.1), channel_id=1, source_target_pairs={{0,4},{1,5},{2,6},{3,7},{4,8},{5,9},{6,10},{7,11},{8,12},{9,13},{1... | collective-permute-start | bytes 1572872 | tf_op jit(solution)/shard_map/ppermute | solution.py:402
  8.4 21.0 %collective-permute-start.7 = (bf16[1024,256]{1,0:T(8,128)(2,1)}, bf16[1024,256]{1,0:T(8,128)(2,1)S(1)}, u32[]{:S(2)}, u32[]{:S(2)}) collective-permute-start(bf16[1024,256]{1,0:T(8,128)(2,1)} %refs_5_.1), channel_id=1, source_target_pairs={{0,12},{1,13},{2,14},{3,15},{4,0},{5,1},{6,2},{7,3},{8,4},{9,5},{1... | collective-permute-start | bytes 1572872 | tf_op jit(solution)/shard_map/ppermute | solution.py:402
  11.4 0.7 copy-start.3
  12.2 0.7 copy-start.4
  13.7 2.8 %copy-start = (bf16[4096,3,256]{2,0,1:T(8,128)(2,1)S(1)}, bf16[4096,3,256]{2,0,1:T(8,128)(2,1)}, u32[]{:S(2)}) copy-start(bf16[4096,3,256]{2,0,1:T(8,128)(2,1)} %param.9) | copy-start | bytes 18874372
  16.5 1.0 copy-start.2
  20.4 19.1 %collective-permute-start.3 = (bf16[1024,256]{1,0:T(8,128)(2,1)S(1)}, bf16[1024,256]{1,0:T(8,128)(2,1)S(1)}, u32[]{:S(2)}, u32[]{:S(2)}) collective-permute-start(bf16[1024,256]{1,0:T(8,128)(2,1)S(1)} %collective-permute-done), channel_id=1, source_target_pairs={{0,4},{1,5},{2,6},{3,7},{4,8},{5,9},{6,10},{7,11},{8,12},{9,13},{1... | collective-permute-start | bytes 1572872 | tf_op jit(solution)/shard_map/ppermute | solution.py:402
  20.8 18.9 %collective-permute-start.4 = (bf16[1024,256]{1,0:T(8,128)(2,1)S(1)}, bf16[1024,256]{1,0:T(8,128)(2,1)S(1)}, u32[]{:S(2)}, u32[]{:S(2)}) collective-permute-start(bf16[1024,256]{1,0:T(8,128)(2,1)S(1)} %collective-permute-done), channel_id=1, source_target_pairs={{0,12},{1,13},{2,14},{3,15},{4,0},{5,1},{6,2},{7,3},{8,4},{9,5},{1... | collective-permute-start | bytes 1572872 | tf_op jit(solution)/shard_map/ppermute | solution.py:402
  23.0 16.6 %collective-permute-start.5 = (bf16[1024,256]{1,0:T(8,128)(2,1)S(1)}, bf16[1024,256]{1,0:T(8,128)(2,1)S(1)}, u32[]{:S(2)}, u32[]{:S(2)}) collective-permute-start(bf16[1024,256]{1,0:T(8,128)(2,1)S(1)} %collective-permute-done.1), channel_id=1, source_target_pairs={{0,2},{1,3},{2,0},{3,1},{4,6},{5,7},{6,4},{7,5},{8,10},{9,11},{10,... | collective-permute-start | bytes 1572872 | tf_op jit(solution)/shard_map/ppermute | solution.py:402
  29.5 11.4 %collective-permute-start.11 = (bf16[2048,256]{1,0:T(8,128)(2,1)S(1)}, bf16[2048,256]{1,0:T(8,128)(2,1)S(1)}, u32[]{:S(2)}, u32[]{:S(2)}) collective-permute-start(bf16[2048,256]{1,0:T(8,128)(2,1)S(1)} %constant_dynamic-update-slice_fusion.refs_2_), channel_id=1, source_target_pairs={{0,1},{1,0},{2,3},{3,2},{4,5},{5,4},{6,7},{7,6},{8,9},{9,8},{10,11... | collective-permute-start | bytes 3145736 | tf_op jit(solution)/shard_map/ppermute | solution.py:402
  30.2 10.8 %collective-permute-start.12 = (bf16[2048,256]{1,0:T(8,128)(2,1)S(1)}, bf16[2048,256]{1,0:T(8,128)(2,1)S(1)}, u32[]{:S(2)}, u32[]{:S(2)}) collective-permute-start(bf16[2048,256]{1,0:T(8,128)(2,1)S(1)} %constant_dynamic-update-slice_fusion.2.refs_3_), channel_id=1, source_target_pairs={{0,1},{1,0},{2,3},{3,2},{4,5},{5,4},{6,7},{7,6},{8,9},{9,8},{10,11... | collective-permute-start | bytes 3145736 | tf_op jit(solution)/shard_map/ppermute | solution.py:402
  39.6 4.6 %collective-permute-start.10 = (bf16[1024,256]{1,0:T(8,128)(2,1)S(1)}, bf16[1024,256]{1,0:T(8,128)(2,1)S(1)}, u32[]{:S(2)}, u32[]{:S(2)}) collective-permute-start(bf16[1024,256]{1,0:T(8,128)(2,1)S(1)} %collective-permute-done.4.refs_6_), channel_id=1, source_target_pairs={{0,1},{1,0},{2,3},{3,2},{4,5},{5,4},{6,7},{7,6},{8,9},{9,8},{10,11... | collective-permute-start | bytes 1572872 | tf_op jit(solution)/shard_map/ppermute | solution.py:402
  40.4 3.8 %collective-permute-start.8 = (bf16[1024,256]{1,0:T(8,128)(2,1)S(1)}, bf16[1024,256]{1,0:T(8,128)(2,1)S(1)}, u32[]{:S(2)}, u32[]{:S(2)}) collective-permute-start(bf16[1024,256]{1,0:T(8,128)(2,1)S(1)} %collective-permute-done.5.refs_4_), channel_id=1, source_target_pairs={{0,1},{1,0},{2,3},{3,2},{4,5},{5,4},{6,7},{7,6},{8,9},{9,8},{10,11... | collective-permute-start | bytes 1572872 | tf_op jit(solution)/shard_map/ppermute | solution.py:402
  40.4 3.8 %collective-permute-start.9 = (bf16[1024,256]{1,0:T(8,128)(2,1)S(1)}, bf16[1024,256]{1,0:T(8,128)(2,1)S(1)}, u32[]{:S(2)}, u32[]{:S(2)}) collective-permute-start(bf16[1024,256]{1,0:T(8,128)(2,1)S(1)} %collective-permute-done.3.refs_5_), channel_id=1, source_target_pairs={{0,1},{1,0},{2,3},{3,2},{4,5},{5,4},{6,7},{7,6},{8,9},{9,8},{10,11... | collective-permute-start | bytes 1572872 | tf_op jit(solution)/shard_map/ppermute | solution.py:402
  40.9 3.3 %slice-start = ((s8[6291456]{0:T(1024)(128)(4,1)}), s8[4194304]{0:T(1024)(128)(4,1)S(1)}, s32[]{:S(2)}) async-start(s8[6291456]{0:T(1024)(128)(4,1)} %bitcast.6), calls=%async_computation.1 | async-start | bytes 8388608
  40.9 3.3 %slice-start.1 = ((s8[6291456]{0:T(1024)(128)(4,1)}), s8[2097152]{0:T(1024)(128)(4,1)S(1)}, s32[]{:S(2)}) async-start(s8[6291456]{0:T(1024)(128)(4,1)} %bitcast.6), calls=%async_computation.2 | async-start | bytes 4194304
  50.0 24.2 %copy-start.1 = (bf16[4096,256]{1,0:T(8,128)(2,1)S(1)}, bf16[4096,256]{1,0:T(8,128)(2,1)}, u32[]{:S(2)}) copy-start(bf16[4096,256]{1,0:T(8,128)(2,1)} %refs_0_.7) | copy-start | bytes 6291460
  65.0 9.2 %collective-permute-start.15 = (bf16[1024,256]{1,0:T(8,128)(2,1)S(1)}, bf16[1024,256]{1,0:T(8,128)(2,1)S(1)}, u32[]{:S(2)}, u32[]{:S(2)}) collective-permute-start(bf16[1024,256]{1,0:T(8,128)(2,1)S(1)} %shard_map.78.refs_1_), channel_id=1, source_target_pairs={{0,1},{1,0},{2,3},{3,2},{4,5},{5,4},{6,7},{7,6},{8,9},{9,8},{10,11... | collective-permute-start | bytes 1572872 | tf_op jit(solution)/shard_map/ppermute | solution.py:402
  66.1 15.0 %collective-permute-start.14 = (bf16[1024,256]{1,0:T(8,128)(2,1)S(1)}, bf16[1024,256]{1,0:T(8,128)(2,1)S(1)}, u32[]{:S(2)}, u32[]{:S(2)}) collective-permute-start(bf16[1024,256]{1,0:T(8,128)(2,1)S(1)} %shard_map.78.refs_1_), channel_id=1, source_target_pairs={{0,8},{1,9},{2,10},{3,11},{4,12},{5,13},{6,14},{7,15},{8,0},{9,1},... | collective-permute-start | bytes 1572872 | tf_op jit(solution)/shard_map/ppermute | solution.py:402
  68.7 14.7 %collective-permute-start.13 = (bf16[1024,256]{1,0:T(8,128)(2,1)S(1)}, bf16[1024,256]{1,0:T(8,128)(2,1)S(1)}, u32[]{:S(2)}, u32[]{:S(2)}) collective-permute-start(bf16[1024,256]{1,0:T(8,128)(2,1)S(1)} %shard_map.78.refs_1_), channel_id=1, source_target_pairs={{0,2},{1,3},{2,0},{3,1},{4,6},{5,7},{6,4},{7,5},{8,10},{9,11},{10,... | collective-permute-start | bytes 1572872 | tf_op jit(solution)/shard_map/ppermute | solution.py:402
  71.5 21.2 %collective-permute-start.19 = (bf16[1024,256]{1,0:T(8,128)(2,1)S(1)}, bf16[1024,256]{1,0:T(8,128)(2,1)S(1)}, u32[]{:S(2)}, u32[]{:S(2)}) collective-permute-start(bf16[1024,256]{1,0:T(8,128)(2,1)S(1)} %shard_map.78.refs_1_), channel_id=1, source_target_pairs={{0,4},{1,5},{2,6},{3,7},{4,8},{5,9},{6,10},{7,11},{8,12},{9,13},{1... | collective-permute-start | bytes 1572872 | tf_op jit(solution)/shard_map/ppermute | solution.py:402
  72.4 20.4 %collective-permute-start.20 = (bf16[1024,256]{1,0:T(8,128)(2,1)S(1)}, bf16[1024,256]{1,0:T(8,128)(2,1)S(1)}, u32[]{:S(2)}, u32[]{:S(2)}) collective-permute-start(bf16[1024,256]{1,0:T(8,128)(2,1)S(1)} %shard_map.78.refs_1_), channel_id=1, source_target_pairs={{0,12},{1,13},{2,14},{3,15},{4,0},{5,1},{6,2},{7,3},{8,4},{9,5},{1... | collective-permute-start | bytes 1572872 | tf_op jit(solution)/shard_map/ppermute | solution.py:402
  83.3 20.6 %collective-permute-start.16 = (bf16[1024,256]{1,0:T(8,128)(2,1)S(1)}, bf16[1024,256]{1,0:T(8,128)(2,1)S(1)}, u32[]{:S(2)}, u32[]{:S(2)}) collective-permute-start(bf16[1024,256]{1,0:T(8,128)(2,1)S(1)} %collective-permute-done.13), channel_id=1, source_target_pairs={{0,4},{1,5},{2,6},{3,7},{4,8},{5,9},{6,10},{7,11},{8,12},{9,13},{1... | collective-permute-start | bytes 1572872 | tf_op jit(solution)/shard_map/ppermute | solution.py:402
  84.4 19.6 %collective-permute-start.17 = (bf16[1024,256]{1,0:T(8,128)(2,1)S(1)}, bf16[1024,256]{1,0:T(8,128)(2,1)S(1)}, u32[]{:S(2)}, u32[]{:S(2)}) collective-permute-start(bf16[1024,256]{1,0:T(8,128)(2,1)S(1)} %collective-permute-done.13), channel_id=1, source_target_pairs={{0,12},{1,13},{2,14},{3,15},{4,0},{5,1},{6,2},{7,3},{8,4},{9,5},{1... | collective-permute-start | bytes 1572872 | tf_op jit(solution)/shard_map/ppermute | solution.py:402
  86.0 17.9 %collective-permute-start.18 = (bf16[1024,256]{1,0:T(8,128)(2,1)S(1)}, bf16[1024,256]{1,0:T(8,128)(2,1)S(1)}, u32[]{:S(2)}, u32[]{:S(2)}) collective-permute-start(bf16[1024,256]{1,0:T(8,128)(2,1)S(1)} %collective-permute-done.14), channel_id=1, source_target_pairs={{0,2},{1,3},{2,0},{3,1},{4,6},{5,7},{6,4},{7,5},{8,10},{9,11},{10,... | collective-permute-start | bytes 1572872 | tf_op jit(solution)/shard_map/ppermute | solution.py:402
  92.8 12.2 %collective-permute-start.24 = (bf16[2048,256]{1,0:T(8,128)(2,1)S(1)}, bf16[2048,256]{1,0:T(8,128)(2,1)S(1)}, u32[]{:S(2)}, u32[]{:S(2)}) collective-permute-start(bf16[2048,256]{1,0:T(8,128)(2,1)S(1)} %constant_dynamic-update-slice_fusion.4.refs_1_), channel_id=1, source_target_pairs={{0,1},{1,0},{2,3},{3,2},{4,5},{5,4},{6,7},{7,6},{8,9},{9,8},{10,11... | collective-permute-start | bytes 3145736 | tf_op jit(solution)/shard_map/ppermute | solution.py:402
  93.8 11.2 %collective-permute-start.25 = (bf16[2048,256]{1,0:T(8,128)(2,1)S(1)}, bf16[2048,256]{1,0:T(8,128)(2,1)S(1)}, u32[]{:S(2)}, u32[]{:S(2)}) collective-permute-start(bf16[2048,256]{1,0:T(8,128)(2,1)S(1)} %constant_dynamic-update-slice_fusion.6.refs_2_), channel_id=1, source_target_pairs={{0,1},{1,0},{2,3},{3,2},{4,5},{5,4},{6,7},{7,6},{8,9},{9,8},{10,11... | collective-permute-start | bytes 3145736 | tf_op jit(solution)/shard_map/ppermute | solution.py:402
  104.0 2.2 %collective-permute-start.21 = (bf16[1024,256]{1,0:T(8,128)(2,1)S(1)}, bf16[1024,256]{1,0:T(8,128)(2,1)S(1)}, u32[]{:S(2)}, u32[]{:S(2)}) collective-permute-start(bf16[1024,256]{1,0:T(8,128)(2,1)S(1)} %collective-permute-done.18.refs_3_), channel_id=1, source_target_pairs={{0,1},{1,0},{2,3},{3,2},{4,5},{5,4},{6,7},{7,6},{8,9},{9,8},{10,11... | collective-permute-start | bytes 1572872 | tf_op jit(solution)/shard_map/ppermute | solution.py:402
  104.5 2.3 %collective-permute-start.22 = (bf16[1024,256]{1,0:T(8,128)(2,1)S(1)}, bf16[1024,256]{1,0:T(8,128)(2,1)S(1)}, u32[]{:S(2)}, u32[]{:S(2)}) collective-permute-start(bf16[1024,256]{1,0:T(8,128)(2,1)S(1)} %collective-permute-done.16.refs_4_), channel_id=1, source_target_pairs={{0,1},{1,0},{2,3},{3,2},{4,5},{5,4},{6,7},{7,6},{8,9},{9,8},{10,11... | collective-permute-start | bytes 1572872 | tf_op jit(solution)/shard_map/ppermute | solution.py:402
  104.6 3.0 %collective-permute-start.23 = (bf16[1024,256]{1,0:T(8,128)(2,1)S(1)}, bf16[1024,256]{1,0:T(8,128)(2,1)S(1)}, u32[]{:S(2)}, u32[]{:S(2)}) collective-permute-start(bf16[1024,256]{1,0:T(8,128)(2,1)S(1)} %collective-permute-done.17.refs_5_), channel_id=1, source_target_pairs={{0,1},{1,0},{2,3},{3,2},{4,5},{5,4},{6,7},{7,6},{8,9},{9,8},{10,11... | collective-permute-start | bytes 1572872 | tf_op jit(solution)/shard_map/ppermute | solution.py:402
